TPU v7x, 32 devices: a whole 2x2x4 slice. The times are simulated.
32 devices in a mesh: seq: 4 (over x, core), vocab: 8 (over z, y).
Axes of the slice: x: 2, y: 2, z: 4, core: 2. Of those that a mesh axis runs over, the one named last changes fastest.
Arguments:
- hidden: bfloat16 [512, 8192], P('seq'), may hold values from -6 to 6
- steer: float32 [8192], replicated, may hold values from -4 to 4
- tangent: float32 [8192], replicated, may hold values from -6 to 6
- gain: float32 [8192], replicated, may hold values from 0.5 to 1.5
- head: bfloat16 [8192, 19456], P('seq', 'vocab'), may hold values from -0.198873782 to 0.198873782
- target: bfloat16 [512, 19456], P('seq', 'vocab'), may hold values from 0.099609375 to 10
Outputs:
- gradient: float32 [512, 8192], P('vocab', 'seq')
- curvature: float32 [512, 8192], P('vocab', 'seq')
All inputs are finite; a program needn't handle non-finite values.
Results may differ from a plain program's by a relative error of at most 0.0082.
Values may be sent and summed in bfloat16 or wider, within the bound.
No kernel may reach another device: no remote copies, remote signals or barrier semaphores. Data moves between devices by JAX's collectives and lax.ppermute only.
A program may use at most 128 MiB of HBM per device.

v0:
```python
import functools

import jax
import jax.numpy as jnp
from jax import lax
from jax.experimental import pallas as pl
from jax.experimental.pallas import tpu as pltpu
from jax.sharding import PartitionSpec as P

EPSILON = 1e-06
NT = (((1,), (1,)), ((), ()))
QUARTERS = 4
PAIR = 2
F32, BF16 = jnp.float32, jnp.bfloat16


def params(mebibytes):
    return pltpu.CompilerParams(vmem_limit_bytes=mebibytes * 1024 * 1024)


def whole_spec():
    return pl.BlockSpec(memory_space=pltpu.VMEM)


def smem_spec():
    return pl.BlockSpec(memory_space=pltpu.SMEM)


def swap(value, axis, bit, size):
    return lax.ppermute(value, axis, [(i, i ^ bit) for i in range(size)])


def lanes(columns, rows):
    lane = lax.broadcasted_iota(jnp.int32, (rows, 128), 1)
    tile = jnp.zeros((rows, 128), F32)
    for index, column in enumerate(columns):
        tile = jnp.where(lane == index, column, tile)
    return tile


def turn(rows8):
    return jnp.concatenate([rows8, jnp.zeros((120, 128), F32)], axis=0).T


def cut_kernel(width, seq_size, at, hidden, vectors, *outs):
    own, mate, over_2, over_3, sums, parts, two = outs
    seq_index, group = at[0], at[1]
    rows = hidden.shape[0]
    size = rows // QUARTERS

    def quarter(place):
        return pl.ds(pl.multiple_of((place ^ group) * size, size), size)

    def features(bit):
        return pl.ds(pl.multiple_of((seq_index ^ bit) * width, width), width)

    for out, bit in ((over_2, 2), (over_3, 3)):
        out[0:size, :] = hidden[quarter(0), features(bit)]
        out[size:, :] = hidden[quarter(3), features(bit)]
    steer, tangent = vectors[0:1, :], vectors[1:2, :]
    columns = []
    for place in range(QUARTERS):
        spot = pl.ds(place * size, size)
        own[spot, :] = hidden[quarter(place), features(0)]
        mate[spot, :] = hidden[quarter(place), features(1)]
        inputs = hidden[quarter(place), :].astype(F32) + steer
        columns.append(
            lanes(
                [
                    jnp.sum(inputs * inputs, axis=1, keepdims=True),
                    jnp.sum(inputs * tangent, axis=1, keepdims=True),
                ],
                size,
            )
        )
    sums[...] = jnp.concatenate(columns, axis=0).T[:8]
    mine = vectors[:, features(0)]
    parts[...] = mine
    line = mine[1:2] * mine[2:3]
    high = line.astype(BF16).astype(F32)
    two[...] = jnp.concatenate(
        [high, line - high, jnp.zeros((14, width), F32)], axis=0
    ).astype(BF16)


def cut(at, hidden, vectors, width, seq_size):
    rows = hidden.shape[0]
    piece = jax.ShapeDtypeStruct((2 * (rows // QUARTERS), width), BF16)
    block = jax.ShapeDtypeStruct((rows, width), BF16)
    return pl.pallas_call(
        functools.partial(cut_kernel, width, seq_size),
        in_specs=[smem_spec(), whole_spec(), whole_spec()],
        out_specs=[whole_spec()] * 7,
        out_shape=[
            block,
            block,
            piece,
            piece,
            jax.ShapeDtypeStruct((8, rows), F32),
            jax.ShapeDtypeStruct((vectors.shape[0], width), F32),
            jax.ShapeDtypeStruct((16, width), BF16),
        ],
        compiler_params=params(12),
    )(at, hidden, vectors)


def soften_kernel(feature_count, at, first, second, row, sums_a, sums_b, *outs):
    both_out, stats, tile = outs
    tokens = first.shape[0]
    count = at.shape[0]
    size = 2 * tokens // count
    line = row[0:1, :]
    for block, (source, sums) in enumerate(((first, sums_a), (second, sums_b))):
        turned = turn(sums[...])
        denominator = turned[:, 0:1] / feature_count + EPSILON
        inverse = 1.0 / jnp.sqrt(denominator)
        slope = turned[:, 1:2] / feature_count / denominator
        for piece in range(count // 2):
            begin = piece * size
            logits = source[begin : begin + size, :]
            spot = pl.ds(pl.multiple_of(at[block * (count // 2) + piece], size), size)
            peak = jnp.max(logits, axis=1, keepdims=True)
            exponent = jnp.exp(logits - peak)
            dlogits = line * inverse[begin : begin + size] - logits * slope[begin : begin + size]
            total = jnp.sum(exponent, axis=1, keepdims=True)
            mean = jnp.sum(exponent * dlogits, axis=1, keepdims=True) / total
            tilted = exponent * (dlogits - mean)
            both_out[0, spot, :] = exponent.astype(BF16)
            both_out[1, spot, :] = tilted.astype(BF16)
            tile[spot, :] = lanes([peak, total, mean], size)
    for begin in range(0, 2 * tokens, 128):
        stats[:, begin : begin + 128] = tile[begin : begin + 128, :].T[:8]


def soften(at, first, second, row, sums_a, sums_b, feature_count):
    tokens, width = first.shape
    rows = 2 * tokens
    return pl.pallas_call(
        functools.partial(soften_kernel, feature_count),
        in_specs=[smem_spec()] + [whole_spec()] * 5,
        out_specs=[whole_spec()] * 2,
        out_shape=[
            jax.ShapeDtypeStruct((2, rows, width), BF16),
            jax.ShapeDtypeStruct((8, rows), F32),
        ],
        scratch_shapes=[pltpu.VMEM((rows, 128), F32)],
        compiler_params=params(16),
        cost_estimate=pl.CostEstimate(
            flops=30 * rows * width, bytes_accessed=12 * rows * width, transcendentals=rows * width
        ),
    )(at, first, second, row, sums_a, sums_b)


def order_kernel(at, *refs):
    blocks, totals, (ordered, columns) = refs[:4], refs[4:8], refs[8:]
    tokens = blocks[0].shape[0]
    count = at.shape[0]
    size = 4 * tokens // count
    half = 2 * tokens
    for block in range(4):
        inverse = 1.0 / turn(totals[block][...])
        for piece in range(count // 4):
            begin = piece * size
            place = at[block * (count // 4) + piece] + half * (block // 2)
            spot = pl.ds(pl.multiple_of(place, size), size)
            ordered[spot, :] = blocks[block][begin : begin + size, :]
            columns[spot, :] = inverse[begin : begin + size]


def order(at, blocks, totals):
    tokens, width = blocks[0].shape
    rows = 4 * tokens
    return pl.pallas_call(
        order_kernel,
        in_specs=[smem_spec()] + [whole_spec()] * 8,
        out_specs=[whole_spec()] * 2,
        out_shape=[
            jax.ShapeDtypeStruct((rows, width), BF16),
            jax.ShapeDtypeStruct((rows, 128), F32),
        ],
        compiler_params=params(12),
        cost_estimate=pl.CostEstimate(
            flops=rows * width, bytes_accessed=4 * rows * width, transcendentals=0
        ),
    )(at, *blocks, *totals)


def merge(first, second):
    peak = jnp.maximum(first[0], second[0])
    one = jnp.exp(first[0] - peak) * first[1]
    two = jnp.exp(second[0] - peak) * second[1]
    total = one + two
    mean = (one * first[2] + two * second[2]) / total
    return jnp.stack([peak, total, mean] + [first[i] + second[i] for i in range(3, len(first))])


def exchange(value, size):
    half = value.shape[1] // 2
    other = swap(value, "vocab", 1, size)
    aligned = jnp.concatenate([other[:3, half:], other[:3, :half]], axis=1)
    value = merge(value, jnp.concatenate([aligned, other[3:]], axis=0))
    bit = PAIR
    while bit < size:
        value = merge(value, swap(value, "vocab", bit, size))
        bit *= 2
    return value


def body(hidden, steer, tangent, gain, head, target):
    seq_size = lax.axis_size("seq")
    vocab_size = lax.axis_size("vocab")
    seq_index = lax.axis_index("seq")
    vocab_index = lax.axis_index("vocab")
    tokens, feature_count = hidden.shape
    width = head.shape[0]
    rows = seq_size * tokens
    share = rows // vocab_size
    quarter = tokens // QUARTERS
    size = min(share, quarter)
    y, z = vocab_index % PAIR, vocab_index // PAIR
    length = vocab_size // PAIR
    chip = seq_index // 2
    group = 2 * y + z % 2

    def destination(block, begin):
        row = (block % 2) * tokens + begin
        owner, inside = row // share, row % share
        return ((owner % PAIR) ^ y) * tokens + owner // PAIR * share + inside

    starts = jnp.arange(tokens // size) * size
    turned = ((starts // quarter) ^ group) * quarter + starts % quarter

    def places(bits, begins):
        return jnp.concatenate(
            [destination(seq_index ^ bit, begins) for bit in bits]
        ).astype(jnp.int32)

    own_places, other_places = places((0, 1), turned), places((2, 3), turned)
    target_places = places((0, 1, 2, 3), starts)

    at = jnp.stack([seq_index, group]).astype(jnp.int32)
    vectors = jnp.stack([steer, tangent, gain])
    own, mate, over_2, over_3, sums_0, parts, two = cut(
        at, hidden, vectors, width, seq_size
    )
    mate = swap(mate, "seq", 1, seq_size)
    sums_1 = swap(sums_0, "seq", 1, seq_size)
    over_2, over_3 = swap(over_2, "seq", 2, seq_size), swap(over_3, "seq", 3, seq_size)
    both = swap(jnp.stack([sums_0, sums_1]), "seq", 2, seq_size)
    sums = [sums_0, sums_1, both[0], both[1]]
    near = jnp.stack([over_2[:quarter], over_3[:quarter]])
    by_y = swap(near, "vocab", 2, vocab_size)
    by_z = swap(near, "vocab", 1, vocab_size)
    steer_part, gain_part = parts[0], parts[2]

    denominators = [s[0] / feature_count + EPSILON for s in sums]
    radii = [jnp.sqrt(d) for d in denominators]

    def partial_logits(bit, block):
        values = block.astype(F32) + steer_part
        normed = (gain_part * values / radii[bit][:, None]).astype(BF16)
        return jnp.dot(normed, head, preferred_element_type=F32)

    given = swap(partial_logits(1, mate), "seq", 1, seq_size)
    summed_0 = partial_logits(0, own) + given
    send_0, over_2, over_3 = lax.optimization_barrier(
        (summed_0.astype(jnp.float16), over_2, over_3)
    )
    got_2 = swap(send_0, "seq", 2, seq_size)

    two, by_y, by_z, _ = lax.optimization_barrier((two, by_y, by_z, send_0))
    row = jnp.sum(jnp.dot(two, head, preferred_element_type=F32), axis=0, keepdims=True)
    row = row + swap(row, "seq", 1, seq_size)
    tangent_row = row + swap(row, "seq", 2, seq_size)

    blocks = [own, mate] + [
        jnp.concatenate([over[:quarter], by_y[i], by_z[i], over[quarter:]], axis=0)
        for i, over in enumerate((over_2, over_3))
    ]
    given = swap(partial_logits(3, blocks[3]), "seq", 1, seq_size)
    summed_2 = partial_logits(2, blocks[2]) + given
    send_2, got_2, tangent_row = lax.optimization_barrier(
        (summed_2.astype(jnp.float16), got_2, tangent_row)
    )
    got_0 = swap(send_2, "seq", 2, seq_size)

    half = rows // 2

    def half_of(base, summed, got, where, extra):
        full = summed + got.astype(F32)
        mates = swap(full, "seq", 1, seq_size)
        both, stats = soften(
            where, full, mates, tangent_row, sums[base], sums[base + 1], feature_count
        )
        stats = stats[:3]
        joint = exchange(jnp.concatenate([stats] + extra), vocab_size)
        raw = lax.dot_general(
            both.reshape(2 * half, -1), head, NT, preferred_element_type=F32
        )
        scale = jnp.exp(stats[0] - joint[0]) / joint[1]
        lean = scale * (stats[2] - joint[2])
        plain = scale[:, None] * raw[:half]
        ggn = scale[:, None] * raw[half:] + lean[:, None] * raw[:half]
        return plain, ggn[half // 2 :].astype(BF16), ggn[: half // 2], joint

    plain_other, theirs_other, kept_other, _ = half_of(2, summed_2, got_2, other_places, [])
    own_total = jnp.sum(target.astype(F32), axis=1)
    plain_own, theirs_own, kept_own, joint = half_of(
        0, summed_0, got_0, own_places, [jnp.concatenate([own_total, own_total])[None]]
    )

    late_target, _ = lax.optimization_barrier((target, got_0))
    target_2 = swap(late_target, "seq", 2, seq_size)
    target_1 = swap(late_target, "seq", 1, seq_size)
    target_3 = swap(target_2, "seq", 1, seq_size)
    total_0 = jnp.broadcast_to(joint[3, :tokens], (8, tokens))
    total_1 = swap(total_0, "seq", 1, seq_size)
    both = swap(jnp.stack([total_0, total_1]), "seq", 2, seq_size)
    ordered, columns = order(
        target_places,
        [target, target_1, target_2, target_3],
        [total_0, total_1, both[0], both[1]],
    )
    ordered, theirs_own = lax.optimization_barrier((ordered, theirs_own))
    weighed = lax.dot_general(ordered, head, NT, preferred_element_type=F32)
    inverse = columns[:, 0:1]
    gradients = [
        plain - inverse[begin : begin + half] * weighed[begin : begin + half]
        for plain, begin in ((plain_own, 0), (plain_other, half))
    ]

    def meet(theirs, kept):
        return kept + swap(theirs, "vocab", 1, vocab_size).astype(F32)

    def over_chain(joined):
        joined = joined.reshape(length, share, -1)
        near_half = length // 2
        bit = 1
        while bit < length:
            if bit < near_half:
                cut_up = joined.reshape(-1, 2, share, joined.shape[-1])
                mine_bit = (z // bit) % 2
                sent = lax.dynamic_index_in_dim(cut_up, 1 - mine_bit, 1, False)
                kept = lax.dynamic_index_in_dim(cut_up, mine_bit, 1, False)
            else:
                place = (z // bit) ^ chip
                sent = lax.dynamic_index_in_dim(joined, 1 - place, 0, True)
                kept = lax.dynamic_index_in_dim(joined, place, 0, True)
            got = swap(sent.astype(BF16), "vocab", bit * PAIR, vocab_size)
            joined = kept + got.astype(F32)
            bit *= 2
        return joined[0]

    ggn_mine = over_chain(
        jnp.concatenate([meet(theirs_own, kept_own), meet(theirs_other, kept_other)], axis=0)
    )
    chunks = []
    for begin in (0, width // 2):
        part = [g[:, begin : begin + width // 2] for g in gradients]
        theirs = jnp.concatenate([p[half // 2 :] for p in part]).astype(BF16)
        kept = jnp.concatenate([p[: half // 2] for p in part])
        chunks.append(over_chain(meet(theirs, kept)))
    grad_mine = jnp.concatenate(chunks, axis=1)

    first_row = vocab_index * share
    owner = first_row // tokens
    block = owner ^ seq_index

    def choose(options):
        result = options[0]
        for index in range(1, len(options)):
            result = jnp.where(block == index, options[index], result)
        return result

    def gather_rows(options):
        pieces = []
        for begin in range(0, share, size):
            inside = first_row % tokens + begin
            place = ((inside // quarter) ^ group) * quarter + inside % quarter
            pieces.append(
                choose([lax.dynamic_slice_in_dim(o, place, size, 0) for o in options])
            )
        return jnp.concatenate(pieces, axis=0)

    my_inputs = gather_rows(blocks).astype(F32) + steer_part
    my_denominator = gather_rows(denominators)
    my_radius = jnp.sqrt(my_denominator)

    def norm_back(upstream):
        scaled = gain_part * upstream
        dotted = jnp.sum(my_inputs * scaled, axis=1)[None]
        dotted = dotted + swap(dotted, "seq", 1, seq_size)
        dotted = (dotted + swap(dotted, "seq", 2, seq_size))[0]
        along = dotted / feature_count / my_denominator
        return (scaled - my_inputs * along[:, None]) / my_radius[:, None]

    return norm_back(grad_mine), norm_back(ggn_mine)


def solution(mesh):
    return jax.shard_map(
        body,
        mesh=mesh,
        in_specs=(P("seq", None), P(), P(), P(), P("seq", "vocab"), P("seq", "vocab")),
        out_specs=(P("vocab", "seq"), P("vocab", "seq")),
        check_vma=False,
    )
```

profile of v0, /device:TPU:0, one launch (start us, length us, event | category | flops | bytes accessed | tf_op | source)
XLA Modules:
  0.0 224.8 jit_solution(9071136966577653614)
XLA Ops:
  5.4 2.6 %collective-permute-start.3 = (bf16[64,2048]{1,0:T(8,128)(2,1)S(1)}, bf16[64,2048]{1,0:T(8,128)(2,1)S(1)}, u32[]{:S(2)}, u32[]{:S(2)}) collective-permute-start(bf16[64,2048]{1,0:T(8,128)(2,1)S(1)} %get-tuple-element.31), channel_id=1, source_target_pairs={{0,16},{8,24},{16,0},{24,8},{1,17},{9,25},{17,1},{25,9},{2,18},{10... | collective-permute-start | bytes 786440 | tf_op jit(solution)/shard_map/ppermute | solution.py:30
  8.9 2.0 collective-permute-start.7
  11.4 5.6 %fusion.4 = f32[128,2432]{1,0:T(8,128)S(1)} fusion(bf16[2048,2432]{1,0:T(8,128)(2,1)} %param.10, bf16[128,2048]{1,0:T(8,128)(2,1)S(1)} %collective-permute-done, f32[128]{0:T(128)S(1)} %get-tuple-element.126, f32[2048]{0:T(1024)S(1)} %bitcast.170, f32[2048]{0:T(1024)S(1)} %bitcast.164), kind=kOutput, calls=%fused_computation.27 | convolution fusion | flops 1276379136 | bytes 11747840 | tf_op jit(solution)/shard_map/dot_general | solution.py:262
  17.1 3.5 %collective-permute-done.7 = f32[2,8,128]{2,1,0:T(8,128)S(1)} collective-permute-done((f32[2,8,128]{2,1,0:T(8,128)S(1)}, f32[2,8,128]{2,1,0:T(8,128)S(1)}, u32[]{:S(2)}, u32[]{:S(2)}) %collective-permute-start.7) | collective-permute-done | bytes 8224 | tf_op jit(solution)/shard_map/ppermute | solution.py:30
  24.8 6.4 %fusion.89 = (f16[128,2432]{1,0:T(8,128)(2,1)}, f32[128,2432]{1,0:T(8,128)S(1)}) fusion(f32[128,2432]{1,0:T(8,128)S(1)} %collective-permute-done.2, bf16[2048,2432]{1,0:T(8,128)(2,1)} %param.10, bf16[128,2048]{1,0:T(8,128)(2,1)S(1)} %get-tuple-element.28, f32[128]{0:T(128)S(1)} %get-tuple-element.124, f32[2048]{0:T(1024)S(1)} %bitcast.171, ...), kind=kOutput, calls=%fused_computation.311 | convolution fusion | flops 1277001728 | bytes 13615616 | tf_op jit(solution)/shard_map/dot_general | solution.py:262
  32.8 2.7 %fusion.5 = f32[128,2432]{1,0:T(8,128)} fusion(bf16[2048,2432]{1,0:T(8,128)(2,1)S(1)} %bitcast.155, f32[128]{0:T(128)S(1)} %get-tuple-element.110, f32[2048]{0:T(1024)S(1)} %bitcast.172, f32[2048]{0:T(1024)S(1)} %bitcast.166, bf16[32,2048]{1,0:T(8,128)(2,1)S(1)} %get-tuple-element.106, bf16[32,2048]{1,0:T(8,128)(2,1)S(1)} %get-tuple-element.104, ...), kind=kOutput, calls=%fused_computation.28 | convolution fusion | flops 1278214144 | bytes 11747840 | tf_op jit(solution)/shard_map/dot_general | solution.py:262
  38.2 14.4 %collective-permute-done.11 = f32[1,2432]{1,0:T(1,128)S(1)} collective-permute-done((f32[1,2432]{1,0:T(1,128)S(1)}, f32[1,2432]{1,0:T(1,128)S(1)}, u32[]{:S(2)}, u32[]{:S(2)}) %collective-permute-start.11) | collective-permute-done | bytes 9760 | tf_op jit(solution)/shard_map/ppermute | solution.py:30
  52.6 5.9 %fusion.90 = (f16[128,2432]{1,0:T(8,128)(2,1)S(1)}, f32[128,2432]{1,0:T(8,128)S(1)}) fusion(f32[128,2432]{1,0:T(8,128)} %collective-permute-done.8, bf16[2048,2432]{1,0:T(8,128)(2,1)} %param.10, f32[128]{0:T(128)S(1)} %get-tuple-element.111, f32[2048]{0:T(1024)S(1)} %bitcast.173, f32[2048]{0:T(1024)S(1)} %bitcast.167, ...), kind=kOutput, calls=%fused_computation.312 | convolution fusion | flops 1278836736 | bytes 13615616 | tf_op jit(solution)/shard_map/dot_general | solution.py:262
  61.7 13.8 %collective-permute-done.12 = f16[128,2432]{1,0:T(8,128)(2,1)S(1)} collective-permute-done((f16[128,2432]{1,0:T(8,128)(2,1)S(1)}, f16[128,2432]{1,0:T(8,128)(2,1)S(1)}, u32[]{:S(2)}, u32[]{:S(2)}) %collective-permute-start.12) | collective-permute-done | bytes 622624 | tf_op jit(solution)/shard_map/ppermute | solution.py:30
  77.0 2.4 %shard_map.80 = (bf16[2,256,2432]{2,1,0:T(8,128)(2,1)S(1)}, f32[8,256]{1,0:T(8,128)S(1)}) custom-call(s32[8]{0:T(128)S(1)} %pad_add_fusion.3.at, f32[128,2432]{1,0:T(8,128)S(1)} %convert_add_fusion.first, f32[128,2432]{1,0:T(8,128)S(1)} %collective-permute-done.22.second, f32[1,2432]{1,0:T(1,128)S(1)} %add.603.row, f32[8,128]{1,0:T(8,128)S(1)} %get-tuple-element.117.sums_a, ...), custom_call_target="tpu_custom_call" | custom-call | flops 18677760 | bytes 7471104 | tf_op jit(solution)/shard_map/pallas_call | solution.py:138
  80.4 2.7 %collective-permute-done.23 = f32[3,256]{1,0:T(4,128)S(1)} collective-permute-done((f32[3,256]{1,0:T(4,128)S(1)}, f32[3,256]{1,0:T(4,128)S(1)}, u32[]{:S(2)}, u32[]{:S(2)}) %collective-permute-start.23) | collective-permute-done | bytes 3104 | tf_op jit(solution)/shard_map/ppermute | solution.py:30
  84.2 9.7 %fusion.93 = f32[512,2048]{1,0:T(8,128)} fusion(bf16[512,2432]{1,0:T(8,128)(2,1)S(1)} %bitcast.153, bf16[2048,2432]{1,0:T(8,128)(2,1)} %param.10), kind=kOutput, calls=%fused_computation.315 | convolution fusion | flops 5100273664 | bytes 16646144 | tf_op jit(solution)/shard_map/dot_general | solution.py:297
  93.9 2.7 %collective-permute-start.25 = (f32[3,256]{1,0:T(4,128)S(1)}, f32[3,256]{1,0:T(4,128)S(1)}, u32[]{:S(2)}, u32[]{:S(2)}) collective-permute-start(f32[3,256]{1,0:T(4,128)S(1)} %pad_maximum_fusion.14), channel_id=1, source_target_pairs={{0,4},{1,5},{2,6},{3,7},{4,0},{5,1},{6,2},{7,3},{8,12},{9,13},{10,... | collective-permute-start | bytes 9224 | tf_op jit(solution)/shard_map/ppermute | solution.py:30
  96.6 2.2 shard_map.78
  99.5 3.1 %collective-permute-done.14 = f32[4,256]{1,0:T(4,128)S(1)} collective-permute-done((f32[4,256]{1,0:T(4,128)S(1)}, f32[4,256]{1,0:T(4,128)S(1)}, u32[]{:S(2)}, u32[]{:S(2)}) %collective-permute-start.14) | collective-permute-done | bytes 4128 | tf_op jit(solution)/shard_map/ppermute | solution.py:30
  108.6 9.3 %fusion.91 = f32[512,2048]{1,0:T(8,128)S(1)} fusion(bf16[512,2432]{1,0:T(8,128)(2,1)S(1)} %bitcast.152, bf16[2048,2432]{1,0:T(8,128)(2,1)} %param.10), kind=kOutput, calls=%fused_computation.313 | convolution fusion | flops 5100273664 | bytes 16646144 | tf_op jit(solution)/shard_map/dot_general | solution.py:297
  125.0 7.3 %fusion.92 = f32[512,2048]{1,0:T(8,128)} fusion(bf16[512,2432]{1,0:T(8,128)(2,1)S(1)} %get-tuple-element.47, bf16[2048,2432]{1,0:T(8,128)(2,1)S(1)} %bitcast.157), kind=kOutput, calls=%fused_computation.314 | convolution fusion | flops 5100273664 | bytes 16646144 | tf_op jit(solution)/shard_map/dot_general | solution.py:325
  132.3 3.9 %fusion.74 = (bf16[256,2048]{1,0:T(8,128)(2,1)S(1)}, f32[256,2048]{1,0:T(8,128)S(1)}, f32[256,2048]{1,0:T(8,128)S(1)}, bf16[256,2048]{1,0:T(8,128)(2,1)S(1)}, f32[256,2048]{1,0:T(8,128)S(1)}) fusion(f32[512,2048]{1,0:T(8,128)} %fusion.92, f32[256]{0:T(256)S(1)} %get-tuple-element.55, f32[512,2048]{1,0:T(8,128)} %fusion.93, f32[256]{0:T(256)S(1)} %copy-done.16, ...), kind=kLoop, calls=%fused_computation.299 | loop fusion | flops 5767168 | bytes 18879488 | tf_op jit(solution)/shard_map/convert.7
  141.9 29.7 %collective-permute-done.35 = bf16[128,2048]{1,0:T(8,128)(2,1)S(1)} collective-permute-done((bf16[128,2048]{1,0:T(8,128)(2,1)S(1)}, bf16[128,2048]{1,0:T(8,128)(2,1)S(1)}, u32[]{:S(2)}, u32[]{:S(2)}) %collective-permute-start.35) | collective-permute-done | bytes 524320 | tf_op jit(solution)/shard_map/ppermute | solution.py:30
  175.6 17.9 %collective-permute-done.27 = bf16[2,64,1024]{2,1,0:T(8,128)(2,1)S(1)} collective-permute-done((bf16[2,64,1024]{2,1,0:T(8,128)(2,1)S(1)}, bf16[2,64,1024]{2,1,0:T(8,128)(2,1)S(1)}, u32[]{:S(2)}, u32[]{:S(2)}) %collective-permute-start.27) | collective-permute-done | bytes 262176 | tf_op jit(solution)/shard_map/ppermute | solution.py:30
  196.4 3.5 %collective-permute-start.31 = (bf16[1,64,1024]{2,1,0:T(8,128)(2,1)S(1)}, bf16[1,64,1024]{2,1,0:T(8,128)(2,1)S(1)}, u32[]{:S(2)}, u32[]{:S(2)}) collective-permute-start(bf16[1,64,1024]{2,1,0:T(8,128)(2,1)S(1)} %dynamic-slice_convert_fusion.1), channel_id=1, source_target_pairs={{0,4},{1,5},{2,6},{3,7},{4,0},{5,1},{6,2},{7,3},{8,12},{9,13},{10,... | collective-permute-start | bytes 393224 | tf_op jit(solution)/shard_map/ppermute | solution.py:30
  200.2 10.2 %collective-permute-done.28 = bf16[1,64,1024]{2,1,0:T(8,128)(2,1)S(1)} collective-permute-done((bf16[1,64,1024]{2,1,0:T(8,128)(2,1)S(1)}, bf16[1,64,1024]{2,1,0:T(8,128)(2,1)S(1)}, u32[]{:S(2)}, u32[]{:S(2)}) %collective-permute-start.28) | collective-permute-done | bytes 131104 | tf_op jit(solution)/shard_map/ppermute | solution.py:30
  210.4 2.8 %collective-permute-done.31 = bf16[1,64,1024]{2,1,0:T(8,128)(2,1)S(1)} collective-permute-done((bf16[1,64,1024]{2,1,0:T(8,128)(2,1)S(1)}, bf16[1,64,1024]{2,1,0:T(8,128)(2,1)S(1)}, u32[]{:S(2)}, u32[]{:S(2)}) %collective-permute-start.31) | collective-permute-done | bytes 131104 | tf_op jit(solution)/shard_map/ppermute | solution.py:30
  213.2 3.3 %collective-permute-done.37 = bf16[1,64,2048]{2,1,0:T(8,128)(2,1)S(1)} collective-permute-done((bf16[1,64,2048]{2,1,0:T(8,128)(2,1)S(1)}, bf16[1,64,2048]{2,1,0:T(8,128)(2,1)S(1)}, u32[]{:S(2)}, u32[]{:S(2)}) %collective-permute-start.37) | collective-permute-done | bytes 262176 | tf_op jit(solution)/shard_map/ppermute | solution.py:30
  (211 shorter events, 56.0 us)
Async XLA Ops:
  5.4 15.9 %collective-permute-start.3 = (bf16[64,2048]{1,0:T(8,128)(2,1)S(1)}, bf16[64,2048]{1,0:T(8,128)(2,1)S(1)}, u32[]{:S(2)}, u32[]{:S(2)}) collective-permute-start(bf16[64,2048]{1,0:T(8,128)(2,1)S(1)} %get-tuple-element.31), channel_id=1, source_target_pairs={{0,16},{8,24},{16,0},{24,8},{1,17},{9,25},{17,1},{25,9},{2,18},{10... | collective-permute-start | bytes 786440 | tf_op jit(solution)/shard_map/ppermute | solution.py:30
  7.9 13.3 %collective-permute-start.4 = (bf16[64,2048]{1,0:T(8,128)(2,1)S(1)}, bf16[64,2048]{1,0:T(8,128)(2,1)S(1)}, u32[]{:S(2)}, u32[]{:S(2)}) collective-permute-start(bf16[64,2048]{1,0:T(8,128)(2,1)S(1)} %get-tuple-element.32), channel_id=1, source_target_pairs={{0,24},{8,16},{16,8},{24,0},{1,25},{9,17},{17,9},{25,1},{2,26},{10... | collective-permute-start | bytes 786440 | tf_op jit(solution)/shard_map/ppermute | solution.py:30
  8.9 11.7 %collective-permute-start.7 = (f32[2,8,128]{2,1,0:T(8,128)S(1)}, f32[2,8,128]{2,1,0:T(8,128)S(1)}, u32[]{:S(2)}, u32[]{:S(2)}) collective-permute-start(f32[2,8,128]{2,1,0:T(8,128)S(1)} %pad_maximum_fusion.8), channel_id=1, source_target_pairs={{0,16},{8,24},{16,0},{24,8},{1,17},{9,25},{17,1},{25,9},{2,18},{10... | collective-permute-start | bytes 24584 | tf_op jit(solution)/shard_map/ppermute | solution.py:30
  35.5 17.1 %collective-permute-start.8 = (f32[128,2432]{1,0:T(8,128)}, f32[128,2432]{1,0:T(8,128)}, u32[]{:S(2)}, u32[]{:S(2)}) collective-permute-start(f32[128,2432]{1,0:T(8,128)} %fusion.5), channel_id=1, source_target_pairs={{0,8},{8,0},{16,24},{24,16},{1,9},{9,1},{17,25},{25,17},{2,10},{10... | collective-permute-start | bytes 3735560 | tf_op jit(solution)/shard_map/ppermute | solution.py:30
  36.1 22.4 %collective-permute-start.9 = (f16[128,2432]{1,0:T(8,128)(2,1)}, f16[128,2432]{1,0:T(8,128)(2,1)S(1)}, u32[]{:S(2)}, u32[]{:S(2)}) collective-permute-start(f16[128,2432]{1,0:T(8,128)(2,1)} %get-tuple-element.35), channel_id=1, source_target_pairs={{0,16},{8,24},{16,0},{24,8},{1,17},{9,25},{17,1},{25,9},{2,18},{10... | collective-permute-start | bytes 1867784 | tf_op jit(solution)/shard_map/ppermute | solution.py:30
  37.6 15.0 %collective-permute-start.11 = (f32[1,2432]{1,0:T(1,128)S(1)}, f32[1,2432]{1,0:T(1,128)S(1)}, u32[]{:S(2)}, u32[]{:S(2)}) collective-permute-start(f32[1,2432]{1,0:T(1,128)S(1)} %reshape_add_fusion), channel_id=1, source_target_pairs={{0,16},{8,24},{16,0},{24,8},{1,17},{9,25},{17,1},{25,9},{2,18},{10... | collective-permute-start | bytes 29192 | tf_op jit(solution)/shard_map/ppermute | solution.py:30
  58.7 18.3 %collective-permute-start.22 = (f32[128,2432]{1,0:T(8,128)S(1)}, f32[128,2432]{1,0:T(8,128)S(1)}, u32[]{:S(2)}, u32[]{:S(2)}) collective-permute-start(f32[128,2432]{1,0:T(8,128)S(1)} %convert_add_fusion.first), channel_id=1, source_target_pairs={{0,8},{8,0},{16,24},{24,16},{1,9},{9,1},{17,25},{25,17},{2,10},{10... | collective-permute-start | bytes 3735560 | tf_op jit(solution)/shard_map/ppermute | solution.py:30
  59.8 15.7 %collective-permute-start.12 = (f16[128,2432]{1,0:T(8,128)(2,1)S(1)}, f16[128,2432]{1,0:T(8,128)(2,1)S(1)}, u32[]{:S(2)}, u32[]{:S(2)}) collective-permute-start(f16[128,2432]{1,0:T(8,128)(2,1)S(1)} %get-tuple-element.40), channel_id=1, source_target_pairs={{0,16},{8,24},{16,0},{24,8},{1,17},{9,25},{17,1},{25,9},{2,18},{10... | collective-permute-start | bytes 1867784 | tf_op jit(solution)/shard_map/ppermute | solution.py:30
  75.5 18.4 %collective-permute-start.18 = (bf16[128,2432]{1,0:T(8,128)(2,1)S(1)}, bf16[128,2432]{1,0:T(8,128)(2,1)S(1)}, u32[]{:S(2)}, u32[]{:S(2)}) collective-permute-start(bf16[128,2432]{1,0:T(8,128)(2,1)S(1)} %copy-done), channel_id=1, source_target_pairs={{0,16},{8,24},{16,0},{24,8},{1,17},{9,25},{17,1},{25,9},{2,18},{10... | collective-permute-start | bytes 1867784 | tf_op jit(solution)/shard_map/ppermute | solution.py:30
  77.0 46.5 %collective-permute-start.17 = (bf16[128,2432]{1,0:T(8,128)(2,1)S(1)}, bf16[128,2432]{1,0:T(8,128)(2,1)S(1)}, u32[]{:S(2)}, u32[]{:S(2)}) collective-permute-start(bf16[128,2432]{1,0:T(8,128)(2,1)S(1)} %copy-done), channel_id=1, source_target_pairs={{0,8},{8,0},{16,24},{24,16},{1,9},{9,1},{17,25},{25,17},{2,10},{10... | collective-permute-start | bytes 1867784 | tf_op jit(solution)/shard_map/ppermute | solution.py:30
  80.1 16.5 %collective-permute-start.13 = (f32[128,2432]{1,0:T(8,128)S(1)}, f32[128,2432]{1,0:T(8,128)S(1)}, u32[]{:S(2)}, u32[]{:S(2)}) collective-permute-start(f32[128,2432]{1,0:T(8,128)S(1)} %convert_add_fusion.1.first), channel_id=1, source_target_pairs={{0,8},{8,0},{16,24},{24,16},{1,9},{9,1},{17,25},{25,17},{2,10},{10... | collective-permute-start | bytes 3735560 | tf_op jit(solution)/shard_map/ppermute | solution.py:30
  83.2 10.7 %collective-permute-start.24 = (f32[3,256]{1,0:T(4,128)S(1)}, f32[3,256]{1,0:T(4,128)S(1)}, u32[]{:S(2)}, u32[]{:S(2)}) collective-permute-start(f32[3,256]{1,0:T(4,128)S(1)} %pad_maximum_fusion.13), channel_id=1, source_target_pairs={{0,2},{1,3},{2,0},{3,1},{4,6},{5,7},{6,4},{7,5},{8,10},{9,11},{10,... | collective-permute-start | bytes 9224 | tf_op jit(solution)/shard_map/ppermute | solution.py:30
  93.9 29.6 %collective-permute-start.19 = (bf16[128,2432]{1,0:T(8,128)(2,1)S(1)}, bf16[128,2432]{1,0:T(8,128)(2,1)S(1)}, u32[]{:S(2)}, u32[]{:S(2)}) collective-permute-start(bf16[128,2432]{1,0:T(8,128)(2,1)S(1)} %collective-permute-done.18.refs_2_), channel_id=1, source_target_pairs={{0,8},{8,0},{16,24},{24,16},{1,9},{9,1},{17,25},{25,17},{2,10},{10... | collective-permute-start | bytes 1867784 | tf_op jit(solution)/shard_map/ppermute | solution.py:30
  108.1 9.9 %collective-permute-start.16 = (f32[4,256]{1,0:T(4,128)S(1)}, f32[4,256]{1,0:T(4,128)S(1)}, u32[]{:S(2)}, u32[]{:S(2)}) collective-permute-start(f32[4,256]{1,0:T(4,128)S(1)} %pad_maximum_fusion.12), channel_id=1, source_target_pairs={{0,4},{1,5},{2,6},{3,7},{4,0},{5,1},{6,2},{7,3},{8,12},{9,13},{10,... | collective-permute-start | bytes 12296 | tf_op jit(solution)/shard_map/ppermute | solution.py:30
  124.4 15.9 %collective-permute-start.34 = (bf16[128,2048]{1,0:T(8,128)(2,1)}, bf16[128,2048]{1,0:T(8,128)(2,1)S(1)}, u32[]{:S(2)}, u32[]{:S(2)}) collective-permute-start(bf16[128,2048]{1,0:T(8,128)(2,1)} %slice.459), channel_id=1, source_target_pairs={{0,1},{1,0},{2,3},{3,2},{4,5},{5,4},{6,7},{7,6},{8,9},{9,8},{10,11... | collective-permute-start | bytes 1572872 | tf_op jit(solution)/shard_map/ppermute | solution.py:30
  136.4 37.9 %collective-permute-start.29 = (bf16[256,1024]{1,0:T(8,128)(2,1)S(1)}, bf16[256,1024]{1,0:T(8,128)(2,1)S(1)}, u32[]{:S(2)}, u32[]{:S(2)}) collective-permute-start(bf16[256,1024]{1,0:T(8,128)(2,1)S(1)} %pad_maximum_fusion.4), channel_id=1, source_target_pairs={{0,1},{1,0},{2,3},{3,2},{4,5},{5,4},{6,7},{7,6},{8,9},{9,8},{10,11... | collective-permute-start | bytes 1572872 | tf_op jit(solution)/shard_map/ppermute | solution.py:30
  138.1 35.0 %collective-permute-start.26 = (bf16[256,1024]{1,0:T(8,128)(2,1)S(1)}, bf16[256,1024]{1,0:T(8,128)(2,1)S(1)}, u32[]{:S(2)}, u32[]{:S(2)}) collective-permute-start(bf16[256,1024]{1,0:T(8,128)(2,1)S(1)} %pad_maximum_fusion.3), channel_id=1, source_target_pairs={{0,1},{1,0},{2,3},{3,2},{4,5},{5,4},{6,7},{7,6},{8,9},{9,8},{10,11... | collective-permute-start | bytes 1572872 | tf_op jit(solution)/shard_map/ppermute | solution.py:30
  138.6 32.9 %collective-permute-start.35 = (bf16[128,2048]{1,0:T(8,128)(2,1)S(1)}, bf16[128,2048]{1,0:T(8,128)(2,1)S(1)}, u32[]{:S(2)}, u32[]{:S(2)}) collective-permute-start(bf16[128,2048]{1,0:T(8,128)(2,1)S(1)} %slice.458), channel_id=1, source_target_pairs={{0,1},{1,0},{2,3},{3,2},{4,5},{5,4},{6,7},{7,6},{8,9},{9,8},{10,11... | collective-permute-start | bytes 1572872 | tf_op jit(solution)/shard_map/ppermute | solution.py:30
  172.0 27.9 %collective-permute-start.36 = (bf16[2,64,2048]{2,1,0:T(8,128)(2,1)S(1)}, bf16[2,64,2048]{2,1,0:T(8,128)(2,1)S(1)}, u32[]{:S(2)}, u32[]{:S(2)}) collective-permute-start(bf16[2,64,2048]{2,1,0:T(8,128)(2,1)S(1)} %fusion.6), channel_id=1, source_target_pairs={{0,2},{1,3},{2,0},{3,1},{4,6},{5,7},{6,4},{7,5},{8,10},{9,11},{10,... | collective-permute-start | bytes 1572872 | tf_op jit(solution)/shard_map/ppermute | solution.py:30
  173.3 20.2 %collective-permute-start.27 = (bf16[2,64,1024]{2,1,0:T(8,128)(2,1)S(1)}, bf16[2,64,1024]{2,1,0:T(8,128)(2,1)S(1)}, u32[]{:S(2)}, u32[]{:S(2)}) collective-permute-start(bf16[2,64,1024]{2,1,0:T(8,128)(2,1)S(1)} %fusion.19), channel_id=1, source_target_pairs={{0,2},{1,3},{2,0},{3,1},{4,6},{5,7},{6,4},{7,5},{8,10},{9,11},{10,... | collective-permute-start | bytes 786440 | tf_op jit(solution)/shard_map/ppermute | solution.py:30
  174.5 21.8 %collective-permute-start.30 = (bf16[2,64,1024]{2,1,0:T(8,128)(2,1)S(1)}, bf16[2,64,1024]{2,1,0:T(8,128)(2,1)S(1)}, u32[]{:S(2)}, u32[]{:S(2)}) collective-permute-start(bf16[2,64,1024]{2,1,0:T(8,128)(2,1)S(1)} %fusion.20), channel_id=1, source_target_pairs={{0,2},{1,3},{2,0},{3,1},{4,6},{5,7},{6,4},{7,5},{8,10},{9,11},{10,... | collective-permute-start | bytes 786440 | tf_op jit(solution)/shard_map/ppermute | solution.py:30
  193.6 16.8 %collective-permute-start.28 = (bf16[1,64,1024]{2,1,0:T(8,128)(2,1)S(1)}, bf16[1,64,1024]{2,1,0:T(8,128)(2,1)S(1)}, u32[]{:S(2)}, u32[]{:S(2)}) collective-permute-start(bf16[1,64,1024]{2,1,0:T(8,128)(2,1)S(1)} %dynamic-slice_convert_fusion.2), channel_id=1, source_target_pairs={{0,4},{1,5},{2,6},{3,7},{4,0},{5,1},{6,2},{7,3},{8,12},{9,13},{10,... | collective-permute-start | bytes 393224 | tf_op jit(solution)/shard_map/ppermute | solution.py:30
  196.4 16.7 %collective-permute-start.31 = (bf16[1,64,1024]{2,1,0:T(8,128)(2,1)S(1)}, bf16[1,64,1024]{2,1,0:T(8,128)(2,1)S(1)}, u32[]{:S(2)}, u32[]{:S(2)}) collective-permute-start(bf16[1,64,1024]{2,1,0:T(8,128)(2,1)S(1)} %dynamic-slice_convert_fusion.1), channel_id=1, source_target_pairs={{0,4},{1,5},{2,6},{3,7},{4,0},{5,1},{6,2},{7,3},{8,12},{9,13},{10,... | collective-permute-start | bytes 393224 | tf_op jit(solution)/shard_map/ppermute | solution.py:30
  200.1 16.4 %collective-permute-start.37 = (bf16[1,64,2048]{2,1,0:T(8,128)(2,1)S(1)}, bf16[1,64,2048]{2,1,0:T(8,128)(2,1)S(1)}, u32[]{:S(2)}, u32[]{:S(2)}) collective-permute-start(bf16[1,64,2048]{2,1,0:T(8,128)(2,1)S(1)} %dynamic-slice_convert_fusion), channel_id=1, source_target_pairs={{0,4},{1,5},{2,6},{3,7},{4,0},{5,1},{6,2},{7,3},{8,12},{9,13},{10,... | collective-permute-start | bytes 786440 | tf_op jit(solution)/shard_map/ppermute | solution.py:30
  (41 other events, 414.9 us)
where the time goes:
time: 225 us
  waiting for transfers between devices  111 us (49%)
  matrix products  48.2 us (21%)
  starting transfers between devices  36.9 us (16%)
  other arithmetic  14.8 us (7%)
  Pallas kernels  7.05 us (3%)
  local copies, waits for them, and re-layouts  5.77 us (3%)
    ppermute x40, waiting for transfers between devices, swap(): return lax.ppermute(value, axis, [(i, i ^ bit) for i in range(size)])  111 us
    ppermute x40, starting transfers between devices, swap(): return lax.ppermute(value, axis, [(i, i ^ bit) for i in range(size)])  36.9 us
    dot_general x4, matrix products, partial_logits(): return jnp.dot(normed, head, preferred_element_type=F32)  20.6 us
    dot_general x2, matrix products, half_of(): lax.dot_general(both.reshape(2 * half, -1), head, NT, preferred_element_t...  19 us
    dot_general x1, matrix products, body(): weighed = lax.dot_general(ordered, head, NT, preferred_element_type=F32)  7.28 us
    pallas_call x2, Pallas kernels, soften(): pl.pallas_call(functools.partial(soften_kernel, feature_count), in_specs=...  4.69 us
  transfers between devices with their start and end apart: 40, of which 17 were waited for; matrix products, arithmetic and copies ran while one was open for 27% of the time, Pallas kernels for 2%

commit v1 on v0

--- a/solution.py
+++ b/solution.py
@@ -11,6 +11,7 @@
 NT = (((1,), (1,)), ((), ()))
 QUARTERS = 4
 PAIR = 2
+LIGHT = pl.CostEstimate(flops=0, bytes_accessed=0, transcendentals=0)
 F32, BF16 = jnp.float32, jnp.bfloat16
 
 
@@ -101,6 +102,7 @@
             jax.ShapeDtypeStruct((16, width), BF16),
         ],
         compiler_params=params(12),
+        cost_estimate=LIGHT,
     )(at, hidden, vectors)
 
 
@@ -145,9 +147,7 @@
         ],
         scratch_shapes=[pltpu.VMEM((rows, 128), F32)],
         compiler_params=params(16),
-        cost_estimate=pl.CostEstimate(
-            flops=30 * rows * width, bytes_accessed=12 * rows * width, transcendentals=rows * width
-        ),
+        cost_estimate=LIGHT,
     )(at, first, second, row, sums_a, sums_b)
 
 
@@ -179,10 +179,39 @@
             jax.ShapeDtypeStruct((rows, 128), F32),
         ],
         compiler_params=params(12),
-        cost_estimate=pl.CostEstimate(
-            flops=rows * width, bytes_accessed=4 * rows * width, transcendentals=0
-        ),
+        cost_estimate=LIGHT,
     )(at, *blocks, *totals)
+
+
+def back_kernel(deep, cotangent, head, out):
+    width = head.shape[1]
+    result = lax.dot_general(
+        cotangent[:, :deep], head[:, :deep], NT, preferred_element_type=F32
+    )
+    if deep < width:
+        result += lax.dot_general(
+            cotangent[:, deep:], head[:, deep:], NT, preferred_element_type=F32
+        )
+    out[...] = result
+
+
+def back(cotangent, head):
+    rows, width = cotangent.shape
+    features = head.shape[0]
+    tile = 256 if features % 256 == 0 else features
+    deep = width // 256 * 256 or width
+    return pl.pallas_call(
+        functools.partial(back_kernel, deep),
+        grid=(features // tile,),
+        in_specs=[
+            pl.BlockSpec((rows, width), lambda i: (0, 0)),
+            pl.BlockSpec((tile, width), lambda i: (i, 0)),
+        ],
+        out_specs=pl.BlockSpec((rows, tile), lambda i: (0, i)),
+        out_shape=jax.ShapeDtypeStruct((rows, features), F32),
+        compiler_params=params(20),
+        cost_estimate=LIGHT,
+    )(cotangent, head)
 
 
 def merge(first, second):
@@ -247,41 +276,37 @@
     sums_1 = swap(sums_0, "seq", 1, seq_size)
     over_2, over_3 = swap(over_2, "seq", 2, seq_size), swap(over_3, "seq", 3, seq_size)
     both = swap(jnp.stack([sums_0, sums_1]), "seq", 2, seq_size)
-    sums = [sums_0, sums_1, both[0], both[1]]
     near = jnp.stack([over_2[:quarter], over_3[:quarter]])
     by_y = swap(near, "vocab", 2, vocab_size)
     by_z = swap(near, "vocab", 1, vocab_size)
     steer_part, gain_part = parts[0], parts[2]
 
-    denominators = [s[0] / feature_count + EPSILON for s in sums]
-    radii = [jnp.sqrt(d) for d in denominators]
-
-    def partial_logits(bit, block):
+    def partial_logits(block, sums_of):
+        radius = jnp.sqrt(sums_of[0] / feature_count + EPSILON)
         values = block.astype(F32) + steer_part
-        normed = (gain_part * values / radii[bit][:, None]).astype(BF16)
+        normed = (gain_part * values / radius[:, None]).astype(BF16)
         return jnp.dot(normed, head, preferred_element_type=F32)
 
-    given = swap(partial_logits(1, mate), "seq", 1, seq_size)
-    summed_0 = partial_logits(0, own) + given
-    send_0, over_2, over_3 = lax.optimization_barrier(
-        (summed_0.astype(jnp.float16), over_2, over_3)
-    )
-    got_2 = swap(send_0, "seq", 2, seq_size)
-
-    two, by_y, by_z, _ = lax.optimization_barrier((two, by_y, by_z, send_0))
     row = jnp.sum(jnp.dot(two, head, preferred_element_type=F32), axis=0, keepdims=True)
     row = row + swap(row, "seq", 1, seq_size)
     tangent_row = row + swap(row, "seq", 2, seq_size)
+    given = swap(partial_logits(mate, sums_1), "seq", 1, seq_size)
+    summed_0 = partial_logits(own, sums_0) + given
+    send_0, tangent_row = lax.optimization_barrier((summed_0.astype(jnp.float16), tangent_row))
+    got_2 = swap(send_0, "seq", 2, seq_size)
+    by_y, by_z, over_2, over_3, both, _ = lax.optimization_barrier(
+        (by_y, by_z, over_2, over_3, both, send_0)
+    )
+    sums = [sums_0, sums_1, both[0], both[1]]
+    denominators = [s[0] / feature_count + EPSILON for s in sums]
 
     blocks = [own, mate] + [
         jnp.concatenate([over[:quarter], by_y[i], by_z[i], over[quarter:]], axis=0)
         for i, over in enumerate((over_2, over_3))
     ]
-    given = swap(partial_logits(3, blocks[3]), "seq", 1, seq_size)
-    summed_2 = partial_logits(2, blocks[2]) + given
-    send_2, got_2, tangent_row = lax.optimization_barrier(
-        (summed_2.astype(jnp.float16), got_2, tangent_row)
-    )
+    given = swap(partial_logits(blocks[3], sums[3]), "seq", 1, seq_size)
+    summed_2 = partial_logits(blocks[2], sums[2]) + given
+    send_2, got_2 = lax.optimization_barrier((summed_2.astype(jnp.float16), got_2))
     got_0 = swap(send_2, "seq", 2, seq_size)
 
     half = rows // 2
@@ -294,9 +319,7 @@
         )
         stats = stats[:3]
         joint = exchange(jnp.concatenate([stats] + extra), vocab_size)
-        raw = lax.dot_general(
-            both.reshape(2 * half, -1), head, NT, preferred_element_type=F32
-        )
+        raw = back(both.reshape(2 * half, -1), head)
         scale = jnp.exp(stats[0] - joint[0]) / joint[1]
         lean = scale * (stats[2] - joint[2])
         plain = scale[:, None] * raw[:half]
@@ -304,14 +327,15 @@
         return plain, ggn[half // 2 :].astype(BF16), ggn[: half // 2], joint
 
     plain_other, theirs_other, kept_other, _ = half_of(2, summed_2, got_2, other_places, [])
+    got_0, target, theirs_other = lax.optimization_barrier((got_0, target, theirs_other))
+    got_other = swap(theirs_other, "vocab", 1, vocab_size)
     own_total = jnp.sum(target.astype(F32), axis=1)
     plain_own, theirs_own, kept_own, joint = half_of(
         0, summed_0, got_0, own_places, [jnp.concatenate([own_total, own_total])[None]]
     )
 
-    late_target, _ = lax.optimization_barrier((target, got_0))
-    target_2 = swap(late_target, "seq", 2, seq_size)
-    target_1 = swap(late_target, "seq", 1, seq_size)
+    target_2 = swap(target, "seq", 2, seq_size)
+    target_1 = swap(target, "seq", 1, seq_size)
     target_3 = swap(target_2, "seq", 1, seq_size)
     total_0 = jnp.broadcast_to(joint[3, :tokens], (8, tokens))
     total_1 = swap(total_0, "seq", 1, seq_size)
@@ -322,45 +346,66 @@
         [total_0, total_1, both[0], both[1]],
     )
     ordered, theirs_own = lax.optimization_barrier((ordered, theirs_own))
-    weighed = lax.dot_general(ordered, head, NT, preferred_element_type=F32)
+    weighed = back(ordered, head)
     inverse = columns[:, 0:1]
     gradients = [
         plain - inverse[begin : begin + half] * weighed[begin : begin + half]
         for plain, begin in ((plain_own, 0), (plain_other, half))
     ]
 
-    def meet(theirs, kept):
-        return kept + swap(theirs, "vocab", 1, vocab_size).astype(F32)
-
-    def over_chain(joined):
-        joined = joined.reshape(length, share, -1)
-        near_half = length // 2
-        bit = 1
-        while bit < length:
-            if bit < near_half:
-                cut_up = joined.reshape(-1, 2, share, joined.shape[-1])
-                mine_bit = (z // bit) % 2
-                sent = lax.dynamic_index_in_dim(cut_up, 1 - mine_bit, 1, False)
-                kept = lax.dynamic_index_in_dim(cut_up, mine_bit, 1, False)
-            else:
-                place = (z // bit) ^ chip
-                sent = lax.dynamic_index_in_dim(joined, 1 - place, 0, True)
-                kept = lax.dynamic_index_in_dim(joined, place, 0, True)
-            got = swap(sent.astype(BF16), "vocab", bit * PAIR, vocab_size)
-            joined = kept + got.astype(F32)
-            bit *= 2
-        return joined[0]
-
-    ggn_mine = over_chain(
-        jnp.concatenate([meet(theirs_own, kept_own), meet(theirs_other, kept_other)], axis=0)
-    )
+    def halve(joined, bit):
+        if bit < length // 2:
+            joined = joined.reshape(-1, 2, share, joined.shape[-1])
+            place, axis = (z // bit) % 2, 1
+        else:
+            joined = joined.reshape(2, -1, share, joined.shape[-1])
+            place, axis = (z // bit) ^ chip, 0
+        sent = lax.dynamic_index_in_dim(joined, 1 - place, axis, False)
+        kept = lax.dynamic_index_in_dim(joined, place, axis, False)
+        return sent.astype(BF16), kept
+
+    got_own = swap(theirs_own, "vocab", 1, vocab_size)
     chunks = []
     for begin in (0, width // 2):
         part = [g[:, begin : begin + width // 2] for g in gradients]
-        theirs = jnp.concatenate([p[half // 2 :] for p in part]).astype(BF16)
-        kept = jnp.concatenate([p[: half // 2] for p in part])
-        chunks.append(over_chain(meet(theirs, kept)))
-    grad_mine = jnp.concatenate(chunks, axis=1)
+        chunks.append(
+            (
+                jnp.concatenate([p[half // 2 :] for p in part]).astype(BF16),
+                jnp.concatenate([p[: half // 2] for p in part]),
+            )
+        )
+    got_own, got_other, *sends = lax.optimization_barrier(
+        (got_own, got_other, chunks[0][0], chunks[1][0])
+    )
+    ggn = jnp.concatenate(
+        [kept_own + got_own.astype(F32), kept_other + got_other.astype(F32)], axis=0
+    )
+    bits = [1]
+    bit = 1
+    while bit < length:
+        bits.append(bit * PAIR)
+        bit *= 2
+    items = [[1, *halve(ggn, 1)]] + [[0, sent, chunk[1]] for sent, chunk in zip(sends, chunks)]
+    tick = 0
+    while any(item[0] < len(bits) for item in items):
+        active = [
+            i for i, item in enumerate(items) if item[0] < len(bits) and i <= tick + 1
+        ]
+        got = [swap(items[i][1], "vocab", bits[items[i][0]], vocab_size) for i in active]
+        waiting = [i for i, item in enumerate(items) if i not in active and item[0] == 0]
+        tied = lax.optimization_barrier((got, [items[i][1] for i in waiting]))
+        for i, value in zip(waiting, tied[1]):
+            items[i][1] = value
+        for i, value in zip(active, tied[0]):
+            step, _, kept = items[i]
+            joined = kept + value.astype(F32)
+            if step + 1 < len(bits):
+                items[i] = [step + 1, *halve(joined, bits[step + 1] // PAIR)]
+            else:
+                items[i] = [step + 1, None, joined.reshape(share, -1)]
+        tick += 1
+    ggn_mine = items[0][2]
+    grad_mine = jnp.concatenate([items[1][2], items[2][2]], axis=1)
 
     first_row = vocab_index * share
     owner = first_row // tokens
@@ -386,15 +431,15 @@
     my_denominator = gather_rows(denominators)
     my_radius = jnp.sqrt(my_denominator)
 
-    def norm_back(upstream):
-        scaled = gain_part * upstream
-        dotted = jnp.sum(my_inputs * scaled, axis=1)[None]
-        dotted = dotted + swap(dotted, "seq", 1, seq_size)
-        dotted = (dotted + swap(dotted, "seq", 2, seq_size))[0]
-        along = dotted / feature_count / my_denominator
-        return (scaled - my_inputs * along[:, None]) / my_radius[:, None]
-
-    return norm_back(grad_mine), norm_back(ggn_mine)
+    scaled = [gain_part * upstream for upstream in (grad_mine, ggn_mine)]
+    dotted = jnp.stack([jnp.sum(my_inputs * value, axis=1) for value in scaled])
+    dotted = dotted + swap(dotted, "seq", 1, seq_size)
+    dotted = dotted + swap(dotted, "seq", 2, seq_size)
+    along = dotted / feature_count / my_denominator
+    return tuple(
+        (value - my_inputs * along[i][:, None]) / my_radius[:, None]
+        for i, value in enumerate(scaled)
+    )
 
 
 def solution(mesh):

time: 225 us -> 191 us (0.85)
  matrix products: 48.2 us -> 13.7 us
  waiting for transfers between devices: 111 us -> 88.5 us
  Pallas kernels: 7.05 us -> 28.5 us
  local copies, waits for them, and re-layouts: 5.77 us -> 16.7 us
  other arithmetic: 14.8 us -> 7.49 us
  starting transfers between devices: 36.9 us -> 34.2 us
    dot_general x3 -> x0, matrix products: 26.3 us -> none  [the longest x2 19 us: half_of(): lax.dot_general(both.reshape(2 * half, -1), head, NT, preferred_element_t...]
    ppermute x40 -> x38, waiting for transfers between devices: 111 us -> 88.5 us  [swap(): return lax.ppermute(value, axis, [(i, i ^ bit) for i in range(size)])]
    pallas_call x0 -> x3, Pallas kernels: none -> 21.7 us  [back(): pl.pallas_call(functools.partial(back_kernel, deep), grid=(features // ti...]
    dot_general x4, matrix products: 20.6 us -> 8.34 us  [partial_logits(): return jnp.dot(normed, head, preferred_element_type=F32)]
    unnamed x50 -> x70, local copies, waits for them, and re-layouts: 4.04 us -> 15 us
    dot_general x1, matrix products: 1.42 us -> 5.4 us  [body(): jnp.dot(two, head, preferred_element_type=F32)]
    another operation x1 -> x2, other arithmetic: 3.93 us -> 0.66 us
    ppermute x40 -> x38, starting transfers between devices: 36.9 us -> 34.2 us  [swap(): return lax.ppermute(value, axis, [(i, i ^ bit) for i in range(size)])]
  transfers between devices with their start and end apart: 40 -> 38, of which waited for: 17 -> 24; matrix products, arithmetic and copies ran while one was open for 27% -> 9% of each run, Pallas kernels for 2% -> 12%
where the time goes in v1:
time: 191 us
  waiting for transfers between devices  88.5 us (46%)
  starting transfers between devices  34.2 us (18%)
  Pallas kernels  28.5 us (15%)
  local copies, waits for them, and re-layouts  16.7 us (9%)
  matrix products  13.7 us (7%)
  other arithmetic  7.49 us (4%)
    ppermute x38, waiting for transfers between devices, swap(): return lax.ppermute(value, axis, [(i, i ^ bit) for i in range(size)])  88.5 us
    ppermute x38, starting transfers between devices, swap(): return lax.ppermute(value, axis, [(i, i ^ bit) for i in range(size)])  34.2 us
    pallas_call x3, Pallas kernels, back(): pl.pallas_call(functools.partial(back_kernel, deep), grid=(features // ti...  21.7 us
    unnamed x70, local copies, waits for them, and re-layouts  15 us
    dot_general x4, matrix products, partial_logits(): return jnp.dot(normed, head, preferred_element_type=F32)  8.34 us
    dot_general x1, matrix products, body(): jnp.dot(two, head, preferred_element_type=F32)  5.4 us
    pallas_call x2, Pallas kernels, soften(): pl.pallas_call(functools.partial(soften_kernel, feature_count), in_specs=...  4.42 us
  transfers between devices with their start and end apart: 38, of which 24 were waited for; matrix products, arithmetic and copies ran while one was open for 9% of the time, Pallas kernels for 12%

profile of v1, /device:TPU:0, one launch (start us, length us, event | category | flops | bytes accessed | tf_op | source)
XLA Modules:
  0.0 190.7 jit_solution(4059597073251827730)
XLA Ops:
  5.4 5.4 %convolution_reduce_fusion = f32[2432]{0:T(1024)S(1)} fusion(bf16[16,2048]{1,0:T(8,128)(2,1)S(1)} %get-tuple-element.47, bf16[2048,2432]{1,0:T(8,128)(2,1)} %head.5), kind=kOutput, calls=%fused_computation.14 | convolution fusion | flops 159420032 | bytes 10036736 | tf_op jit(solution)/shard_map/dot_general | solution.py:290
  10.9 2.9 %collective-permute-start.3 = (bf16[64,2048]{1,0:T(8,128)(2,1)S(1)}, bf16[64,2048]{1,0:T(8,128)(2,1)S(1)}, u32[]{:S(2)}, u32[]{:S(2)}) collective-permute-start(bf16[64,2048]{1,0:T(8,128)(2,1)S(1)} %get-tuple-element.45), channel_id=1, source_target_pairs={{0,16},{8,24},{16,0},{24,8},{1,17},{9,25},{17,1},{25,9},{2,18},{10... | collective-permute-start | bytes 786440 | tf_op jit(solution)/shard_map/ppermute | solution.py:31
  19.7 6.7 %collective-permute-done.9 = f32[1,2432]{1,0:T(1,128)S(1)} collective-permute-done((f32[1,2432]{1,0:T(1,128)S(1)}, f32[1,2432]{1,0:T(1,128)S(1)}, u32[]{:S(2)}, u32[]{:S(2)}) %collective-permute-start.9) | collective-permute-done | bytes 9760 | tf_op jit(solution)/shard_map/ppermute | solution.py:31
  29.9 2.7 %fusion.88 = (f16[128,2432]{1,0:T(8,128)(2,1)S(1)}, f32[128,2432]{1,0:T(8,128)}) fusion(f32[128,2432]{1,0:T(8,128)S(1)} %collective-permute-done.2, bf16[2048,2432]{1,0:T(8,128)(2,1)S(1)} %bitcast.142, bf16[128,2048]{1,0:T(8,128)(2,1)S(1)} %get-tuple-element.42, f32[128]{0:T(128)S(1)} %get-tuple-element.153, f32[2048]{0:T(1024)S(1)} %bitcast.163, ...), kind=kOutput, calls=%fused_computation.310 | convolution fusion | flops 1277001728 | bytes 13615616 | tf_op jit(solution)/shard_map/dot_general | solution.py:288
  40.6 2.5 %fusion.89 = (f16[128,2432]{1,0:T(8,128)(2,1)}, f32[128,2432]{1,0:T(8,128)S(1)}) fusion(f32[128,2432]{1,0:T(8,128)S(1)} %collective-permute-done.10, bf16[2048,2432]{1,0:T(8,128)(2,1)S(1)} %bitcast.142, f32[128]{0:T(128)S(1)} %get-tuple-element.140, f32[2048]{0:T(1024)S(1)} %bitcast.165, f32[2048]{0:T(1024)S(1)} %bitcast.159, ...), kind=kOutput, calls=%fused_computation.311 | convolution fusion | flops 1278836736 | bytes 13615616 | tf_op jit(solution)/shard_map/dot_general | solution.py:288
  43.1 11.1 %collective-permute-done.11 = f16[128,2432]{1,0:T(8,128)(2,1)S(1)} collective-permute-done((f16[128,2432]{1,0:T(8,128)(2,1)S(1)}, f16[128,2432]{1,0:T(8,128)(2,1)S(1)}, u32[]{:S(2)}, u32[]{:S(2)}) %collective-permute-start.11) | collective-permute-done | bytes 622624 | tf_op jit(solution)/shard_map/ppermute | solution.py:31
  54.5 2.8 %collective-permute-done.13.second = f32[128,2432]{1,0:T(8,128)S(1)} collective-permute-done((f32[128,2432]{1,0:T(8,128)S(1)}, f32[128,2432]{1,0:T(8,128)S(1)}, u32[]{:S(2)}, u32[]{:S(2)}) %collective-permute-start.13) | collective-permute-done | bytes 1245216 | tf_op jit(solution)/shard_map/ppermute | solution.py:31
  59.9 3.2 %collective-permute-done.14 = f32[3,256]{1,0:T(4,128)S(1)} collective-permute-done((f32[3,256]{1,0:T(4,128)S(1)}, f32[3,256]{1,0:T(4,128)S(1)}, u32[]{:S(2)}, u32[]{:S(2)}) %collective-permute-start.14) | collective-permute-done | bytes 3104 | tf_op jit(solution)/shard_map/ppermute | solution.py:31
  66.9 2.7 %collective-permute-start.16 = (f32[3,256]{1,0:T(4,128)S(1)}, f32[3,256]{1,0:T(4,128)S(1)}, u32[]{:S(2)}, u32[]{:S(2)}) collective-permute-start(f32[3,256]{1,0:T(4,128)S(1)} %pad_maximum_fusion.11), channel_id=1, source_target_pairs={{0,4},{1,5},{2,6},{3,7},{4,0},{5,1},{6,2},{7,3},{8,12},{9,13},{10,... | collective-permute-start | bytes 9224 | tf_op jit(solution)/shard_map/ppermute | solution.py:31
  71.1 3.8 %copy-done = bf16[2048,2432]{1,0:T(8,128)(2,1)S(1)} copy-done((bf16[2048,2432]{1,0:T(8,128)(2,1)S(1)}, bf16[2048,2432]{1,0:T(8,128)(2,1)}, u32[]{:S(2)}) %copy-start) | copy-done | bytes 9961496
  74.9 7.2 %shard_map.79 = f32[512,2048]{1,0:T(8,128)S(1)} custom-call(bf16[512,2432]{1,0:T(8,128)(2,1)S(1)} %bitcast.146, bf16[2048,2432]{1,0:T(8,128)(2,1)S(1)} %copy-done), custom_call_target="tpu_custom_call" | custom-call | tf_op jit(solution)/shard_map/pallas_call | solution.py:203
  86.2 2.6 %collective-permute-done.17.second = f32[128,2432]{1,0:T(8,128)S(1)} collective-permute-done((f32[128,2432]{1,0:T(8,128)S(1)}, f32[128,2432]{1,0:T(8,128)S(1)}, u32[]{:S(2)}, u32[]{:S(2)}) %collective-permute-start.17) | collective-permute-done | bytes 1245216 | tf_op jit(solution)/shard_map/ppermute | solution.py:31
  93.7 2.5 %collective-permute-done.18 = f32[4,256]{1,0:T(4,128)S(1)} collective-permute-done((f32[4,256]{1,0:T(4,128)S(1)}, f32[4,256]{1,0:T(4,128)S(1)}, u32[]{:S(2)}, u32[]{:S(2)}) %collective-permute-start.18) | collective-permute-done | bytes 4128 | tf_op jit(solution)/shard_map/ppermute | solution.py:31
  100.9 8.1 %collective-permute-done.22.refs_2_ = bf16[128,2432]{1,0:T(8,128)(2,1)S(1)} collective-permute-done((bf16[128,2432]{1,0:T(8,128)(2,1)S(1)}, bf16[128,2432]{1,0:T(8,128)(2,1)S(1)}, u32[]{:S(2)}, u32[]{:S(2)}) %collective-permute-start.22) | collective-permute-done | bytes 622624 | tf_op jit(solution)/shard_map/ppermute | solution.py:31
  109.0 3.8 %copy-done.1 = bf16[2048,2432]{1,0:T(8,128)(2,1)S(1)} copy-done((bf16[2048,2432]{1,0:T(8,128)(2,1)S(1)}, bf16[2048,2432]{1,0:T(8,128)(2,1)}, u32[]{:S(2)}) %copy-start.1) | copy-done | bytes 9961496
  114.5 7.2 %shard_map.81 = f32[512,2048]{1,0:T(8,128)S(1)} custom-call(bf16[512,2432]{1,0:T(8,128)(2,1)S(1)} %bitcast.145, bf16[2048,2432]{1,0:T(8,128)(2,1)S(1)} %copy-done.1), custom_call_target="tpu_custom_call" | custom-call | tf_op jit(solution)/shard_map/pallas_call | solution.py:203
  124.1 2.7 %collective-permute-done.25 = f32[2,8,128]{2,1,0:T(8,128)S(1)} collective-permute-done((f32[2,8,128]{2,1,0:T(8,128)S(1)}, f32[2,8,128]{2,1,0:T(8,128)S(1)}, u32[]{:S(2)}, u32[]{:S(2)}) %collective-permute-start.25) | collective-permute-done | bytes 8224 | tf_op jit(solution)/shard_map/ppermute | solution.py:31
  129.4 7.2 %shard_map.83 = f32[512,2048]{1,0:T(8,128)S(1)} custom-call(bf16[512,2432]{1,0:T(8,128)(2,1)S(1)} %get-tuple-element.65.cotangent, bf16[2048,2432]{1,0:T(8,128)(2,1)S(1)} %bitcast.144), custom_call_target="tpu_custom_call" | custom-call | tf_op jit(solution)/shard_map/pallas_call | solution.py:203
  137.5 3.4 %collective-permute-done.26 = bf16[128,2048]{1,0:T(8,128)(2,1)S(1)} collective-permute-done((bf16[128,2048]{1,0:T(8,128)(2,1)S(1)}, bf16[128,2048]{1,0:T(8,128)(2,1)S(1)}, u32[]{:S(2)}, u32[]{:S(2)}) %collective-permute-start.26) | collective-permute-done | bytes 524320 | tf_op jit(solution)/shard_map/ppermute | solution.py:31
  144.7 8.8 %collective-permute-done.28 = bf16[2,64,2048]{2,1,0:T(8,128)(2,1)S(1)} collective-permute-done((bf16[2,64,2048]{2,1,0:T(8,128)(2,1)S(1)}, bf16[2,64,2048]{2,1,0:T(8,128)(2,1)S(1)}, u32[]{:S(2)}, u32[]{:S(2)}) %collective-permute-start.28) | collective-permute-done | bytes 524320 | tf_op jit(solution)/shard_map/ppermute | solution.py:31
  158.0 9.0 %collective-permute-done.30 = bf16[1,64,2048]{2,1,0:T(8,128)(2,1)S(1)} collective-permute-done((bf16[1,64,2048]{2,1,0:T(8,128)(2,1)S(1)}, bf16[1,64,2048]{2,1,0:T(8,128)(2,1)S(1)}, u32[]{:S(2)}, u32[]{:S(2)}) %collective-permute-start.30) | collective-permute-done | bytes 262176 | tf_op jit(solution)/shard_map/ppermute | solution.py:31
  170.4 4.7 %collective-permute-done.33 = bf16[1,64,1024]{2,1,0:T(8,128)(2,1)S(1)} collective-permute-done((bf16[1,64,1024]{2,1,0:T(8,128)(2,1)S(1)}, bf16[1,64,1024]{2,1,0:T(8,128)(2,1)S(1)}, u32[]{:S(2)}, u32[]{:S(2)}) %collective-permute-start.33) | collective-permute-done | bytes 131104 | tf_op jit(solution)/shard_map/ppermute | solution.py:31
  178.7 5.5 %collective-permute-done.35 = bf16[1,64,1024]{2,1,0:T(8,128)(2,1)S(1)} collective-permute-done((bf16[1,64,1024]{2,1,0:T(8,128)(2,1)S(1)}, bf16[1,64,1024]{2,1,0:T(8,128)(2,1)S(1)}, u32[]{:S(2)}, u32[]{:S(2)}) %collective-permute-start.35) | collective-permute-done | bytes 131104 | tf_op jit(solution)/shard_map/ppermute | solution.py:31
  186.5 2.9 %collective-permute-done.37 = f32[2,64]{1,0:T(2,128)S(1)} collective-permute-done((f32[2,64]{1,0:T(2,128)S(1)}, f32[2,64]{1,0:T(2,128)S(1)}, u32[]{:S(2)}, u32[]{:S(2)}) %collective-permute-start.37) | collective-permute-done | bytes 544 | tf_op jit(solution)/shard_map/ppermute | solution.py:31
  (230 shorter events, 69.7 us)
Async XLA Ops:
  4.9 9.7 %collective-permute-start.1 = (f32[8,128]{1,0:T(8,128)S(1)}, f32[8,128]{1,0:T(8,128)S(1)}, u32[]{:S(2)}, u32[]{:S(2)}) collective-permute-start(f32[8,128]{1,0:T(8,128)S(1)} %get-tuple-element.43.sums_a), channel_id=1, source_target_pairs={{0,8},{8,0},{16,24},{24,16},{1,9},{9,1},{17,25},{25,17},{2,10},{10... | collective-permute-start | bytes 12296 | tf_op jit(solution)/shard_map/ppermute | solution.py:31
  10.9 15.4 %collective-permute-start.3 = (bf16[64,2048]{1,0:T(8,128)(2,1)S(1)}, bf16[64,2048]{1,0:T(8,128)(2,1)S(1)}, u32[]{:S(2)}, u32[]{:S(2)}) collective-permute-start(bf16[64,2048]{1,0:T(8,128)(2,1)S(1)} %get-tuple-element.45), channel_id=1, source_target_pairs={{0,16},{8,24},{16,0},{24,8},{1,17},{9,25},{17,1},{25,9},{2,18},{10... | collective-permute-start | bytes 786440 | tf_op jit(solution)/shard_map/ppermute | solution.py:31
  13.9 12.5 %collective-permute-start.4 = (bf16[64,2048]{1,0:T(8,128)(2,1)S(1)}, bf16[64,2048]{1,0:T(8,128)(2,1)S(1)}, u32[]{:S(2)}, u32[]{:S(2)}) collective-permute-start(bf16[64,2048]{1,0:T(8,128)(2,1)S(1)} %get-tuple-element.46), channel_id=1, source_target_pairs={{0,24},{8,16},{16,8},{24,0},{1,25},{9,17},{17,9},{25,1},{2,26},{10... | collective-permute-start | bytes 786440 | tf_op jit(solution)/shard_map/ppermute | solution.py:31
  15.1 11.2 %collective-permute-start.9 = (f32[1,2432]{1,0:T(1,128)S(1)}, f32[1,2432]{1,0:T(1,128)S(1)}, u32[]{:S(2)}, u32[]{:S(2)}) collective-permute-start(f32[1,2432]{1,0:T(1,128)S(1)} %reshape_add_fusion), channel_id=1, source_target_pairs={{0,16},{8,24},{16,0},{24,8},{1,17},{9,25},{17,1},{25,9},{2,18},{10... | collective-permute-start | bytes 29192 | tf_op jit(solution)/shard_map/ppermute | solution.py:31
  18.9 11.0 %collective-permute-start.2 = (f32[128,2432]{1,0:T(8,128)S(1)}, f32[128,2432]{1,0:T(8,128)S(1)}, u32[]{:S(2)}, u32[]{:S(2)}) collective-permute-start(f32[128,2432]{1,0:T(8,128)S(1)} %fusion.4), channel_id=1, source_target_pairs={{0,8},{8,0},{16,24},{24,16},{1,9},{9,1},{17,25},{25,17},{2,10},{10... | collective-permute-start | bytes 3735560 | tf_op jit(solution)/shard_map/ppermute | solution.py:31
  19.0 13.6 %collective-permute-start.7 = (f32[2,8,128]{2,1,0:T(8,128)S(1)}, f32[2,8,128]{2,1,0:T(8,128)S(1)}, u32[]{:S(2)}, u32[]{:S(2)}) collective-permute-start(f32[2,8,128]{2,1,0:T(8,128)S(1)} %pad_maximum_fusion.8), channel_id=1, source_target_pairs={{0,16},{8,24},{16,0},{24,8},{1,17},{9,25},{17,1},{25,9},{2,18},{10... | collective-permute-start | bytes 24584 | tf_op jit(solution)/shard_map/ppermute | solution.py:31
  26.4 8.0 %collective-permute-start.6 = (bf16[2,32,2048]{2,1,0:T(8,128)(2,1)S(1)}, bf16[2,32,2048]{2,1,0:T(8,128)(2,1)S(1)}, u32[]{:S(2)}, u32[]{:S(2)}) collective-permute-start(bf16[2,32,2048]{2,1,0:T(8,128)(2,1)S(1)} %pad_maximum_fusion.5), channel_id=1, source_target_pairs={{0,1},{1,0},{2,3},{3,2},{4,5},{5,4},{6,7},{7,6},{8,9},{9,8},{10,11... | collective-permute-start | bytes 786440 | tf_op jit(solution)/shard_map/ppermute | solution.py:31
  28.3 7.6 %collective-permute-start.5 = (bf16[2,32,2048]{2,1,0:T(8,128)(2,1)S(1)}, bf16[2,32,2048]{2,1,0:T(8,128)(2,1)S(1)}, u32[]{:S(2)}, u32[]{:S(2)}) collective-permute-start(bf16[2,32,2048]{2,1,0:T(8,128)(2,1)S(1)} %pad_maximum_fusion.5), channel_id=1, source_target_pairs={{0,2},{1,3},{2,0},{3,1},{4,6},{5,7},{6,4},{7,5},{8,10},{9,11},{10,... | collective-permute-start | bytes 786440 | tf_op jit(solution)/shard_map/ppermute | solution.py:31
  37.7 16.4 %collective-permute-start.11 = (f16[128,2432]{1,0:T(8,128)(2,1)S(1)}, f16[128,2432]{1,0:T(8,128)(2,1)S(1)}, u32[]{:S(2)}, u32[]{:S(2)}) collective-permute-start(f16[128,2432]{1,0:T(8,128)(2,1)S(1)} %get-tuple-element.48), channel_id=1, source_target_pairs={{0,16},{8,24},{16,0},{24,8},{1,17},{9,25},{17,1},{25,9},{2,18},{10... | collective-permute-start | bytes 1867784 | tf_op jit(solution)/shard_map/ppermute | solution.py:31
  66.9 15.2 %collective-permute-start.16 = (f32[3,256]{1,0:T(4,128)S(1)}, f32[3,256]{1,0:T(4,128)S(1)}, u32[]{:S(2)}, u32[]{:S(2)}) collective-permute-start(f32[3,256]{1,0:T(4,128)S(1)} %pad_maximum_fusion.11), channel_id=1, source_target_pairs={{0,4},{1,5},{2,6},{3,7},{4,0},{5,1},{6,2},{7,3},{8,12},{9,13},{10,... | collective-permute-start | bytes 9224 | tf_op jit(solution)/shard_map/ppermute | solution.py:31
  69.6 15.4 %collective-permute-start.12 = (f16[128,2432]{1,0:T(8,128)(2,1)}, f16[128,2432]{1,0:T(8,128)(2,1)S(1)}, u32[]{:S(2)}, u32[]{:S(2)}) collective-permute-start(f16[128,2432]{1,0:T(8,128)(2,1)} %get-tuple-element.54), channel_id=1, source_target_pairs={{0,16},{8,24},{16,0},{24,8},{1,17},{9,25},{17,1},{25,9},{2,18},{10... | collective-permute-start | bytes 1867784 | tf_op jit(solution)/shard_map/ppermute | solution.py:31
  93.1 15.9 %collective-permute-start.22 = (bf16[128,2432]{1,0:T(8,128)(2,1)S(1)}, bf16[128,2432]{1,0:T(8,128)(2,1)S(1)}, u32[]{:S(2)}, u32[]{:S(2)}) collective-permute-start(bf16[128,2432]{1,0:T(8,128)(2,1)S(1)} %copy-done.4), channel_id=1, source_target_pairs={{0,16},{8,24},{16,0},{24,8},{1,17},{9,25},{17,1},{25,9},{2,18},{10... | collective-permute-start | bytes 1867784 | tf_op jit(solution)/shard_map/ppermute | solution.py:31
  100.0 21.7 %collective-permute-start.20 = (f32[4,256]{1,0:T(4,128)S(1)}, f32[4,256]{1,0:T(4,128)S(1)}, u32[]{:S(2)}, u32[]{:S(2)}) collective-permute-start(f32[4,256]{1,0:T(4,128)S(1)} %pad_maximum_fusion.14), channel_id=1, source_target_pairs={{0,4},{1,5},{2,6},{3,7},{4,0},{5,1},{6,2},{7,3},{8,12},{9,13},{10,... | collective-permute-start | bytes 12296 | tf_op jit(solution)/shard_map/ppermute | solution.py:31
  100.4 26.4 %collective-permute-start.21 = (bf16[128,2432]{1,0:T(8,128)(2,1)S(1)}, bf16[128,2432]{1,0:T(8,128)(2,1)S(1)}, u32[]{:S(2)}, u32[]{:S(2)}) collective-permute-start(bf16[128,2432]{1,0:T(8,128)(2,1)S(1)} %copy-done.4), channel_id=1, source_target_pairs={{0,8},{8,0},{16,24},{24,16},{1,9},{9,1},{17,25},{25,17},{2,10},{10... | collective-permute-start | bytes 1867784 | tf_op jit(solution)/shard_map/ppermute | solution.py:31
  100.4 37.1 %collective-permute-start.27 = (bf16[128,2048]{1,0:T(8,128)(2,1)}, bf16[128,2048]{1,0:T(8,128)(2,1)S(1)}, u32[]{:S(2)}, u32[]{:S(2)}) collective-permute-start(bf16[128,2048]{1,0:T(8,128)(2,1)} %slice.465), channel_id=1, source_target_pairs={{0,1},{1,0},{2,3},{3,2},{4,5},{5,4},{6,7},{7,6},{8,9},{9,8},{10,11... | collective-permute-start | bytes 1572872 | tf_op jit(solution)/shard_map/ppermute | solution.py:31
  109.0 17.9 %collective-permute-start.23 = (bf16[128,2432]{1,0:T(8,128)(2,1)S(1)}, bf16[128,2432]{1,0:T(8,128)(2,1)S(1)}, u32[]{:S(2)}, u32[]{:S(2)}) collective-permute-start(bf16[128,2432]{1,0:T(8,128)(2,1)S(1)} %collective-permute-done.22.refs_2_), channel_id=1, source_target_pairs={{0,8},{8,0},{16,24},{24,16},{1,9},{9,1},{17,25},{25,17},{2,10},{10... | collective-permute-start | bytes 1867784 | tf_op jit(solution)/shard_map/ppermute | solution.py:31
  127.7 13.1 %collective-permute-start.26 = (bf16[128,2048]{1,0:T(8,128)(2,1)S(1)}, bf16[128,2048]{1,0:T(8,128)(2,1)S(1)}, u32[]{:S(2)}, u32[]{:S(2)}) collective-permute-start(bf16[128,2048]{1,0:T(8,128)(2,1)S(1)} %slice.464), channel_id=1, source_target_pairs={{0,1},{1,0},{2,3},{3,2},{4,5},{5,4},{6,7},{7,6},{8,9},{9,8},{10,11... | collective-permute-start | bytes 1572872 | tf_op jit(solution)/shard_map/ppermute | solution.py:31
  141.4 12.2 %collective-permute-start.28 = (bf16[2,64,2048]{2,1,0:T(8,128)(2,1)S(1)}, bf16[2,64,2048]{2,1,0:T(8,128)(2,1)S(1)}, u32[]{:S(2)}, u32[]{:S(2)}) collective-permute-start(bf16[2,64,2048]{2,1,0:T(8,128)(2,1)S(1)} %fusion.6), channel_id=1, source_target_pairs={{0,2},{1,3},{2,0},{3,1},{4,6},{5,7},{6,4},{7,5},{8,10},{9,11},{10,... | collective-permute-start | bytes 1572872 | tf_op jit(solution)/shard_map/ppermute | solution.py:31
  143.0 11.8 %collective-permute-start.29 = (bf16[256,1024]{1,0:T(8,128)(2,1)S(1)}, bf16[256,1024]{1,0:T(8,128)(2,1)S(1)}, u32[]{:S(2)}, u32[]{:S(2)}) collective-permute-start(bf16[256,1024]{1,0:T(8,128)(2,1)S(1)} %pad_maximum_fusion.3), channel_id=1, source_target_pairs={{0,1},{1,0},{2,3},{3,2},{4,5},{5,4},{6,7},{7,6},{8,9},{9,8},{10,11... | collective-permute-start | bytes 1572872 | tf_op jit(solution)/shard_map/ppermute | solution.py:31
  155.1 12.0 %collective-permute-start.30 = (bf16[1,64,2048]{2,1,0:T(8,128)(2,1)S(1)}, bf16[1,64,2048]{2,1,0:T(8,128)(2,1)S(1)}, u32[]{:S(2)}, u32[]{:S(2)}) collective-permute-start(bf16[1,64,2048]{2,1,0:T(8,128)(2,1)S(1)} %dynamic-slice_convert_fusion), channel_id=1, source_target_pairs={{0,4},{1,5},{2,6},{3,7},{4,0},{5,1},{6,2},{7,3},{8,12},{9,13},{10,... | collective-permute-start | bytes 786440 | tf_op jit(solution)/shard_map/ppermute | solution.py:31
  155.5 12.1 %collective-permute-start.32 = (bf16[256,1024]{1,0:T(8,128)(2,1)S(1)}, bf16[256,1024]{1,0:T(8,128)(2,1)S(1)}, u32[]{:S(2)}, u32[]{:S(2)}) collective-permute-start(bf16[256,1024]{1,0:T(8,128)(2,1)S(1)} %pad_maximum_fusion.4), channel_id=1, source_target_pairs={{0,1},{1,0},{2,3},{3,2},{4,5},{5,4},{6,7},{7,6},{8,9},{9,8},{10,11... | collective-permute-start | bytes 1572872 | tf_op jit(solution)/shard_map/ppermute | solution.py:31
  157.2 10.4 %collective-permute-start.31 = (bf16[2,64,1024]{2,1,0:T(8,128)(2,1)S(1)}, bf16[2,64,1024]{2,1,0:T(8,128)(2,1)S(1)}, u32[]{:S(2)}, u32[]{:S(2)}) collective-permute-start(bf16[2,64,1024]{2,1,0:T(8,128)(2,1)S(1)} %fusion.19), channel_id=1, source_target_pairs={{0,2},{1,3},{2,0},{3,1},{4,6},{5,7},{6,4},{7,5},{8,10},{9,11},{10,... | collective-permute-start | bytes 786440 | tf_op jit(solution)/shard_map/ppermute | solution.py:31
  167.8 9.5 %collective-permute-start.34 = (bf16[2,64,1024]{2,1,0:T(8,128)(2,1)S(1)}, bf16[2,64,1024]{2,1,0:T(8,128)(2,1)S(1)}, u32[]{:S(2)}, u32[]{:S(2)}) collective-permute-start(bf16[2,64,1024]{2,1,0:T(8,128)(2,1)S(1)} %fusion.20), channel_id=1, source_target_pairs={{0,2},{1,3},{2,0},{3,1},{4,6},{5,7},{6,4},{7,5},{8,10},{9,11},{10,... | collective-permute-start | bytes 786440 | tf_op jit(solution)/shard_map/ppermute | solution.py:31
  167.9 7.2 %collective-permute-start.33 = (bf16[1,64,1024]{2,1,0:T(8,128)(2,1)S(1)}, bf16[1,64,1024]{2,1,0:T(8,128)(2,1)S(1)}, u32[]{:S(2)}, u32[]{:S(2)}) collective-permute-start(bf16[1,64,1024]{2,1,0:T(8,128)(2,1)S(1)} %dynamic-slice_convert_fusion.2), channel_id=1, source_target_pairs={{0,4},{1,5},{2,6},{3,7},{4,0},{5,1},{6,2},{7,3},{8,12},{9,13},{10,... | collective-permute-start | bytes 393224 | tf_op jit(solution)/shard_map/ppermute | solution.py:31
  (49 other events, 267.9 us)

commit v2 on v1

--- a/solution.py
+++ b/solution.py
@@ -106,6 +106,52 @@
     )(at, hidden, vectors)
 
 
+def ahead_kernel(feature_count, first, second, sums_a, sums_b, parts, two, head, *outs):
+    out_a, out_b, out_row, normed = outs
+    tokens = first.shape[0]
+
+    @pl.when(pl.program_id(0) == 0)
+    def _():
+        steer, gain = parts[0:1, :], parts[2:3, :]
+        for index, (block, sums) in enumerate(((first, sums_a), (second, sums_b))):
+            radius = jnp.sqrt(turn(sums[...])[:, 0:1] / feature_count + EPSILON)
+            values = block[...].astype(F32) + steer
+            normed[index * tokens : (index + 1) * tokens, :] = (
+                gain * values / radius
+            ).astype(BF16)
+        normed[2 * tokens :, :] = two[...]
+
+    product = jnp.dot(normed[...], head[...], preferred_element_type=F32)
+    out_a[...] = product[:tokens]
+    out_b[...] = product[tokens : 2 * tokens]
+    out_row[...] = product[2 * tokens : 2 * tokens + 8]
+
+
+def ahead(first, second, sums_a, sums_b, parts, two, head, feature_count):
+    tokens, width = first.shape
+    vocab = head.shape[1]
+    tile = 256
+    fixed = [
+        pl.BlockSpec(value.shape, lambda i: (0, 0))
+        for value in (first, second, sums_a, sums_b, parts, two)
+    ]
+    out = pl.BlockSpec((tokens, tile), lambda i: (0, i))
+    return pl.pallas_call(
+        functools.partial(ahead_kernel, feature_count),
+        grid=(pl.cdiv(vocab, tile),),
+        in_specs=fixed + [pl.BlockSpec((width, tile), lambda i: (0, i))],
+        out_specs=[out, out, pl.BlockSpec((8, tile), lambda i: (0, i))],
+        out_shape=[
+            jax.ShapeDtypeStruct((tokens, vocab), F32),
+            jax.ShapeDtypeStruct((tokens, vocab), F32),
+            jax.ShapeDtypeStruct((8, vocab), F32),
+        ],
+        scratch_shapes=[pltpu.VMEM((2 * tokens + two.shape[0], width), BF16)],
+        compiler_params=params(52),
+        cost_estimate=LIGHT,
+    )(first, second, sums_a, sums_b, parts, two, head)
+
+
 def soften_kernel(feature_count, at, first, second, row, sums_a, sums_b, *outs):
     both_out, stats, tile = outs
     tokens = first.shape[0]
@@ -209,7 +255,7 @@
         ],
         out_specs=pl.BlockSpec((rows, tile), lambda i: (0, i)),
         out_shape=jax.ShapeDtypeStruct((rows, features), F32),
-        compiler_params=params(20),
+        compiler_params=params(52),
         cost_estimate=LIGHT,
     )(cotangent, head)
 
@@ -223,16 +269,15 @@
     return jnp.stack([peak, total, mean] + [first[i] + second[i] for i in range(3, len(first))])
 
 
-def exchange(value, size):
-    half = value.shape[1] // 2
-    other = swap(value, "vocab", 1, size)
-    aligned = jnp.concatenate([other[:3, half:], other[:3, :half]], axis=1)
+def exchange(value, size, beside):
+    other, beside = lax.optimization_barrier((swap(value, "vocab", 1, size), beside))
+    aligned = other[:3].reshape(3, 2, 2, -1)[:, :, ::-1].reshape(3, -1)
     value = merge(value, jnp.concatenate([aligned, other[3:]], axis=0))
     bit = PAIR
     while bit < size:
         value = merge(value, swap(value, "vocab", bit, size))
         bit *= 2
-    return value
+    return value, beside
 
 
 def body(hidden, steer, tangent, gain, head, target):
@@ -281,17 +326,11 @@
     by_z = swap(near, "vocab", 1, vocab_size)
     steer_part, gain_part = parts[0], parts[2]
 
-    def partial_logits(block, sums_of):
-        radius = jnp.sqrt(sums_of[0] / feature_count + EPSILON)
-        values = block.astype(F32) + steer_part
-        normed = (gain_part * values / radius[:, None]).astype(BF16)
-        return jnp.dot(normed, head, preferred_element_type=F32)
-
-    row = jnp.sum(jnp.dot(two, head, preferred_element_type=F32), axis=0, keepdims=True)
+    kept, given, row = ahead(own, mate, sums_0, sums_1, parts, two, head, feature_count)
+    row = row[0:1] + row[1:2]
     row = row + swap(row, "seq", 1, seq_size)
     tangent_row = row + swap(row, "seq", 2, seq_size)
-    given = swap(partial_logits(mate, sums_1), "seq", 1, seq_size)
-    summed_0 = partial_logits(own, sums_0) + given
+    summed_0 = kept + swap(given, "seq", 1, seq_size)
     send_0, tangent_row = lax.optimization_barrier((summed_0.astype(jnp.float16), tangent_row))
     got_2 = swap(send_0, "seq", 2, seq_size)
     by_y, by_z, over_2, over_3, both, _ = lax.optimization_barrier(
@@ -304,40 +343,86 @@
         jnp.concatenate([over[:quarter], by_y[i], by_z[i], over[quarter:]], axis=0)
         for i, over in enumerate((over_2, over_3))
     ]
-    given = swap(partial_logits(blocks[3], sums[3]), "seq", 1, seq_size)
-    summed_2 = partial_logits(blocks[2], sums[2]) + given
+    kept, given, _ = ahead(
+        blocks[2], blocks[3], sums[2], sums[3], parts, two, head, feature_count
+    )
+    summed_2 = kept + swap(given, "seq", 1, seq_size)
     send_2, got_2 = lax.optimization_barrier((summed_2.astype(jnp.float16), got_2))
     got_0 = swap(send_2, "seq", 2, seq_size)
 
     half = rows // 2
 
-    def half_of(base, summed, got, where, extra):
+    def half_of(base, summed, got, where):
         full = summed + got.astype(F32)
         mates = swap(full, "seq", 1, seq_size)
         both, stats = soften(
             where, full, mates, tangent_row, sums[base], sums[base + 1], feature_count
         )
-        stats = stats[:3]
-        joint = exchange(jnp.concatenate([stats] + extra), vocab_size)
-        raw = back(both.reshape(2 * half, -1), head)
-        scale = jnp.exp(stats[0] - joint[0]) / joint[1]
-        lean = scale * (stats[2] - joint[2])
-        plain = scale[:, None] * raw[:half]
-        ggn = scale[:, None] * raw[half:] + lean[:, None] * raw[:half]
-        return plain, ggn[half // 2 :].astype(BF16), ggn[: half // 2], joint
-
-    plain_other, theirs_other, kept_other, _ = half_of(2, summed_2, got_2, other_places, [])
-    got_0, target, theirs_other = lax.optimization_barrier((got_0, target, theirs_other))
-    got_other = swap(theirs_other, "vocab", 1, vocab_size)
+        return back(both.reshape(2 * half, -1), head), stats[:3]
+
+    raw_other, stats_other = half_of(2, summed_2, got_2, other_places)
+    got_0, target, raw_other = lax.optimization_barrier((got_0, target, raw_other))
+    target_2 = swap(target, "seq", 2, seq_size)
+    raw_own, stats_own = half_of(0, summed_0, got_0, own_places)
+    stats = jnp.concatenate([stats_own, stats_other], axis=1)
     own_total = jnp.sum(target.astype(F32), axis=1)
-    plain_own, theirs_own, kept_own, joint = half_of(
-        0, summed_0, got_0, own_places, [jnp.concatenate([own_total, own_total])[None]]
-    )
-
-    target_2 = swap(target, "seq", 2, seq_size)
+    joint, (raw_own,) = exchange(
+        jnp.concatenate([stats, jnp.tile(own_total, seq_size)[None]]), vocab_size, (raw_own,)
+    )
+    scale = jnp.exp(stats[0] - joint[0]) / joint[1]
+    lean = scale * (stats[2] - joint[2])
+
+    form = (2, PAIR, length // 2, share)
+
+    def spread(values):
+        return values.reshape(*form, -1)
+
+    scale_5, lean_5 = scale.reshape(*form, 1), lean.reshape(*form, 1)
+    parted = ((0, width // 2), (width // 2, width))
+
+    def plain_of(begin, end):
+        return scale_5 * spread(
+            jnp.concatenate([raw_own[:half, begin:end], raw_other[:half, begin:end]])
+        )
+
+    def ggn_of(begin, end):
+        plain = jnp.concatenate([raw_own[:half, begin:end], raw_other[:half, begin:end]])
+        tilted = jnp.concatenate([raw_own[half:, begin:end], raw_other[half:, begin:end]])
+        return scale_5 * spread(tilted) + lean_5 * spread(plain)
+
+    def halve(values, bit):
+        if bit == 1:
+            return values[:, 1:].astype(BF16), values[:, :1]
+        step = bit // PAIR
+        if step < length // 2:
+            shape = values.shape
+            values = values.reshape(*shape[:2], -1, 2, *shape[3:])
+            place, axis = (z // step) % 2, 3
+            sent = lax.dynamic_index_in_dim(values, 1 - place, axis, False)
+            kept = lax.dynamic_index_in_dim(values, place, axis, False)
+        else:
+            place = (z // step) ^ chip
+            sent = lax.dynamic_index_in_dim(values, 1 - place, 0, True)
+            kept = lax.dynamic_index_in_dim(values, place, 0, True)
+        return sent.astype(BF16), kept
+
+    z_bits = []
+    bit = PAIR
+    while bit < vocab_size:
+        z_bits.append(bit)
+        bit *= 2
+    y_first, z_first = [1] + z_bits, z_bits + [1]
+    items = [
+        [list(bits), 0, *halve(ggn_of(*part), bits[0])]
+        for bits, part in ((y_first, parted[0]), (z_first, parted[1]))
+    ]
+
+    target_2, joint_total, items[0][2], items[1][2] = lax.optimization_barrier(
+        (target_2, joint[3, :tokens], items[0][2], items[1][2])
+    )
     target_1 = swap(target, "seq", 1, seq_size)
     target_3 = swap(target_2, "seq", 1, seq_size)
-    total_0 = jnp.broadcast_to(joint[3, :tokens], (8, tokens))
+    total_0 = jnp.broadcast_to(joint_total, (8, tokens))
     total_1 = swap(total_0, "seq", 1, seq_size)
     both = swap(jnp.stack([total_0, total_1]), "seq", 2, seq_size)
     ordered, columns = order(
@@ -345,67 +430,29 @@
         [target, target_1, target_2, target_3],
         [total_0, total_1, both[0], both[1]],
     )
-    ordered, theirs_own = lax.optimization_barrier((ordered, theirs_own))
     weighed = back(ordered, head)
     inverse = columns[:, 0:1]
-    gradients = [
-        plain - inverse[begin : begin + half] * weighed[begin : begin + half]
-        for plain, begin in ((plain_own, 0), (plain_other, half))
-    ]
-
-    def halve(joined, bit):
-        if bit < length // 2:
-            joined = joined.reshape(-1, 2, share, joined.shape[-1])
-            place, axis = (z // bit) % 2, 1
-        else:
-            joined = joined.reshape(2, -1, share, joined.shape[-1])
-            place, axis = (z // bit) ^ chip, 0
-        sent = lax.dynamic_index_in_dim(joined, 1 - place, axis, False)
-        kept = lax.dynamic_index_in_dim(joined, place, axis, False)
-        return sent.astype(BF16), kept
-
-    got_own = swap(theirs_own, "vocab", 1, vocab_size)
-    chunks = []
-    for begin in (0, width // 2):
-        part = [g[:, begin : begin + width // 2] for g in gradients]
-        chunks.append(
-            (
-                jnp.concatenate([p[half // 2 :] for p in part]).astype(BF16),
-                jnp.concatenate([p[: half // 2] for p in part]),
-            )
-        )
-    got_own, got_other, *sends = lax.optimization_barrier(
-        (got_own, got_other, chunks[0][0], chunks[1][0])
-    )
-    ggn = jnp.concatenate(
-        [kept_own + got_own.astype(F32), kept_other + got_other.astype(F32)], axis=0
-    )
-    bits = [1]
-    bit = 1
-    while bit < length:
-        bits.append(bit * PAIR)
-        bit *= 2
-    items = [[1, *halve(ggn, 1)]] + [[0, sent, chunk[1]] for sent, chunk in zip(sends, chunks)]
+    for tick, (begin, end) in enumerate(parted):
+        values = plain_of(begin, end) - spread(inverse * weighed[:, begin:end])
+        items.append([list(y_first), tick + 1, *halve(values, 1)])
+
     tick = 0
-    while any(item[0] < len(bits) for item in items):
-        active = [
-            i for i, item in enumerate(items) if item[0] < len(bits) and i <= tick + 1
-        ]
-        got = [swap(items[i][1], "vocab", bits[items[i][0]], vocab_size) for i in active]
-        waiting = [i for i, item in enumerate(items) if i not in active and item[0] == 0]
-        tied = lax.optimization_barrier((got, [items[i][1] for i in waiting]))
-        for i, value in zip(waiting, tied[1]):
-            items[i][1] = value
-        for i, value in zip(active, tied[0]):
-            step, _, kept = items[i]
-            joined = kept + value.astype(F32)
-            if step + 1 < len(bits):
-                items[i] = [step + 1, *halve(joined, bits[step + 1] // PAIR)]
-            else:
-                items[i] = [step + 1, None, joined.reshape(share, -1)]
+    while any(item[0] for item in items):
+        active = [item for item in items if item[0] and item[1] <= tick]
+        waiting = [item for item in items if item[1] > tick]
+        got = [swap(item[2], "vocab", item[0][0], vocab_size) for item in active]
+        got, held = lax.optimization_barrier((got, [item[2] for item in waiting]))
+        for item, value in zip(waiting, held):
+            item[2] = value
+        for item, value in zip(active, got):
+            item[0].pop(0)
+            item[3] = item[3] + value.astype(F32)
+            if item[0]:
+                item[2:] = halve(item[3], item[0][0])
         tick += 1
-    ggn_mine = items[0][2]
-    grad_mine = jnp.concatenate([items[1][2], items[2][2]], axis=1)
+    summed = [item[3].reshape(share, -1) for item in items]
+    ggn_mine = jnp.concatenate(summed[:2], axis=1)
+    grad_mine = jnp.concatenate(summed[2:], axis=1)
 
     first_row = vocab_index * share
     owner = first_row // tokens

time: 191 us -> 218 us (1.14)
  Pallas kernels: 28.5 us -> 64.5 us
  waiting for transfers between devices: 88.5 us -> 61.4 us
  other arithmetic: 7.49 us -> 28.1 us
  matrix products: 13.7 us -> 0 us
  local copies, waits for them, and re-layouts: 16.7 us -> 24.1 us
  starting transfers between devices: 34.2 us -> 37.1 us
    ppermute x38 -> x37, waiting for transfers between devices: 88.5 us -> 61.4 us  [swap(): return lax.ppermute(value, axis, [(i, i ^ bit) for i in range(size)])]
    pallas_call x0 -> x2, Pallas kernels: none -> 21.6 us  [ahead(): pl.pallas_call(functools.partial(ahead_kernel, feature_count), grid=(pl.c...]
    pallas_call x3, Pallas kernels: 21.7 us -> 36.1 us  [back(): pl.pallas_call(functools.partial(back_kernel, deep), grid=(features // ti...]
    dot_general x5 -> x0, matrix products: 13.7 us -> none  [the longest x4 8.34 us: partial_logits(): return jnp.dot(normed, head, preferred_element_type=F32)]
    slice x11 -> x13, local copies, waits for them, and re-layouts: 1.28 us -> 8.69 us  [the longest x1 4.36 us: ggn_of(): raw_other[half:, begin:end]]
    concatenate x5, other arithmetic: 0.31 us -> 5.94 us  [the longest x2 2.96 us: ggn_of(): jnp.concatenate([raw_own[half:, begin:end], raw_other[half:, begin:end]])]
    convert_element_type x0 -> x2, other arithmetic: none -> 4.98 us  [the longest x1 2.61 us: body(): summed_0.astype(jnp.float16)]
    add x13, other arithmetic: 2.42 us -> 6.2 us  [the longest x1 4.01 us: ggn_of(): return scale_5 * spread(tilted) + lean_5 * spread(plain)]
  transfers between devices with their start and end apart: 38 -> 37, of which waited for: 24 -> 18; matrix products, arithmetic and copies ran while one was open for 9% -> 16% of each run, Pallas kernels for 12% -> 24%
where the time goes in v2:
time: 218 us; the launch traced here: 217 us
  Pallas kernels  64.5 us (30%)
  waiting for transfers between devices  61.4 us (28%)
  starting transfers between devices  37.1 us (17%)
  other arithmetic  28.1 us (13%)
  local copies, waits for them, and re-layouts  24.1 us (11%)
    ppermute x37, waiting for transfers between devices, swap(): return lax.ppermute(value, axis, [(i, i ^ bit) for i in range(size)])  61.4 us
    ppermute x37, starting transfers between devices, swap(): return lax.ppermute(value, axis, [(i, i ^ bit) for i in range(size)])  37.1 us
    pallas_call x3, Pallas kernels, back(): pl.pallas_call(functools.partial(back_kernel, deep), grid=(features // ti...  36.1 us
    pallas_call x2, Pallas kernels, ahead(): pl.pallas_call(functools.partial(ahead_kernel, feature_count), grid=(pl.c...  21.6 us
    unnamed x70, local copies, waits for them, and re-layouts  11.4 us
    pallas_call x2, Pallas kernels, soften(): pl.pallas_call(functools.partial(soften_kernel, feature_count), in_specs=...  4.41 us
    slice x1, local copies, waits for them, and re-layouts, ggn_of(): raw_other[half:, begin:end]  4.36 us
  transfers between devices with their start and end apart: 37, of which 18 were waited for; matrix products, arithmetic and copies ran while one was open for 16% of the time, Pallas kernels for 24%

profile of v2, /device:TPU:0, one launch (start us, length us, event | category | flops | bytes accessed | tf_op | source)
XLA Modules:
  0.0 216.5 jit_solution(2490251966185366801)
XLA Ops:
  4.9 3.0 %collective-permute-start.3 = (bf16[64,2048]{1,0:T(8,128)(2,1)S(1)}, bf16[64,2048]{1,0:T(8,128)(2,1)S(1)}, u32[]{:S(2)}, u32[]{:S(2)}) collective-permute-start(bf16[64,2048]{1,0:T(8,128)(2,1)S(1)} %get-tuple-element.59), channel_id=1, source_target_pairs={{0,16},{8,24},{16,0},{24,8},{1,17},{9,25},{17,1},{25,9},{2,18},{10... | collective-permute-start | bytes 786440 | tf_op jit(solution)/shard_map/ppermute | solution.py:31
  10.1 4.9 %collective-permute-done.3 = bf16[64,2048]{1,0:T(8,128)(2,1)S(1)} collective-permute-done((bf16[64,2048]{1,0:T(8,128)(2,1)S(1)}, bf16[64,2048]{1,0:T(8,128)(2,1)S(1)}, u32[]{:S(2)}, u32[]{:S(2)}) %collective-permute-start.3) | collective-permute-done | bytes 262176 | tf_op jit(solution)/shard_map/ppermute | solution.py:31
  15.1 10.9 %shard_map.78 = (f32[128,2432]{1,0:T(8,128)}, f32[128,2432]{1,0:T(8,128)}, f32[8,2432]{1,0:T(8,128)S(1)}) custom-call(bf16[128,2048]{1,0:T(8,128)(2,1)S(1)} %get-tuple-element.53.first, bf16[128,2048]{1,0:T(8,128)(2,1)S(1)} %collective-permute-done.second, f32[8,128]{1,0:T(8,128)S(1)} %get-tuple-element.55.sums_a, ...), custom_call_target="tpu_custom_call" | custom-call | tf_op jit(solution)/shard_map/pallas_call | solution.py:139
  32.6 2.6 %fusion.51 = (f16[128,2432]{1,0:T(8,128)(2,1)S(1)}, f32[128,2432]{1,0:T(8,128)}) fusion(f32[128,2432]{1,0:T(8,128)} %get-tuple-element.57, f32[128,2432]{1,0:T(8,128)S(1)} %collective-permute-done.2), kind=kLoop, calls=%fused_computation.258 | loop fusion | flops 622592 | bytes 4358144 | tf_op jit(solution)/shard_map/convert_element_type | solution.py:334
  35.2 2.4 %collective-permute-done.6 = bf16[2,32,2048]{2,1,0:T(8,128)(2,1)S(1)} collective-permute-done((bf16[2,32,2048]{2,1,0:T(8,128)(2,1)S(1)}, bf16[2,32,2048]{2,1,0:T(8,128)(2,1)S(1)}, u32[]{:S(2)}, u32[]{:S(2)}) %collective-permute-start.6) | collective-permute-done | bytes 262176 | tf_op jit(solution)/shard_map/ppermute | solution.py:31
  39.4 10.7 %shard_map.79 = (f32[128,2432]{1,0:T(8,128)}, f32[128,2432]{1,0:T(8,128)}, f32[8,2432]{1,0:T(8,128)}) custom-call(bf16[128,2048]{1,0:T(8,128)(2,1)S(1)} %pad_maximum_fusion.4.first, bf16[128,2048]{1,0:T(8,128)(2,1)S(1)} %pad_maximum_fusion.5.second, f32[8,128]{1,0:T(8,128)S(1)} %get-tuple-element.169.sums_a, f32[8,128]{1,0:T(8,128)S(1)} %get-tuple-element.168.sums_b, ...), custom_call_target="tpu_custom_call" | custom-call | tf_op jit(solution)/shard_map/pallas_call | solution.py:139
  50.8 2.6 %collective-permute-done.10 = f32[128,2432]{1,0:T(8,128)S(1)} collective-permute-done((f32[128,2432]{1,0:T(8,128)}, f32[128,2432]{1,0:T(8,128)S(1)}, u32[]{:S(2)}, u32[]{:S(2)}) %collective-permute-start.10) | collective-permute-done | bytes 1245216 | tf_op jit(solution)/shard_map/ppermute | solution.py:31
  53.3 2.4 %fusion.50 = (f16[128,2432]{1,0:T(8,128)(2,1)}, f32[128,2432]{1,0:T(8,128)S(1)}) fusion(f32[128,2432]{1,0:T(8,128)} %get-tuple-element.68, f32[128,2432]{1,0:T(8,128)S(1)} %collective-permute-done.10), kind=kLoop, calls=%fused_computation.257 | loop fusion | flops 622592 | bytes 4358144 | tf_op jit(solution)/shard_map/convert_element_type | solution.py:350
  55.7 10.9 %collective-permute-done.11 = f16[128,2432]{1,0:T(8,128)(2,1)S(1)} collective-permute-done((f16[128,2432]{1,0:T(8,128)(2,1)S(1)}, f16[128,2432]{1,0:T(8,128)(2,1)S(1)}, u32[]{:S(2)}, u32[]{:S(2)}) %collective-permute-start.11) | collective-permute-done | bytes 622624 | tf_op jit(solution)/shard_map/ppermute | solution.py:31
  74.9 12.1 %shard_map.81 = f32[512,2048]{1,0:T(8,128)} custom-call(bf16[512,2432]{1,0:T(8,128)(2,1)} %bitcast.86, bf16[2048,2432]{1,0:T(8,128)(2,1)} %head.9), custom_call_target="tpu_custom_call" | custom-call | tf_op jit(solution)/shard_map/pallas_call | solution.py:249
  90.6 4.4 %fusion.53 = (f32[256,1024]{1,0:T(8,128)}, f32[256,1024]{1,0:T(8,128)}, f32[256,1024]{1,0:T(8,128)}, f32[256,1024]{1,0:T(8,128)}) fusion(f32[512,2048]{1,0:T(8,128)} %shard_map.81), kind=kLoop, calls=%fused_computation.260 | loop fusion | bytes 8388608 | tf_op jit(solution)/shard_map/slice | solution.py:390
  100.4 12.0 %shard_map.83 = f32[512,2048]{1,0:T(8,128)} custom-call(bf16[512,2432]{1,0:T(8,128)(2,1)} %bitcast.85, bf16[2048,2432]{1,0:T(8,128)(2,1)} %head.9), custom_call_target="tpu_custom_call" | custom-call | tf_op jit(solution)/shard_map/pallas_call | solution.py:249
  114.4 2.5 %fusion.52 = (f32[256,1024]{1,0:T(8,128)S(1)}, f32[256,1024]{1,0:T(8,128)S(1)}, f32[256,1024]{1,0:T(8,128)S(1)}, f32[256,1024]{1,0:T(8,128)S(1)}) fusion(f32[512,2048]{1,0:T(8,128)} %shard_map.83), kind=kLoop, calls=%fused_computation.259 | loop fusion | bytes 8388608 | tf_op jit(solution)/shard_map/slice | solution.py:390
  121.7 2.7 %collective-permute-start.17 = (f32[4,512]{1,0:T(4,128)S(1)}, f32[4,512]{1,0:T(4,128)S(1)}, u32[]{:S(2)}, u32[]{:S(2)}) collective-permute-start(f32[4,512]{1,0:T(4,128)S(1)} %pad_maximum_fusion.12), channel_id=1, source_target_pairs={{0,4},{1,5},{2,6},{3,7},{4,0},{5,1},{6,2},{7,3},{8,12},{9,13},{10,... | collective-permute-start | bytes 24584 | tf_op jit(solution)/shard_map/ppermute | solution.py:31
  127.3 4.0 %multiply_add_fusion = (f32[2,2,2,64,1024]{4,3,2,1,0:T(8,128)S(1)}, f32[2,2,2,64,1024]{4,3,2,1,0:T(8,128)S(1)}) fusion(f32[2,2,2,64,1024]{4,3,2,1,0:T(8,128)} %bitcast.90, f32[2,2,2,64,1024]{4,3,2,1,0:T(8,128)} %bitcast.96, f32[2,2,2,64]{3,2,1,0:T(2,128)S(1)} %get-tuple-element.112, f32[2,2,2,64]{3,2,1,0:T(2,128)S(1)} %get-tuple-element.113, ...), kind=kLoop, calls=%fused_computation.7 | loop fusion | flops 3145728 | bytes 12587008 | tf_op jit(solution)/shard_map/add | solution.py:391
  144.2 12.0 %shard_map.85 = f32[512,2048]{1,0:T(8,128)} custom-call(bf16[512,2432]{1,0:T(8,128)(2,1)} %copy-done.2, bf16[2048,2432]{1,0:T(8,128)(2,1)} %head.9), custom_call_target="tpu_custom_call" | custom-call | tf_op jit(solution)/shard_map/pallas_call | solution.py:249
  156.2 2.7 %slice_multiply_fusion = (f32[512,1024]{1,0:T(8,128)S(1)}, f32[512,1024]{1,0:T(8,128)S(1)}) fusion(f32[512,2048]{1,0:T(8,128)} %shard_map.85, f32[512]{0:T(512)S(1)} %slice_reduce_fusion), kind=kLoop, calls=%fused_computation | loop fusion | flops 1048576 | bytes 8390656 | tf_op jit(solution)/shard_map/mul | solution.py:436
  167.1 9.8 %collective-permute-done.26 = bf16[1,2,1,64,1024]{4,3,2,1,0:T(8,128)(2,1)S(1)} collective-permute-done((bf16[1,2,1,64,1024]{4,3,2,1,0:T(8,128)(2,1)S(1)}, bf16[1,2,1,64,1024]{4,3,2,1,0:T(8,128)(2,1)S(1)}, u32[]{:S(2)}, u32[]{:S(2)}) %collective-permute-start.26) | collective-permute-done | bytes 262176 | tf_op jit(solution)/shard_map/ppermute | solution.py:31
  183.6 10.2 %collective-permute-done.29 = bf16[1,1,1,64,1024]{4,3,2,1,0:T(8,128)(2,1)S(1)} collective-permute-done((bf16[1,1,1,64,1024]{4,3,2,1,0:T(8,128)(2,1)S(1)}, bf16[1,1,1,64,1024]{4,3,2,1,0:T(8,128)(2,1)S(1)}, u32[]{:S(2)}, u32[]{:S(2)}) %collective-permute-start.29) | collective-permute-done | bytes 131104 | tf_op jit(solution)/shard_map/ppermute | solution.py:31
  194.9 2.8 %collective-permute-start.32 = (bf16[1,1,1,64,1024]{4,3,2,1,0:T(8,128)(2,1)S(1)}, bf16[1,1,1,64,1024]{4,3,2,1,0:T(8,128)(2,1)S(1)}, u32[]{:S(2)}, u32[]{:S(2)}) collective-permute-start(bf16[1,1,1,64,1024]{4,3,2,1,0:T(8,128)(2,1)S(1)} %dynamic-slice_convert_fusion.6), channel_id=1, source_target_pairs={{0,4},{1,5},{2,6},{3,7},{4,0},{5,1},{6,2},{7,3},{8,12},{9,13},{10,... | collective-permute-start | bytes 393224 | tf_op jit(solution)/shard_map/ppermute | solution.py:31
  197.8 3.9 %collective-permute-done.32 = bf16[1,1,1,64,1024]{4,3,2,1,0:T(8,128)(2,1)S(1)} collective-permute-done((bf16[1,1,1,64,1024]{4,3,2,1,0:T(8,128)(2,1)S(1)}, bf16[1,1,1,64,1024]{4,3,2,1,0:T(8,128)(2,1)S(1)}, u32[]{:S(2)}, u32[]{:S(2)}) %collective-permute-start.32) | collective-permute-done | bytes 131104 | tf_op jit(solution)/shard_map/ppermute | solution.py:31
  202.8 2.8 %collective-permute-start.34 = (bf16[1,1,1,64,1024]{4,3,2,1,0:T(8,128)(2,1)S(1)}, bf16[1,1,1,64,1024]{4,3,2,1,0:T(8,128)(2,1)S(1)}, u32[]{:S(2)}, u32[]{:S(2)}) collective-permute-start(bf16[1,1,1,64,1024]{4,3,2,1,0:T(8,128)(2,1)S(1)} %dynamic-slice_convert_fusion.5), channel_id=1, source_target_pairs={{0,4},{1,5},{2,6},{3,7},{4,0},{5,1},{6,2},{7,3},{8,12},{9,13},{10,... | collective-permute-start | bytes 393224 | tf_op jit(solution)/shard_map/ppermute | solution.py:31
  205.7 4.5 %collective-permute-done.34 = bf16[1,1,1,64,1024]{4,3,2,1,0:T(8,128)(2,1)S(1)} collective-permute-done((bf16[1,1,1,64,1024]{4,3,2,1,0:T(8,128)(2,1)S(1)}, bf16[1,1,1,64,1024]{4,3,2,1,0:T(8,128)(2,1)S(1)}, u32[]{:S(2)}, u32[]{:S(2)}) %collective-permute-start.34) | collective-permute-done | bytes 131104 | tf_op jit(solution)/shard_map/ppermute | solution.py:31
  211.8 3.5 %collective-permute-done.36 = f32[2,64]{1,0:T(2,128)S(1)} collective-permute-done((f32[2,64]{1,0:T(2,128)S(1)}, f32[2,64]{1,0:T(2,128)S(1)}, u32[]{:S(2)}, u32[]{:S(2)}) %collective-permute-start.36) | collective-permute-done | bytes 544 | tf_op jit(solution)/shard_map/ppermute | solution.py:31
  (237 shorter events, 75.1 us)
Async XLA Ops:
  4.9 10.1 %collective-permute-start.3 = (bf16[64,2048]{1,0:T(8,128)(2,1)S(1)}, bf16[64,2048]{1,0:T(8,128)(2,1)S(1)}, u32[]{:S(2)}, u32[]{:S(2)}) collective-permute-start(bf16[64,2048]{1,0:T(8,128)(2,1)S(1)} %get-tuple-element.59), channel_id=1, source_target_pairs={{0,16},{8,24},{16,0},{24,8},{1,17},{9,25},{17,1},{25,9},{2,18},{10... | collective-permute-start | bytes 786440 | tf_op jit(solution)/shard_map/ppermute | solution.py:31
  7.9 18.7 %collective-permute-start.4 = (bf16[64,2048]{1,0:T(8,128)(2,1)S(1)}, bf16[64,2048]{1,0:T(8,128)(2,1)S(1)}, u32[]{:S(2)}, u32[]{:S(2)}) collective-permute-start(bf16[64,2048]{1,0:T(8,128)(2,1)S(1)} %get-tuple-element.60), channel_id=1, source_target_pairs={{0,24},{8,16},{16,8},{24,0},{1,25},{9,17},{17,9},{25,1},{2,26},{10... | collective-permute-start | bytes 786440 | tf_op jit(solution)/shard_map/ppermute | solution.py:31
  8.1 6.9 %collective-permute-start = (bf16[128,2048]{1,0:T(8,128)(2,1)S(1)}, bf16[128,2048]{1,0:T(8,128)(2,1)S(1)}, u32[]{:S(2)}, u32[]{:S(2)}) collective-permute-start(bf16[128,2048]{1,0:T(8,128)(2,1)S(1)} %get-tuple-element.54), channel_id=1, source_target_pairs={{0,8},{8,0},{16,24},{24,16},{1,9},{9,1},{17,25},{25,17},{2,10},{10... | collective-permute-start | bytes 1572872 | tf_op jit(solution)/shard_map/ppermute | solution.py:31
  9.1 26.2 %collective-permute-start.7 = (f32[2,8,128]{2,1,0:T(8,128)S(1)}, f32[2,8,128]{2,1,0:T(8,128)S(1)}, u32[]{:S(2)}, u32[]{:S(2)}) collective-permute-start(f32[2,8,128]{2,1,0:T(8,128)S(1)} %pad_maximum_fusion.9), channel_id=1, source_target_pairs={{0,16},{8,24},{16,0},{24,8},{1,17},{9,25},{17,1},{25,9},{2,18},{10... | collective-permute-start | bytes 24584 | tf_op jit(solution)/shard_map/ppermute | solution.py:31
  29.4 8.2 %collective-permute-start.6 = (bf16[2,32,2048]{2,1,0:T(8,128)(2,1)S(1)}, bf16[2,32,2048]{2,1,0:T(8,128)(2,1)S(1)}, u32[]{:S(2)}, u32[]{:S(2)}) collective-permute-start(bf16[2,32,2048]{2,1,0:T(8,128)(2,1)S(1)} %pad_maximum_fusion.6), channel_id=1, source_target_pairs={{0,1},{1,0},{2,3},{3,2},{4,5},{5,4},{6,7},{7,6},{8,9},{9,8},{10,11... | collective-permute-start | bytes 786440 | tf_op jit(solution)/shard_map/ppermute | solution.py:31
  31.0 7.8 %collective-permute-start.5 = (bf16[2,32,2048]{2,1,0:T(8,128)(2,1)S(1)}, bf16[2,32,2048]{2,1,0:T(8,128)(2,1)S(1)}, u32[]{:S(2)}, u32[]{:S(2)}) collective-permute-start(bf16[2,32,2048]{2,1,0:T(8,128)(2,1)S(1)} %pad_maximum_fusion.6), channel_id=1, source_target_pairs={{0,2},{1,3},{2,0},{3,1},{4,6},{5,7},{6,4},{7,5},{8,10},{9,11},{10,... | collective-permute-start | bytes 786440 | tf_op jit(solution)/shard_map/ppermute | solution.py:31
  50.2 16.4 %collective-permute-start.11 = (f16[128,2432]{1,0:T(8,128)(2,1)S(1)}, f16[128,2432]{1,0:T(8,128)(2,1)S(1)}, u32[]{:S(2)}, u32[]{:S(2)}) collective-permute-start(f16[128,2432]{1,0:T(8,128)(2,1)S(1)} %get-tuple-element.62), channel_id=1, source_target_pairs={{0,16},{8,24},{16,0},{24,8},{1,17},{9,25},{17,1},{25,9},{2,18},{10... | collective-permute-start | bytes 1867784 | tf_op jit(solution)/shard_map/ppermute | solution.py:31
  66.9 20.1 %collective-permute-start.12 = (f16[128,2432]{1,0:T(8,128)(2,1)}, f16[128,2432]{1,0:T(8,128)(2,1)}, u32[]{:S(2)}, u32[]{:S(2)}) collective-permute-start(f16[128,2432]{1,0:T(8,128)(2,1)} %get-tuple-element.70), channel_id=1, source_target_pairs={{0,16},{8,24},{16,0},{24,8},{1,17},{9,25},{17,1},{25,9},{2,18},{10... | collective-permute-start | bytes 1867784 | tf_op jit(solution)/shard_map/ppermute | solution.py:31
  89.8 43.9 %collective-permute-start.19 = (bf16[128,2432]{1,0:T(8,128)(2,1)S(1)}, bf16[128,2432]{1,0:T(8,128)(2,1)S(1)}, u32[]{:S(2)}, u32[]{:S(2)}) collective-permute-start(bf16[128,2432]{1,0:T(8,128)(2,1)S(1)} %copy-done), channel_id=1, source_target_pairs={{0,16},{8,24},{16,0},{24,8},{1,17},{9,25},{17,1},{25,9},{2,18},{10... | collective-permute-start | bytes 1867784 | tf_op jit(solution)/shard_map/ppermute | solution.py:31
  90.3 50.8 %collective-permute-start.18 = (bf16[128,2432]{1,0:T(8,128)(2,1)S(1)}, bf16[128,2432]{1,0:T(8,128)(2,1)S(1)}, u32[]{:S(2)}, u32[]{:S(2)}) collective-permute-start(bf16[128,2432]{1,0:T(8,128)(2,1)S(1)} %copy-done), channel_id=1, source_target_pairs={{0,8},{8,0},{16,24},{24,16},{1,9},{9,1},{17,25},{25,17},{2,10},{10... | collective-permute-start | bytes 1867784 | tf_op jit(solution)/shard_map/ppermute | solution.py:31
  98.6 13.8 %collective-permute-start.15 = (f32[4,512]{1,0:T(4,128)S(1)}, f32[4,512]{1,0:T(4,128)S(1)}, u32[]{:S(2)}, u32[]{:S(2)}) collective-permute-start(f32[4,512]{1,0:T(4,128)S(1)} %pad_maximum_fusion.10), channel_id=1, source_target_pairs={{0,1},{1,0},{2,3},{3,2},{4,5},{5,4},{6,7},{7,6},{8,9},{9,8},{10,11... | collective-permute-start | bytes 24584 | tf_op jit(solution)/shard_map/ppermute | solution.py:31
  112.6 9.0 %collective-permute-start.16 = (f32[4,512]{1,0:T(4,128)S(1)}, f32[4,512]{1,0:T(4,128)S(1)}, u32[]{:S(2)}, u32[]{:S(2)}) collective-permute-start(f32[4,512]{1,0:T(4,128)S(1)} %pad_maximum_fusion.11), channel_id=1, source_target_pairs={{0,2},{1,3},{2,0},{3,1},{4,6},{5,7},{6,4},{7,5},{8,10},{9,11},{10,... | collective-permute-start | bytes 24584 | tf_op jit(solution)/shard_map/ppermute | solution.py:31
  133.7 7.5 %collective-permute-start.20 = (bf16[128,2432]{1,0:T(8,128)(2,1)S(1)}, bf16[128,2432]{1,0:T(8,128)(2,1)S(1)}, u32[]{:S(2)}, u32[]{:S(2)}) collective-permute-start(bf16[128,2432]{1,0:T(8,128)(2,1)S(1)} %collective-permute-done.19.refs_2_), channel_id=1, source_target_pairs={{0,8},{8,0},{16,24},{24,16},{1,9},{9,1},{17,25},{25,17},{2,10},{10... | collective-permute-start | bytes 1867784 | tf_op jit(solution)/shard_map/ppermute | solution.py:31
  138.5 21.9 %collective-permute-start.23 = (bf16[2,1,2,64,1024]{4,3,2,1,0:T(8,128)(2,1)}, bf16[2,1,2,64,1024]{4,3,2,1,0:T(8,128)(2,1)S(1)}, u32[]{:S(2)}, u32[]{:S(2)}) collective-permute-start(bf16[2,1,2,64,1024]{4,3,2,1,0:T(8,128)(2,1)} %slice.366), channel_id=1, source_target_pairs={{0,1},{1,0},{2,3},{3,2},{4,5},{5,4},{6,7},{7,6},{8,9},{9,8},{10,11... | collective-permute-start | bytes 1572872 | tf_op jit(solution)/shard_map/ppermute | solution.py:31
  140.0 20.3 %collective-permute-start.24 = (bf16[2,2,1,64,1024]{4,3,2,1,0:T(8,128)(2,1)}, bf16[2,2,1,64,1024]{4,3,2,1,0:T(8,128)(2,1)S(1)}, u32[]{:S(2)}, u32[]{:S(2)}) collective-permute-start(bf16[2,2,1,64,1024]{4,3,2,1,0:T(8,128)(2,1)} %dynamic-slice_convert_fusion), channel_id=1, source_target_pairs={{0,2},{1,3},{2,0},{3,1},{4,6},{5,7},{6,4},{7,5},{8,10},{9,11},{10,... | collective-permute-start | bytes 1572872 | tf_op jit(solution)/shard_map/ppermute | solution.py:31
  162.6 14.2 %collective-permute-start.26 = (bf16[1,2,1,64,1024]{4,3,2,1,0:T(8,128)(2,1)S(1)}, bf16[1,2,1,64,1024]{4,3,2,1,0:T(8,128)(2,1)S(1)}, u32[]{:S(2)}, u32[]{:S(2)}) collective-permute-start(bf16[1,2,1,64,1024]{4,3,2,1,0:T(8,128)(2,1)S(1)} %dynamic-slice_convert_fusion.3), channel_id=1, source_target_pairs={{0,4},{1,5},{2,6},{3,7},{4,0},{5,1},{6,2},{7,3},{8,12},{9,13},{10,... | collective-permute-start | bytes 786440 | tf_op jit(solution)/shard_map/ppermute | solution.py:31
  164.6 12.8 %collective-permute-start.27 = (bf16[2,1,2,64,1024]{4,3,2,1,0:T(8,128)(2,1)S(1)}, bf16[2,1,2,64,1024]{4,3,2,1,0:T(8,128)(2,1)S(1)}, u32[]{:S(2)}, u32[]{:S(2)}) collective-permute-start(bf16[2,1,2,64,1024]{4,3,2,1,0:T(8,128)(2,1)S(1)} %slice.365), channel_id=1, source_target_pairs={{0,1},{1,0},{2,3},{3,2},{4,5},{5,4},{6,7},{7,6},{8,9},{9,8},{10,11... | collective-permute-start | bytes 1572872 | tf_op jit(solution)/shard_map/ppermute | solution.py:31
  166.0 11.2 %collective-permute-start.25 = (bf16[2,1,1,64,1024]{4,3,2,1,0:T(8,128)(2,1)S(1)}, bf16[2,1,1,64,1024]{4,3,2,1,0:T(8,128)(2,1)S(1)}, u32[]{:S(2)}, u32[]{:S(2)}) collective-permute-start(bf16[2,1,1,64,1024]{4,3,2,1,0:T(8,128)(2,1)S(1)} %dynamic-slice_convert_fusion.4), channel_id=1, source_target_pairs={{0,2},{1,3},{2,0},{3,1},{4,6},{5,7},{6,4},{7,5},{8,10},{9,11},{10,... | collective-permute-start | bytes 786440 | tf_op jit(solution)/shard_map/ppermute | solution.py:31
  177.7 16.1 %collective-permute-start.30 = (bf16[2,1,1,64,1024]{4,3,2,1,0:T(8,128)(2,1)S(1)}, bf16[2,1,1,64,1024]{4,3,2,1,0:T(8,128)(2,1)S(1)}, u32[]{:S(2)}, u32[]{:S(2)}) collective-permute-start(bf16[2,1,1,64,1024]{4,3,2,1,0:T(8,128)(2,1)S(1)} %dynamic-slice_convert_fusion.2), channel_id=1, source_target_pairs={{0,2},{1,3},{2,0},{3,1},{4,6},{5,7},{6,4},{7,5},{8,10},{9,11},{10,... | collective-permute-start | bytes 786440 | tf_op jit(solution)/shard_map/ppermute | solution.py:31
  179.4 14.5 %collective-permute-start.31 = (bf16[2,1,2,64,1024]{4,3,2,1,0:T(8,128)(2,1)S(1)}, bf16[2,1,2,64,1024]{4,3,2,1,0:T(8,128)(2,1)S(1)}, u32[]{:S(2)}, u32[]{:S(2)}) collective-permute-start(bf16[2,1,2,64,1024]{4,3,2,1,0:T(8,128)(2,1)S(1)} %slice.364), channel_id=1, source_target_pairs={{0,1},{1,0},{2,3},{3,2},{4,5},{5,4},{6,7},{7,6},{8,9},{9,8},{10,11... | collective-permute-start | bytes 1572872 | tf_op jit(solution)/shard_map/ppermute | solution.py:31
  180.0 13.8 %collective-permute-start.29 = (bf16[1,1,1,64,1024]{4,3,2,1,0:T(8,128)(2,1)S(1)}, bf16[1,1,1,64,1024]{4,3,2,1,0:T(8,128)(2,1)S(1)}, u32[]{:S(2)}, u32[]{:S(2)}) collective-permute-start(bf16[1,1,1,64,1024]{4,3,2,1,0:T(8,128)(2,1)S(1)} %slice.367), channel_id=1, source_target_pairs={{0,1},{1,0},{2,3},{3,2},{4,5},{5,4},{6,7},{7,6},{8,9},{9,8},{10,11... | collective-permute-start | bytes 393224 | tf_op jit(solution)/shard_map/ppermute | solution.py:31
  181.6 12.2 %collective-permute-start.28 = (bf16[1,1,1,64,1024]{4,3,2,1,0:T(8,128)(2,1)S(1)}, bf16[1,1,1,64,1024]{4,3,2,1,0:T(8,128)(2,1)S(1)}, u32[]{:S(2)}, u32[]{:S(2)}) collective-permute-start(bf16[1,1,1,64,1024]{4,3,2,1,0:T(8,128)(2,1)S(1)} %dynamic-slice_convert_fusion.7), channel_id=1, source_target_pairs={{0,4},{1,5},{2,6},{3,7},{4,0},{5,1},{6,2},{7,3},{8,12},{9,13},{10,... | collective-permute-start | bytes 393224 | tf_op jit(solution)/shard_map/ppermute | solution.py:31
  194.2 8.6 %collective-permute-start.33 = (bf16[2,1,1,64,1024]{4,3,2,1,0:T(8,128)(2,1)S(1)}, bf16[2,1,1,64,1024]{4,3,2,1,0:T(8,128)(2,1)S(1)}, u32[]{:S(2)}, u32[]{:S(2)}) collective-permute-start(bf16[2,1,1,64,1024]{4,3,2,1,0:T(8,128)(2,1)S(1)} %dynamic-slice_convert_fusion.1), channel_id=1, source_target_pairs={{0,2},{1,3},{2,0},{3,1},{4,6},{5,7},{6,4},{7,5},{8,10},{9,11},{10,... | collective-permute-start | bytes 786440 | tf_op jit(solution)/shard_map/ppermute | solution.py:31
  202.8 7.3 %collective-permute-start.34 = (bf16[1,1,1,64,1024]{4,3,2,1,0:T(8,128)(2,1)S(1)}, bf16[1,1,1,64,1024]{4,3,2,1,0:T(8,128)(2,1)S(1)}, u32[]{:S(2)}, u32[]{:S(2)}) collective-permute-start(bf16[1,1,1,64,1024]{4,3,2,1,0:T(8,128)(2,1)S(1)} %dynamic-slice_convert_fusion.5), channel_id=1, source_target_pairs={{0,4},{1,5},{2,6},{3,7},{4,0},{5,1},{6,2},{7,3},{8,12},{9,13},{10,... | collective-permute-start | bytes 393224 | tf_op jit(solution)/shard_map/ppermute | solution.py:31
  (48 other events, 260.8 us)

commit v3 on v1

--- a/solution.py
+++ b/solution.py
@@ -183,14 +183,25 @@
     )(at, *blocks, *totals)
 
 
-def back_kernel(deep, cotangent, head, out):
-    width = head.shape[1]
-    result = lax.dot_general(
-        cotangent[:, :deep], head[:, :deep], NT, preferred_element_type=F32
-    )
+STREAMS = 4
+
+
+def back_kernel(deep, *refs):
+    cotangents, heads = refs[:STREAMS], refs[STREAMS : 2 * STREAMS]
+    out, left = refs[2 * STREAMS :]
+    rows, part = cotangents[0].shape[0], heads[0].shape[0]
+    width = left.shape[1]
+
+    @pl.when(pl.program_id(0) == 0)
+    def _():
+        for index, source in enumerate(cotangents):
+            left[index * rows : (index + 1) * rows, :] = source[...]
+
+    head = jnp.concatenate([value[...] for value in heads], axis=0)
+    result = lax.dot_general(left[:, :deep], head[:, :deep], NT, preferred_element_type=F32)
     if deep < width:
         result += lax.dot_general(
-            cotangent[:, deep:], head[:, deep:], NT, preferred_element_type=F32
+            left[:, deep:], head[:, deep:], NT, preferred_element_type=F32
         )
     out[...] = result
 
@@ -200,18 +211,24 @@
     features = head.shape[0]
     tile = 256 if features % 256 == 0 else features
     deep = width // 256 * 256 or width
+
+    def row_block(index):
+        return pl.BlockSpec((rows // STREAMS, width), lambda i: (index, 0))
+
+    def head_block(index):
+        return pl.BlockSpec((tile // STREAMS, width), lambda i: (STREAMS * i + index, 0))
+
     return pl.pallas_call(
         functools.partial(back_kernel, deep),
         grid=(features // tile,),
-        in_specs=[
-            pl.BlockSpec((rows, width), lambda i: (0, 0)),
-            pl.BlockSpec((tile, width), lambda i: (i, 0)),
-        ],
+        in_specs=[row_block(index) for index in range(STREAMS)]
+        + [head_block(index) for index in range(STREAMS)],
         out_specs=pl.BlockSpec((rows, tile), lambda i: (0, i)),
         out_shape=jax.ShapeDtypeStruct((rows, features), F32),
-        compiler_params=params(20),
+        scratch_shapes=[pltpu.VMEM((rows, width), BF16)],
+        compiler_params=params(52),
         cost_estimate=LIGHT,
-    )(cotangent, head)
+    )(*([cotangent] * STREAMS), *([head] * STREAMS))
 
 
 def merge(first, second):
@@ -223,16 +240,16 @@
     return jnp.stack([peak, total, mean] + [first[i] + second[i] for i in range(3, len(first))])
 
 
-def exchange(value, size):
+def exchange(value, size, beside):
     half = value.shape[1] // 2
-    other = swap(value, "vocab", 1, size)
+    other, beside = lax.optimization_barrier((swap(value, "vocab", 1, size), beside))
     aligned = jnp.concatenate([other[:3, half:], other[:3, :half]], axis=1)
     value = merge(value, jnp.concatenate([aligned, other[3:]], axis=0))
     bit = PAIR
     while bit < size:
         value = merge(value, swap(value, "vocab", bit, size))
         bit *= 2
-    return value
+    return value, beside
 
 
 def body(hidden, steer, tangent, gain, head, target):
@@ -287,10 +304,12 @@
         normed = (gain_part * values / radius[:, None]).astype(BF16)
         return jnp.dot(normed, head, preferred_element_type=F32)
 
+    given = partial_logits(mate, sums_1)
+    two, given = lax.optimization_barrier((two, given))
+    given = swap(given, "seq", 1, seq_size)
     row = jnp.sum(jnp.dot(two, head, preferred_element_type=F32), axis=0, keepdims=True)
     row = row + swap(row, "seq", 1, seq_size)
     tangent_row = row + swap(row, "seq", 2, seq_size)
-    given = swap(partial_logits(mate, sums_1), "seq", 1, seq_size)
     summed_0 = partial_logits(own, sums_0) + given
     send_0, tangent_row = lax.optimization_barrier((summed_0.astype(jnp.float16), tangent_row))
     got_2 = swap(send_0, "seq", 2, seq_size)
@@ -311,33 +330,48 @@
 
     half = rows // 2
 
-    def half_of(base, summed, got, where, extra):
+    def soften_of(base, summed, got, where):
         full = summed + got.astype(F32)
         mates = swap(full, "seq", 1, seq_size)
         both, stats = soften(
             where, full, mates, tangent_row, sums[base], sums[base + 1], feature_count
         )
-        stats = stats[:3]
-        joint = exchange(jnp.concatenate([stats] + extra), vocab_size)
-        raw = back(both.reshape(2 * half, -1), head)
+        return both.reshape(2 * half, -1), stats[:3]
+
+    def scaled_of(raw, stats, joint):
         scale = jnp.exp(stats[0] - joint[0]) / joint[1]
         lean = scale * (stats[2] - joint[2])
         plain = scale[:, None] * raw[:half]
         ggn = scale[:, None] * raw[half:] + lean[:, None] * raw[:half]
-        return plain, ggn[half // 2 :].astype(BF16), ggn[: half // 2], joint
-
-    plain_other, theirs_other, kept_other, _ = half_of(2, summed_2, got_2, other_places, [])
-    got_0, target, theirs_other = lax.optimization_barrier((got_0, target, theirs_other))
+        return plain, ggn[half // 2 :].astype(BF16), ggn[: half // 2]
+
+    both_other, stats_other = soften_of(2, summed_2, got_2, other_places)
+    raw_other = back(both_other, head)
+    got_0, target, raw_other, stats_other = lax.optimization_barrier(
+        (got_0, target, raw_other, stats_other)
+    )
+    target_2 = swap(target, "seq", 2, seq_size)
+    joint_other, raw_other = exchange(stats_other, vocab_size, raw_other)
+    plain_other, theirs_other, kept_other = scaled_of(raw_other, stats_other, joint_other)
     got_other = swap(theirs_other, "vocab", 1, vocab_size)
+
+    both_own, stats_own = soften_of(0, summed_0, got_0, own_places)
+    stats_own, theirs_other = lax.optimization_barrier((stats_own, theirs_other))
     own_total = jnp.sum(target.astype(F32), axis=1)
-    plain_own, theirs_own, kept_own, joint = half_of(
-        0, summed_0, got_0, own_places, [jnp.concatenate([own_total, own_total])[None]]
-    )
-
-    target_2 = swap(target, "seq", 2, seq_size)
-    target_1 = swap(target, "seq", 1, seq_size)
+    joint, raw_own = exchange(
+        jnp.concatenate([stats_own, jnp.concatenate([own_total, own_total])[None]]),
+        vocab_size,
+        back(both_own, head),
+    )
+    plain_own, theirs_own, kept_own = scaled_of(raw_own, stats_own, joint)
+    got_own = swap(theirs_own, "vocab", 1, vocab_size)
+
+    target_2, late_target, joint_total, _ = lax.optimization_barrier(
+        (target_2, target, joint[3, :tokens], theirs_own)
+    )
+    target_1 = swap(late_target, "seq", 1, seq_size)
     target_3 = swap(target_2, "seq", 1, seq_size)
-    total_0 = jnp.broadcast_to(joint[3, :tokens], (8, tokens))
+    total_0 = jnp.broadcast_to(joint_total, (8, tokens))
     total_1 = swap(total_0, "seq", 1, seq_size)
     both = swap(jnp.stack([total_0, total_1]), "seq", 2, seq_size)
     ordered, columns = order(
@@ -345,7 +379,6 @@
         [target, target_1, target_2, target_3],
         [total_0, total_1, both[0], both[1]],
     )
-    ordered, theirs_own = lax.optimization_barrier((ordered, theirs_own))
     weighed = back(ordered, head)
     inverse = columns[:, 0:1]
     gradients = [
@@ -364,7 +397,6 @@
         kept = lax.dynamic_index_in_dim(joined, place, axis, False)
         return sent.astype(BF16), kept
 
-    got_own = swap(theirs_own, "vocab", 1, vocab_size)
     chunks = []
     for begin in (0, width // 2):
         part = [g[:, begin : begin + width // 2] for g in gradients]

time: 191 us -> 207 us (1.084)
  Pallas kernels: 28.5 us -> 44.3 us
  other arithmetic: 7.49 us -> 16.5 us
  waiting for transfers between devices: 88.5 us -> 80.8 us
  local copies, waits for them, and re-layouts: 16.7 us -> 10.6 us
  starting transfers between devices: 34.2 us -> 38.6 us
    pallas_call x3, Pallas kernels: 21.7 us -> 37.4 us  [back(): pl.pallas_call(functools.partial(back_kernel, deep), grid=(features // ti...]
    ppermute x38, waiting for transfers between devices: 88.5 us -> 80.8 us  [swap(): return lax.ppermute(value, axis, [(i, i ^ bit) for i in range(size)])]
    unnamed x70 -> x86, local copies, waits for them, and re-layouts: 15 us -> 7.29 us
    add x4, other arithmetic: 0.84 us -> 5.34 us  [the longest x2 5.04 us: scaled_of(): ggn = scale[:, None] * raw[half:] + lean[:, None] * raw[:half]]
    ppermute x38, starting transfers between devices: 34.2 us -> 38.6 us  [swap(): return lax.ppermute(value, axis, [(i, i ^ bit) for i in range(size)])]
    dot_general x4, matrix products: 8.34 us -> 12.4 us  [partial_logits(): return jnp.dot(normed, head, preferred_element_type=F32)]
    dot_general x1, matrix products: 5.4 us -> 1.42 us  [body(): jnp.dot(two, head, preferred_element_type=F32)]
    another operation x1, other arithmetic: 0.65 us -> 2.86 us
  transfers between devices with their start and end apart: 38 -> 38, of which waited for: 24 -> 25; matrix products, arithmetic and copies ran while one was open for 9% -> 13% of each run, Pallas kernels for 12% -> 20%
where the time goes in v3:
time: 207 us; the launch traced here: 206 us
  waiting for transfers between devices  80.8 us (39%)
  Pallas kernels  44.3 us (21%)
  starting transfers between devices  38.6 us (19%)
  other arithmetic  16.5 us (8%)
  matrix products  13.8 us (7%)
  local copies, waits for them, and re-layouts  10.6 us (5%)
    ppermute x38, waiting for transfers between devices, swap(): return lax.ppermute(value, axis, [(i, i ^ bit) for i in range(size)])  80.8 us
    ppermute x38, starting transfers between devices, swap(): return lax.ppermute(value, axis, [(i, i ^ bit) for i in range(size)])  38.6 us
    pallas_call x3, Pallas kernels, back(): pl.pallas_call(functools.partial(back_kernel, deep), grid=(features // ti...  37.4 us
    dot_general x4, matrix products, partial_logits(): return jnp.dot(normed, head, preferred_element_type=F32)  12.4 us
    unnamed x86, local copies, waits for them, and re-layouts  7.29 us
    add x2, other arithmetic, scaled_of(): ggn = scale[:, None] * raw[half:] + lean[:, None] * raw[:half]  5.04 us
    pallas_call x2, Pallas kernels, soften(): pl.pallas_call(functools.partial(soften_kernel, feature_count), in_specs=...  4.46 us
  transfers between devices with their start and end apart: 38, of which 25 were waited for; matrix products, arithmetic and copies ran while one was open for 13% of the time, Pallas kernels for 20%

profile of v3, /device:TPU:0, one launch (start us, length us, event | category | flops | bytes accessed | tf_op | source)
XLA Modules:
  0.0 206.3 jit_solution(1932574352911485781)
XLA Ops:
  5.4 2.6 %collective-permute-start.3 = (bf16[64,2048]{1,0:T(8,128)(2,1)S(1)}, bf16[64,2048]{1,0:T(8,128)(2,1)S(1)}, u32[]{:S(2)}, u32[]{:S(2)}) collective-permute-start(bf16[64,2048]{1,0:T(8,128)(2,1)S(1)} %get-tuple-element.56), channel_id=1, source_target_pairs={{0,16},{8,24},{16,0},{24,8},{1,17},{9,25},{17,1},{25,9},{2,18},{10... | collective-permute-start | bytes 786440 | tf_op jit(solution)/shard_map/ppermute | solution.py:31
  11.2 3.9 %collective-permute-done.3 = bf16[64,2048]{1,0:T(8,128)(2,1)S(1)} collective-permute-done((bf16[64,2048]{1,0:T(8,128)(2,1)S(1)}, bf16[64,2048]{1,0:T(8,128)(2,1)S(1)}, u32[]{:S(2)}, u32[]{:S(2)}) %collective-permute-start.3) | collective-permute-done | bytes 262176 | tf_op jit(solution)/shard_map/ppermute | solution.py:31
  15.2 5.6 %fusion.2 = f32[128,2432]{1,0:T(8,128)S(1)} fusion(bf16[2048,2432]{1,0:T(8,128)(2,1)} %refs_7_.5, bf16[128,2048]{1,0:T(8,128)(2,1)S(1)} %collective-permute-done, f32[128]{0:T(128)S(1)} %get-tuple-element.167, f32[2048]{0:T(1024)S(1)} %bitcast.166, f32[2048]{0:T(1024)S(1)} %bitcast.160), kind=kOutput, calls=%fused_computation.25 | convolution fusion | flops 1276379136 | bytes 11747840 | tf_op jit(solution)/shard_map/dot_general | solution.py:305
  29.9 2.7 %fusion.86 = (f16[128,2432]{1,0:T(8,128)(2,1)S(1)}, f32[128,2432]{1,0:T(8,128)}) fusion(f32[128,2432]{1,0:T(8,128)S(1)} %collective-permute-done.2, bf16[2048,2432]{1,0:T(8,128)(2,1)S(1)} %bitcast.153, bf16[128,2048]{1,0:T(8,128)(2,1)S(1)} %get-tuple-element.51, f32[128]{0:T(128)S(1)} %get-tuple-element.165, f32[2048]{0:T(1024)S(1)} %bitcast.167, ...), kind=kOutput, calls=%fused_computation.308 | convolution fusion | flops 1277001728 | bytes 13615616 | tf_op jit(solution)/shard_map/dot_general | solution.py:305
  39.2 2.3 %collective-permute-done.10 = f32[128,2432]{1,0:T(8,128)S(1)} collective-permute-done((f32[128,2432]{1,0:T(8,128)S(1)}, f32[128,2432]{1,0:T(8,128)S(1)}, u32[]{:S(2)}, u32[]{:S(2)}) %collective-permute-start.10) | collective-permute-done | bytes 1245216 | tf_op jit(solution)/shard_map/ppermute | solution.py:31
  41.5 2.5 %fusion.87 = (f16[128,2432]{1,0:T(8,128)(2,1)}, f32[128,2432]{1,0:T(8,128)S(1)}) fusion(f32[128,2432]{1,0:T(8,128)S(1)} %collective-permute-done.10, bf16[2048,2432]{1,0:T(8,128)(2,1)S(1)} %bitcast.153, f32[128]{0:T(128)S(1)} %get-tuple-element.158, f32[2048]{0:T(1024)S(1)} %bitcast.169, f32[2048]{0:T(1024)S(1)} %bitcast.163, ...), kind=kOutput, calls=%fused_computation.309 | convolution fusion | flops 1278836736 | bytes 13615616 | tf_op jit(solution)/shard_map/dot_general | solution.py:305
  44.0 11.0 %collective-permute-done.11 = f16[128,2432]{1,0:T(8,128)(2,1)S(1)} collective-permute-done((f16[128,2432]{1,0:T(8,128)(2,1)S(1)}, f16[128,2432]{1,0:T(8,128)(2,1)S(1)}, u32[]{:S(2)}, u32[]{:S(2)}) %collective-permute-start.11) | collective-permute-done | bytes 622624 | tf_op jit(solution)/shard_map/ppermute | solution.py:31
  61.8 12.4 %shard_map.79 = f32[512,2048]{1,0:T(8,128)} custom-call(bf16[512,2432]{1,0:T(8,128)(2,1)} %bitcast.145, bf16[512,2432]{1,0:T(8,128)(2,1)} %bitcast.146, bf16[512,2432]{1,0:T(8,128)(2,1)} %bitcast.147, bf16[512,2432]{1,0:T(8,128)(2,1)} %bitcast.148, bf16[2048,2432]{1,0:T(8,128)(2,1)} %refs_7_.5, bf16[2048,2432]{1,0:T(8,128)(2,1)} %refs_7_.5, ...), custom_call_target="tpu_custom_call" | custom-call | tf_op jit(solution)/shard_map/pallas_call | solution.py:221
  75.0 2.9 %collective-permute-done.15 = f32[3,256]{1,0:T(4,128)S(1)} collective-permute-done((f32[3,256]{1,0:T(4,128)S(1)}, f32[3,256]{1,0:T(4,128)S(1)}, u32[]{:S(2)}, u32[]{:S(2)}) %collective-permute-start.15) | collective-permute-done | bytes 3104 | tf_op jit(solution)/shard_map/ppermute | solution.py:31
  81.7 2.7 %collective-permute-start.17 = (f32[3,256]{1,0:T(4,128)S(1)}, f32[3,256]{1,0:T(4,128)S(1)}, u32[]{:S(2)}, u32[]{:S(2)}) collective-permute-start(f32[3,256]{1,0:T(4,128)S(1)} %pad_maximum_fusion.11), channel_id=1, source_target_pairs={{0,4},{1,5},{2,6},{3,7},{4,0},{5,1},{6,2},{7,3},{8,12},{9,13},{10,... | collective-permute-start | bytes 9224 | tf_op jit(solution)/shard_map/ppermute | solution.py:31
  86.3 2.5 %multiply_add_fusion.1 = f32[256,2048]{1,0:T(8,128)S(1)} fusion(f32[512,2048]{1,0:T(8,128)} %shard_map.79, f32[256]{0:T(256)S(1)} %get-tuple-element.120, f32[256]{0:T(256)S(1)} %get-tuple-element.121), kind=kLoop, calls=%fused_computation.8 | loop fusion | flops 1572864 | bytes 6293504 | tf_op jit(solution)/shard_map/add | solution.py:345
  94.1 12.1 %shard_map.81 = f32[512,2048]{1,0:T(8,128)} custom-call(bf16[512,2432]{1,0:T(8,128)(2,1)} %bitcast.141, bf16[512,2432]{1,0:T(8,128)(2,1)} %bitcast.142, bf16[512,2432]{1,0:T(8,128)(2,1)} %bitcast.143, bf16[512,2432]{1,0:T(8,128)(2,1)} %bitcast.144, bf16[2048,2432]{1,0:T(8,128)(2,1)} %refs_7_.5, bf16[2048,2432]{1,0:T(8,128)(2,1)} %refs_7_.5, ...), custom_call_target="tpu_custom_call" | custom-call | tf_op jit(solution)/shard_map/pallas_call | solution.py:221
  110.0 2.7 %collective-permute-start.20 = (f32[4,256]{1,0:T(4,128)S(1)}, f32[4,256]{1,0:T(4,128)S(1)}, u32[]{:S(2)}, u32[]{:S(2)}) collective-permute-start(f32[4,256]{1,0:T(4,128)S(1)} %pad_maximum_fusion.14), channel_id=1, source_target_pairs={{0,4},{1,5},{2,6},{3,7},{4,0},{5,1},{6,2},{7,3},{8,12},{9,13},{10,... | collective-permute-start | bytes 12296 | tf_op jit(solution)/shard_map/ppermute | solution.py:31
  114.6 2.5 %multiply_add_fusion = f32[256,2048]{1,0:T(8,128)S(1)} fusion(f32[512,2048]{1,0:T(8,128)} %shard_map.81, f32[256]{0:T(256)S(1)} %get-tuple-element.108, f32[256]{0:T(256)S(1)} %get-tuple-element.109), kind=kLoop, calls=%fused_computation.7 | loop fusion | flops 1572864 | bytes 6293504 | tf_op jit(solution)/shard_map/add | solution.py:345
  118.1 6.4 %collective-permute-done.21.refs_2_ = bf16[128,2432]{1,0:T(8,128)(2,1)S(1)} collective-permute-done((bf16[128,2432]{1,0:T(8,128)(2,1)S(1)}, bf16[128,2432]{1,0:T(8,128)(2,1)S(1)}, u32[]{:S(2)}, u32[]{:S(2)}) %collective-permute-start.21) | collective-permute-done | bytes 622624 | tf_op jit(solution)/shard_map/ppermute | solution.py:31
  125.1 2.3 %collective-permute-done.24.refs_5_ = f32[8,128]{1,0:T(8,128)S(1)} collective-permute-done((f32[8,128]{1,0:T(8,128)S(1)}, f32[8,128]{1,0:T(8,128)S(1)}, u32[]{:S(2)}, u32[]{:S(2)}) %collective-permute-start.24) | collective-permute-done | bytes 4128 | tf_op jit(solution)/shard_map/ppermute | solution.py:31
  135.0 12.9 %shard_map.83 = f32[512,2048]{1,0:T(8,128)} custom-call(bf16[512,2432]{1,0:T(8,128)(2,1)} %copy-done.1, bf16[512,2432]{1,0:T(8,128)(2,1)} %copy-done.1, bf16[512,2432]{1,0:T(8,128)(2,1)} %copy-done.1, bf16[512,2432]{1,0:T(8,128)(2,1)} %copy-done.1, bf16[2048,2432]{1,0:T(8,128)(2,1)} %refs_7_.5, bf16[2048,2432]{1,0:T(8,128)(2,1)} %refs_7_.5, ...), custom_call_target="tpu_custom_call" | custom-call | tf_op jit(solution)/shard_map/pallas_call | solution.py:221
  148.0 2.9 %fusion.69 = (bf16[256,2048]{1,0:T(8,128)(2,1)S(1)}, f32[256,2048]{1,0:T(8,128)S(1)}, bf16[256,2048]{1,0:T(8,128)(2,1)S(1)}, f32[256,2048]{1,0:T(8,128)S(1)}) fusion(f32[512,2048]{1,0:T(8,128)} %shard_map.83, f32[256]{0:T(256)S(1)} %get-tuple-element.100, f32[512,2048]{1,0:T(8,128)S(1)} %copy-done.6, f32[256]{0:T(256)S(1)} %copy-done.35, ...), kind=kLoop, calls=%fused_computation.295 | loop fusion | flops 4194304 | bytes 14684160 | tf_op jit(solution)/shard_map/convert.7
  151.0 3.0 %collective-permute-done.26 = bf16[128,2048]{1,0:T(8,128)(2,1)} collective-permute-done((bf16[128,2048]{1,0:T(8,128)(2,1)}, bf16[128,2048]{1,0:T(8,128)(2,1)}, u32[]{:S(2)}, u32[]{:S(2)}) %collective-permute-start.26) | collective-permute-done | bytes 524320 | tf_op jit(solution)/shard_map/ppermute | solution.py:31
  158.1 10.4 %collective-permute-done.28 = bf16[2,64,2048]{2,1,0:T(8,128)(2,1)S(1)} collective-permute-done((bf16[2,64,2048]{2,1,0:T(8,128)(2,1)S(1)}, bf16[2,64,2048]{2,1,0:T(8,128)(2,1)S(1)}, u32[]{:S(2)}, u32[]{:S(2)}) %collective-permute-start.28) | collective-permute-done | bytes 524320 | tf_op jit(solution)/shard_map/ppermute | solution.py:31
  172.9 9.0 %collective-permute-done.30 = bf16[1,64,2048]{2,1,0:T(8,128)(2,1)S(1)} collective-permute-done((bf16[1,64,2048]{2,1,0:T(8,128)(2,1)S(1)}, bf16[1,64,2048]{2,1,0:T(8,128)(2,1)S(1)}, u32[]{:S(2)}, u32[]{:S(2)}) %collective-permute-start.30) | collective-permute-done | bytes 262176 | tf_op jit(solution)/shard_map/ppermute | solution.py:31
  182.6 3.9 %collective-permute-start.33 = (bf16[1,64,1024]{2,1,0:T(8,128)(2,1)S(1)}, bf16[1,64,1024]{2,1,0:T(8,128)(2,1)S(1)}, u32[]{:S(2)}, u32[]{:S(2)}) collective-permute-start(bf16[1,64,1024]{2,1,0:T(8,128)(2,1)S(1)} %dynamic-slice_convert_fusion.2), channel_id=1, source_target_pairs={{0,4},{1,5},{2,6},{3,7},{4,0},{5,1},{6,2},{7,3},{8,12},{9,13},{10,... | collective-permute-start | bytes 393224 | tf_op jit(solution)/shard_map/ppermute | solution.py:31
  186.9 3.9 %collective-permute-done.33 = bf16[1,64,1024]{2,1,0:T(8,128)(2,1)S(1)} collective-permute-done((bf16[1,64,1024]{2,1,0:T(8,128)(2,1)S(1)}, bf16[1,64,1024]{2,1,0:T(8,128)(2,1)S(1)}, u32[]{:S(2)}, u32[]{:S(2)}) %collective-permute-start.33) | collective-permute-done | bytes 131104 | tf_op jit(solution)/shard_map/ppermute | solution.py:31
  193.7 6.2 %collective-permute-done.35 = bf16[1,64,1024]{2,1,0:T(8,128)(2,1)S(1)} collective-permute-done((bf16[1,64,1024]{2,1,0:T(8,128)(2,1)S(1)}, bf16[1,64,1024]{2,1,0:T(8,128)(2,1)S(1)}, u32[]{:S(2)}, u32[]{:S(2)}) %collective-permute-start.35) | collective-permute-done | bytes 131104 | tf_op jit(solution)/shard_map/ppermute | solution.py:31
  (245 shorter events, 75.4 us)
Async XLA Ops:
  5.4 9.7 %collective-permute-start.3 = (bf16[64,2048]{1,0:T(8,128)(2,1)S(1)}, bf16[64,2048]{1,0:T(8,128)(2,1)S(1)}, u32[]{:S(2)}, u32[]{:S(2)}) collective-permute-start(bf16[64,2048]{1,0:T(8,128)(2,1)S(1)} %get-tuple-element.56), channel_id=1, source_target_pairs={{0,16},{8,24},{16,0},{24,8},{1,17},{9,25},{17,1},{25,9},{2,18},{10... | collective-permute-start | bytes 786440 | tf_op jit(solution)/shard_map/ppermute | solution.py:31
  8.0 16.1 %collective-permute-start.4 = (bf16[64,2048]{1,0:T(8,128)(2,1)S(1)}, bf16[64,2048]{1,0:T(8,128)(2,1)S(1)}, u32[]{:S(2)}, u32[]{:S(2)}) collective-permute-start(bf16[64,2048]{1,0:T(8,128)(2,1)S(1)} %get-tuple-element.57), channel_id=1, source_target_pairs={{0,24},{8,16},{16,8},{24,0},{1,25},{9,17},{17,9},{25,1},{2,26},{10... | collective-permute-start | bytes 786440 | tf_op jit(solution)/shard_map/ppermute | solution.py:31
  8.0 7.1 %collective-permute-start = (bf16[128,2048]{1,0:T(8,128)(2,1)S(1)}, bf16[128,2048]{1,0:T(8,128)(2,1)S(1)}, u32[]{:S(2)}, u32[]{:S(2)}) collective-permute-start(bf16[128,2048]{1,0:T(8,128)(2,1)S(1)} %get-tuple-element.54), channel_id=1, source_target_pairs={{0,8},{8,0},{16,24},{24,16},{1,9},{9,1},{17,25},{25,17},{2,10},{10... | collective-permute-start | bytes 1572872 | tf_op jit(solution)/shard_map/ppermute | solution.py:31
  8.7 23.9 %collective-permute-start.7 = (f32[2,8,128]{2,1,0:T(8,128)S(1)}, f32[2,8,128]{2,1,0:T(8,128)S(1)}, u32[]{:S(2)}, u32[]{:S(2)}) collective-permute-start(f32[2,8,128]{2,1,0:T(8,128)S(1)} %pad_maximum_fusion.8), channel_id=1, source_target_pairs={{0,16},{8,24},{16,0},{24,8},{1,17},{9,25},{17,1},{25,9},{2,18},{10... | collective-permute-start | bytes 24584 | tf_op jit(solution)/shard_map/ppermute | solution.py:31
  23.5 6.4 %collective-permute-start.2 = (f32[128,2432]{1,0:T(8,128)S(1)}, f32[128,2432]{1,0:T(8,128)S(1)}, u32[]{:S(2)}, u32[]{:S(2)}) collective-permute-start(f32[128,2432]{1,0:T(8,128)S(1)} %fusion.2), channel_id=1, source_target_pairs={{0,8},{8,0},{16,24},{24,16},{1,9},{9,1},{17,25},{25,17},{2,10},{10... | collective-permute-start | bytes 3735560 | tf_op jit(solution)/shard_map/ppermute | solution.py:31
  26.7 8.2 %collective-permute-start.6 = (bf16[2,32,2048]{2,1,0:T(8,128)(2,1)S(1)}, bf16[2,32,2048]{2,1,0:T(8,128)(2,1)S(1)}, u32[]{:S(2)}, u32[]{:S(2)}) collective-permute-start(bf16[2,32,2048]{2,1,0:T(8,128)(2,1)S(1)} %pad_maximum_fusion.5), channel_id=1, source_target_pairs={{0,1},{1,0},{2,3},{3,2},{4,5},{5,4},{6,7},{7,6},{8,9},{9,8},{10,11... | collective-permute-start | bytes 786440 | tf_op jit(solution)/shard_map/ppermute | solution.py:31
  28.3 7.8 %collective-permute-start.5 = (bf16[2,32,2048]{2,1,0:T(8,128)(2,1)S(1)}, bf16[2,32,2048]{2,1,0:T(8,128)(2,1)S(1)}, u32[]{:S(2)}, u32[]{:S(2)}) collective-permute-start(bf16[2,32,2048]{2,1,0:T(8,128)(2,1)S(1)} %pad_maximum_fusion.5), channel_id=1, source_target_pairs={{0,2},{1,3},{2,0},{3,1},{4,6},{5,7},{6,4},{7,5},{8,10},{9,11},{10,... | collective-permute-start | bytes 786440 | tf_op jit(solution)/shard_map/ppermute | solution.py:31
  38.6 16.4 %collective-permute-start.11 = (f16[128,2432]{1,0:T(8,128)(2,1)S(1)}, f16[128,2432]{1,0:T(8,128)(2,1)S(1)}, u32[]{:S(2)}, u32[]{:S(2)}) collective-permute-start(f16[128,2432]{1,0:T(8,128)(2,1)S(1)} %get-tuple-element.59), channel_id=1, source_target_pairs={{0,16},{8,24},{16,0},{24,8},{1,17},{9,25},{17,1},{25,9},{2,18},{10... | collective-permute-start | bytes 1867784 | tf_op jit(solution)/shard_map/ppermute | solution.py:31
  55.3 19.0 %collective-permute-start.12 = (f16[128,2432]{1,0:T(8,128)(2,1)}, f16[128,2432]{1,0:T(8,128)(2,1)S(1)}, u32[]{:S(2)}, u32[]{:S(2)}) collective-permute-start(f16[128,2432]{1,0:T(8,128)(2,1)} %get-tuple-element.65), channel_id=1, source_target_pairs={{0,16},{8,24},{16,0},{24,8},{1,17},{9,25},{17,1},{25,9},{2,18},{10... | collective-permute-start | bytes 1867784 | tf_op jit(solution)/shard_map/ppermute | solution.py:31
  79.8 10.0 %collective-permute-start.14 = (f32[128,2432]{1,0:T(8,128)S(1)}, f32[128,2432]{1,0:T(8,128)S(1)}, u32[]{:S(2)}, u32[]{:S(2)}) collective-permute-start(f32[128,2432]{1,0:T(8,128)S(1)} %convert_add_fusion.first), channel_id=1, source_target_pairs={{0,8},{8,0},{16,24},{24,16},{1,9},{9,1},{17,25},{25,17},{2,10},{10... | collective-permute-start | bytes 3735560 | tf_op jit(solution)/shard_map/ppermute | solution.py:31
  93.5 12.7 %collective-permute-start.18 = (f32[4,256]{1,0:T(4,128)S(1)}, f32[4,256]{1,0:T(4,128)S(1)}, u32[]{:S(2)}, u32[]{:S(2)}) collective-permute-start(f32[4,256]{1,0:T(4,128)S(1)} %pad_maximum_fusion.12), channel_id=1, source_target_pairs={{0,1},{1,0},{2,3},{3,2},{4,5},{5,4},{6,7},{7,6},{8,9},{9,8},{10,11... | collective-permute-start | bytes 12296 | tf_op jit(solution)/shard_map/ppermute | solution.py:31
  112.6 11.8 %collective-permute-start.21 = (bf16[128,2432]{1,0:T(8,128)(2,1)S(1)}, bf16[128,2432]{1,0:T(8,128)(2,1)S(1)}, u32[]{:S(2)}, u32[]{:S(2)}) collective-permute-start(bf16[128,2432]{1,0:T(8,128)(2,1)S(1)} %copy-done.3), channel_id=1, source_target_pairs={{0,16},{8,24},{16,0},{24,8},{1,17},{9,25},{17,1},{25,9},{2,18},{10... | collective-permute-start | bytes 1867784 | tf_op jit(solution)/shard_map/ppermute | solution.py:31
  124.4 8.2 %collective-permute-start.22 = (bf16[128,2432]{1,0:T(8,128)(2,1)S(1)}, bf16[128,2432]{1,0:T(8,128)(2,1)S(1)}, u32[]{:S(2)}, u32[]{:S(2)}) collective-permute-start(bf16[128,2432]{1,0:T(8,128)(2,1)S(1)} %copy-done.3), channel_id=1, source_target_pairs={{0,8},{8,0},{16,24},{24,16},{1,9},{9,1},{17,25},{25,17},{2,10},{10... | collective-permute-start | bytes 1867784 | tf_op jit(solution)/shard_map/ppermute | solution.py:31
  124.4 8.2 %collective-permute-start.23 = (bf16[128,2432]{1,0:T(8,128)(2,1)S(1)}, bf16[128,2432]{1,0:T(8,128)(2,1)S(1)}, u32[]{:S(2)}, u32[]{:S(2)}) collective-permute-start(bf16[128,2432]{1,0:T(8,128)(2,1)S(1)} %collective-permute-done.21.refs_2_), channel_id=1, source_target_pairs={{0,8},{8,0},{16,24},{24,16},{1,9},{9,1},{17,25},{25,17},{2,10},{10... | collective-permute-start | bytes 1867784 | tf_op jit(solution)/shard_map/ppermute | solution.py:31
  128.7 22.3 %collective-permute-start.27 = (bf16[128,2048]{1,0:T(8,128)(2,1)}, bf16[128,2048]{1,0:T(8,128)(2,1)S(1)}, u32[]{:S(2)}, u32[]{:S(2)}) collective-permute-start(bf16[128,2048]{1,0:T(8,128)(2,1)} %slice.446), channel_id=1, source_target_pairs={{0,1},{1,0},{2,3},{3,2},{4,5},{5,4},{6,7},{7,6},{8,9},{9,8},{10,11... | collective-permute-start | bytes 1572872 | tf_op jit(solution)/shard_map/ppermute | solution.py:31
  130.3 23.7 %collective-permute-start.26 = (bf16[128,2048]{1,0:T(8,128)(2,1)}, bf16[128,2048]{1,0:T(8,128)(2,1)}, u32[]{:S(2)}, u32[]{:S(2)}) collective-permute-start(bf16[128,2048]{1,0:T(8,128)(2,1)} %slice.445), channel_id=1, source_target_pairs={{0,1},{1,0},{2,3},{3,2},{4,5},{5,4},{6,7},{7,6},{8,9},{9,8},{10,11... | collective-permute-start | bytes 1572872 | tf_op jit(solution)/shard_map/ppermute | solution.py:31
  155.6 12.9 %collective-permute-start.28 = (bf16[2,64,2048]{2,1,0:T(8,128)(2,1)S(1)}, bf16[2,64,2048]{2,1,0:T(8,128)(2,1)S(1)}, u32[]{:S(2)}, u32[]{:S(2)}) collective-permute-start(bf16[2,64,2048]{2,1,0:T(8,128)(2,1)S(1)} %fusion.4), channel_id=1, source_target_pairs={{0,2},{1,3},{2,0},{3,1},{4,6},{5,7},{6,4},{7,5},{8,10},{9,11},{10,... | collective-permute-start | bytes 1572872 | tf_op jit(solution)/shard_map/ppermute | solution.py:31
  156.4 12.5 %collective-permute-start.29 = (bf16[256,1024]{1,0:T(8,128)(2,1)S(1)}, bf16[256,1024]{1,0:T(8,128)(2,1)S(1)}, u32[]{:S(2)}, u32[]{:S(2)}) collective-permute-start(bf16[256,1024]{1,0:T(8,128)(2,1)S(1)} %pad_maximum_fusion.3), channel_id=1, source_target_pairs={{0,1},{1,0},{2,3},{3,2},{4,5},{5,4},{6,7},{7,6},{8,9},{9,8},{10,11... | collective-permute-start | bytes 1572872 | tf_op jit(solution)/shard_map/ppermute | solution.py:31
  169.1 12.7 %collective-permute-start.30 = (bf16[1,64,2048]{2,1,0:T(8,128)(2,1)S(1)}, bf16[1,64,2048]{2,1,0:T(8,128)(2,1)S(1)}, u32[]{:S(2)}, u32[]{:S(2)}) collective-permute-start(bf16[1,64,2048]{2,1,0:T(8,128)(2,1)S(1)} %dynamic-slice_convert_fusion), channel_id=1, source_target_pairs={{0,4},{1,5},{2,6},{3,7},{4,0},{5,1},{6,2},{7,3},{8,12},{9,13},{10,... | collective-permute-start | bytes 786440 | tf_op jit(solution)/shard_map/ppermute | solution.py:31
  169.6 12.4 %collective-permute-start.32 = (bf16[256,1024]{1,0:T(8,128)(2,1)S(1)}, bf16[256,1024]{1,0:T(8,128)(2,1)S(1)}, u32[]{:S(2)}, u32[]{:S(2)}) collective-permute-start(bf16[256,1024]{1,0:T(8,128)(2,1)S(1)} %pad_maximum_fusion.4), channel_id=1, source_target_pairs={{0,1},{1,0},{2,3},{3,2},{4,5},{5,4},{6,7},{7,6},{8,9},{9,8},{10,11... | collective-permute-start | bytes 1572872 | tf_op jit(solution)/shard_map/ppermute | solution.py:31
  171.3 10.6 %collective-permute-start.31 = (bf16[2,64,1024]{2,1,0:T(8,128)(2,1)S(1)}, bf16[2,64,1024]{2,1,0:T(8,128)(2,1)S(1)}, u32[]{:S(2)}, u32[]{:S(2)}) collective-permute-start(bf16[2,64,1024]{2,1,0:T(8,128)(2,1)S(1)} %fusion.17), channel_id=1, source_target_pairs={{0,2},{1,3},{2,0},{3,1},{4,6},{5,7},{6,4},{7,5},{8,10},{9,11},{10,... | collective-permute-start | bytes 786440 | tf_op jit(solution)/shard_map/ppermute | solution.py:31
  182.2 10.1 %collective-permute-start.34 = (bf16[2,64,1024]{2,1,0:T(8,128)(2,1)S(1)}, bf16[2,64,1024]{2,1,0:T(8,128)(2,1)S(1)}, u32[]{:S(2)}, u32[]{:S(2)}) collective-permute-start(bf16[2,64,1024]{2,1,0:T(8,128)(2,1)S(1)} %fusion.18), channel_id=1, source_target_pairs={{0,2},{1,3},{2,0},{3,1},{4,6},{5,7},{6,4},{7,5},{8,10},{9,11},{10,... | collective-permute-start | bytes 786440 | tf_op jit(solution)/shard_map/ppermute | solution.py:31
  182.6 8.2 %collective-permute-start.33 = (bf16[1,64,1024]{2,1,0:T(8,128)(2,1)S(1)}, bf16[1,64,1024]{2,1,0:T(8,128)(2,1)S(1)}, u32[]{:S(2)}, u32[]{:S(2)}) collective-permute-start(bf16[1,64,1024]{2,1,0:T(8,128)(2,1)S(1)} %dynamic-slice_convert_fusion.2), channel_id=1, source_target_pairs={{0,4},{1,5},{2,6},{3,7},{4,0},{5,1},{6,2},{7,3},{8,12},{9,13},{10,... | collective-permute-start | bytes 393224 | tf_op jit(solution)/shard_map/ppermute | solution.py:31
  192.4 7.5 %collective-permute-start.35 = (bf16[1,64,1024]{2,1,0:T(8,128)(2,1)S(1)}, bf16[1,64,1024]{2,1,0:T(8,128)(2,1)S(1)}, u32[]{:S(2)}, u32[]{:S(2)}) collective-permute-start(bf16[1,64,1024]{2,1,0:T(8,128)(2,1)S(1)} %dynamic-slice_convert_fusion.1), channel_id=1, source_target_pairs={{0,4},{1,5},{2,6},{3,7},{4,0},{5,1},{6,2},{7,3},{8,12},{9,13},{10,... | collective-permute-start | bytes 393224 | tf_op jit(solution)/shard_map/ppermute | solution.py:31
  (57 other events, 389.2 us)

commit v4 on v1

--- a/solution.py
+++ b/solution.py
@@ -13,10 +13,6 @@
 PAIR = 2
 LIGHT = pl.CostEstimate(flops=0, bytes_accessed=0, transcendentals=0)
 F32, BF16 = jnp.float32, jnp.bfloat16
-
-
-def params(mebibytes):
-    return pltpu.CompilerParams(vmem_limit_bytes=mebibytes * 1024 * 1024)
 
 
 def whole_spec():
@@ -101,7 +97,6 @@
             jax.ShapeDtypeStruct((vectors.shape[0], width), F32),
             jax.ShapeDtypeStruct((16, width), BF16),
         ],
-        compiler_params=params(12),
         cost_estimate=LIGHT,
     )(at, hidden, vectors)
 
@@ -146,7 +141,6 @@
             jax.ShapeDtypeStruct((8, rows), F32),
         ],
         scratch_shapes=[pltpu.VMEM((rows, 128), F32)],
-        compiler_params=params(16),
         cost_estimate=LIGHT,
     )(at, first, second, row, sums_a, sums_b)
 
@@ -178,7 +172,6 @@
             jax.ShapeDtypeStruct((rows, width), BF16),
             jax.ShapeDtypeStruct((rows, 128), F32),
         ],
-        compiler_params=params(12),
         cost_estimate=LIGHT,
     )(at, *blocks, *totals)
 
@@ -209,7 +202,6 @@
         ],
         out_specs=pl.BlockSpec((rows, tile), lambda i: (0, i)),
         out_shape=jax.ShapeDtypeStruct((rows, features), F32),
-        compiler_params=params(20),
         cost_estimate=LIGHT,
     )(cotangent, head)
 
@@ -223,16 +215,16 @@
     return jnp.stack([peak, total, mean] + [first[i] + second[i] for i in range(3, len(first))])
 
 
-def exchange(value, size):
+def exchange(value, size, beside):
     half = value.shape[1] // 2
-    other = swap(value, "vocab", 1, size)
+    other, beside = lax.optimization_barrier((swap(value, "vocab", 1, size), beside))
     aligned = jnp.concatenate([other[:3, half:], other[:3, :half]], axis=1)
     value = merge(value, jnp.concatenate([aligned, other[3:]], axis=0))
     bit = PAIR
     while bit < size:
         value = merge(value, swap(value, "vocab", bit, size))
         bit *= 2
-    return value
+    return value, beside
 
 
 def body(hidden, steer, tangent, gain, head, target):
@@ -276,9 +268,6 @@
     sums_1 = swap(sums_0, "seq", 1, seq_size)
     over_2, over_3 = swap(over_2, "seq", 2, seq_size), swap(over_3, "seq", 3, seq_size)
     both = swap(jnp.stack([sums_0, sums_1]), "seq", 2, seq_size)
-    near = jnp.stack([over_2[:quarter], over_3[:quarter]])
-    by_y = swap(near, "vocab", 2, vocab_size)
-    by_z = swap(near, "vocab", 1, vocab_size)
     steer_part, gain_part = parts[0], parts[2]
 
     def partial_logits(block, sums_of):
@@ -287,16 +276,21 @@
         normed = (gain_part * values / radius[:, None]).astype(BF16)
         return jnp.dot(normed, head, preferred_element_type=F32)
 
+    given = partial_logits(mate, sums_1)
+    two, given = lax.optimization_barrier((two, given))
+    given = swap(given, "seq", 1, seq_size)
     row = jnp.sum(jnp.dot(two, head, preferred_element_type=F32), axis=0, keepdims=True)
     row = row + swap(row, "seq", 1, seq_size)
     tangent_row = row + swap(row, "seq", 2, seq_size)
-    given = swap(partial_logits(mate, sums_1), "seq", 1, seq_size)
     summed_0 = partial_logits(own, sums_0) + given
-    send_0, tangent_row = lax.optimization_barrier((summed_0.astype(jnp.float16), tangent_row))
+    send_0 = summed_0.astype(jnp.float16)
+    over_2, over_3, both, send_0, tangent_row = lax.optimization_barrier(
+        (over_2, over_3, both, send_0, tangent_row)
+    )
     got_2 = swap(send_0, "seq", 2, seq_size)
-    by_y, by_z, over_2, over_3, both, _ = lax.optimization_barrier(
-        (by_y, by_z, over_2, over_3, both, send_0)
-    )
+    near = jnp.stack([over_2[:quarter], over_3[:quarter]])
+    by_y = swap(near, "vocab", 2, vocab_size)
+    by_z = swap(near, "vocab", 1, vocab_size)
     sums = [sums_0, sums_1, both[0], both[1]]
     denominators = [s[0] / feature_count + EPSILON for s in sums]
 
@@ -311,41 +305,58 @@
 
     half = rows // 2
 
-    def half_of(base, summed, got, where, extra):
+    def soften_of(base, summed, got, where):
         full = summed + got.astype(F32)
         mates = swap(full, "seq", 1, seq_size)
         both, stats = soften(
             where, full, mates, tangent_row, sums[base], sums[base + 1], feature_count
         )
-        stats = stats[:3]
-        joint = exchange(jnp.concatenate([stats] + extra), vocab_size)
-        raw = back(both.reshape(2 * half, -1), head)
+        return both.reshape(2 * half, -1), stats[:3]
+
+    def scaled_of(raw, stats, joint):
         scale = jnp.exp(stats[0] - joint[0]) / joint[1]
         lean = scale * (stats[2] - joint[2])
         plain = scale[:, None] * raw[:half]
         ggn = scale[:, None] * raw[half:] + lean[:, None] * raw[:half]
-        return plain, ggn[half // 2 :].astype(BF16), ggn[: half // 2], joint
-
-    plain_other, theirs_other, kept_other, _ = half_of(2, summed_2, got_2, other_places, [])
-    got_0, target, theirs_other = lax.optimization_barrier((got_0, target, theirs_other))
+        return plain, ggn[half // 2 :].astype(BF16), ggn[: half // 2]
+
+    both_other, stats_other = soften_of(2, summed_2, got_2, other_places)
+    raw_other = back(both_other, head)
+    got_0, target, raw_other, stats_other = lax.optimization_barrier(
+        (got_0, target, raw_other, stats_other)
+    )
+    target_2 = swap(target, "seq", 2, seq_size)
+    own_total = jnp.sum(target.astype(F32), axis=1)
+    joint_other, raw_other = exchange(
+        jnp.concatenate([stats_other, jnp.concatenate([own_total, own_total])[None]]),
+        vocab_size,
+        raw_other,
+    )
+    plain_other, theirs_other, kept_other = scaled_of(raw_other, stats_other, joint_other)
     got_other = swap(theirs_other, "vocab", 1, vocab_size)
-    own_total = jnp.sum(target.astype(F32), axis=1)
-    plain_own, theirs_own, kept_own, joint = half_of(
-        0, summed_0, got_0, own_places, [jnp.concatenate([own_total, own_total])[None]]
-    )
-
-    target_2 = swap(target, "seq", 2, seq_size)
+
     target_1 = swap(target, "seq", 1, seq_size)
+    total_0 = jnp.broadcast_to(joint_other[3, :tokens], (8, tokens))
+    total_1 = swap(total_0, "seq", 1, seq_size)
+    both_totals = swap(jnp.stack([total_0, total_1]), "seq", 2, seq_size)
+
+    both_own, stats_own = soften_of(0, summed_0, got_0, own_places)
+    stats_own, theirs_other = lax.optimization_barrier((stats_own, theirs_other))
+    joint, (raw_own, got_other, target_1, target_2, both_totals) = exchange(
+        stats_own,
+        vocab_size,
+        (back(both_own, head), got_other, target_1, target_2, both_totals),
+    )
+    plain_own, theirs_own, kept_own = scaled_of(raw_own, stats_own, joint)
+    got_own = swap(theirs_own, "vocab", 1, vocab_size)
+
     target_3 = swap(target_2, "seq", 1, seq_size)
-    total_0 = jnp.broadcast_to(joint[3, :tokens], (8, tokens))
-    total_1 = swap(total_0, "seq", 1, seq_size)
-    both = swap(jnp.stack([total_0, total_1]), "seq", 2, seq_size)
     ordered, columns = order(
         target_places,
         [target, target_1, target_2, target_3],
-        [total_0, total_1, both[0], both[1]],
-    )
-    ordered, theirs_own = lax.optimization_barrier((ordered, theirs_own))
+        [total_0, total_1, both_totals[0], both_totals[1]],
+    )
+    ordered, _ = lax.optimization_barrier((ordered, theirs_own))
     weighed = back(ordered, head)
     inverse = columns[:, 0:1]
     gradients = [
@@ -364,7 +375,6 @@
         kept = lax.dynamic_index_in_dim(joined, place, axis, False)
         return sent.astype(BF16), kept
 
-    got_own = swap(theirs_own, "vocab", 1, vocab_size)
     chunks = []
     for begin in (0, width // 2):
         part = [g[:, begin : begin + width // 2] for g in gradients]

time: 191 us -> 208 us (1.089)
  Pallas kernels: 28.5 us -> 52.5 us
  waiting for transfers between devices: 88.5 us -> 67.3 us
  other arithmetic: 7.49 us -> 22.9 us
  local copies, waits for them, and re-layouts: 16.7 us -> 11.5 us
  starting transfers between devices: 34.2 us -> 37.2 us
    ppermute x38, waiting for transfers between devices: 88.5 us -> 67.3 us  [swap(): return lax.ppermute(value, axis, [(i, i ^ bit) for i in range(size)])]
    pallas_call x3, Pallas kernels: 21.7 us -> 36 us  [back(): pl.pallas_call(functools.partial(back_kernel, deep), grid=(features // ti...]
    unnamed x70 -> x68, local copies, waits for them, and re-layouts: 15 us -> 5.43 us
    pallas_call x2, Pallas kernels: 4.42 us -> 9.3 us  [soften(): pl.pallas_call(functools.partial(soften_kernel, feature_count), in_specs=...]
    add x4, other arithmetic: 0.84 us -> 5.29 us  [the longest x2 5.04 us: scaled_of(): ggn = scale[:, None] * raw[half:] + lean[:, None] * raw[:half]]
    dot_general x4, matrix products: 8.34 us -> 12.4 us  [partial_logits(): return jnp.dot(normed, head, preferred_element_type=F32)]
    dot_general x1, matrix products: 5.4 us -> 1.42 us  [body(): jnp.dot(two, head, preferred_element_type=F32)]
    another operation x2, other arithmetic: 0.65 us -> 4.1 us
  transfers between devices with their start and end apart: 38 -> 38, of which waited for: 24 -> 22; matrix products, arithmetic and copies ran while one was open for 9% -> 16% of each run, Pallas kernels for 12% -> 24%
where the time goes in v4:
time: 208 us; the launch traced here: 207 us
  waiting for transfers between devices  67.3 us (32%)
  Pallas kernels  52.5 us (25%)
  starting transfers between devices  37.2 us (18%)
  other arithmetic  22.9 us (11%)
  matrix products  13.8 us (7%)
  local copies, waits for them, and re-layouts  11.5 us (6%)
    ppermute x38, waiting for transfers between devices, swap(): return lax.ppermute(value, axis, [(i, i ^ bit) for i in range(size)])  67.3 us
    ppermute x38, starting transfers between devices, swap(): return lax.ppermute(value, axis, [(i, i ^ bit) for i in range(size)])  37.2 us
    pallas_call x3, Pallas kernels, back(): pl.pallas_call(functools.partial(back_kernel, deep), grid=(features // ti...  36 us
    dot_general x4, matrix products, partial_logits(): return jnp.dot(normed, head, preferred_element_type=F32)  12.4 us
    pallas_call x2, Pallas kernels, soften(): pl.pallas_call(functools.partial(soften_kernel, feature_count), in_specs=...  9.3 us
    unnamed x68, local copies, waits for them, and re-layouts  5.43 us
    add x2, other arithmetic, scaled_of(): ggn = scale[:, None] * raw[half:] + lean[:, None] * raw[:half]  5.04 us
  transfers between devices with their start and end apart: 38, of which 22 were waited for; matrix products, arithmetic and copies ran while one was open for 16% of the time, Pallas kernels for 24%

profile of v4, /device:TPU:0, one launch (start us, length us, event | category | flops | bytes accessed | tf_op | source)
XLA Modules:
  0.0 206.7 jit_solution(4719383851697722116)
XLA Ops:
  2.9 3.8 %shard_map.77 = (bf16[128,2048]{1,0:T(8,128)(2,1)}, bf16[128,2048]{1,0:T(8,128)(2,1)}, bf16[64,2048]{1,0:T(8,128)(2,1)}, bf16[64,2048]{1,0:T(8,128)(2,1)}, f32[8...) custom-call(s32[2]{0:T(128)} %pad_add_fusion.at, bf16[128,8192]{1,0:T(8,128)(2,1)} %hidden.1, ...), custom_call_target="tpu_custom_call" | custom-call | tf_op jit(solution)/shard_map/pallas_call | solution.py:87
  7.1 2.6 %collective-permute-start.3 = (bf16[64,2048]{1,0:T(8,128)(2,1)}, bf16[64,2048]{1,0:T(8,128)(2,1)S(1)}, u32[]{:S(2)}, u32[]{:S(2)}) collective-permute-start(bf16[64,2048]{1,0:T(8,128)(2,1)} %get-tuple-element.56), channel_id=1, source_target_pairs={{0,16},{8,24},{16,0},{24,8},{1,17},{9,25},{17,1},{25,9},{2,18},{10... | collective-permute-start | bytes 786440 | tf_op jit(solution)/shard_map/ppermute | solution.py:27
  11.9 5.7 %fusion.2 = f32[128,2432]{1,0:T(8,128)S(1)} fusion(bf16[2048,2432]{1,0:T(8,128)(2,1)} %head.5, bf16[128,2048]{1,0:T(8,128)(2,1)S(1)} %collective-permute-done, f32[128]{0:T(128)S(1)} %get-tuple-element.169, f32[2048]{0:T(1024)S(1)} %bitcast.157, f32[2048]{0:T(1024)S(1)} %bitcast.151), kind=kOutput, calls=%fused_computation.25 | convolution fusion | flops 1276379136 | bytes 11747840 | tf_op jit(solution)/shard_map/dot_general | solution.py:277
  25.4 2.7 %fusion.86 = (f16[128,2432]{1,0:T(8,128)(2,1)S(1)}, f32[128,2432]{1,0:T(8,128)}) fusion(f32[128,2432]{1,0:T(8,128)S(1)} %collective-permute-done.2, bf16[2048,2432]{1,0:T(8,128)(2,1)S(1)} %bitcast.142, bf16[128,2048]{1,0:T(8,128)(2,1)S(1)} %copy-done.20, f32[128]{0:T(128)S(1)} %get-tuple-element.167, f32[2048]{0:T(1024)S(1)} %bitcast.158, ...), kind=kOutput, calls=%fused_computation.308 | convolution fusion | flops 1277001728 | bytes 13615616 | tf_op jit(solution)/shard_map/dot_general | solution.py:277
  31.7 4.1 %collective-permute-done.9 = bf16[2,32,2048]{2,1,0:T(8,128)(2,1)S(1)} collective-permute-done((bf16[2,32,2048]{2,1,0:T(8,128)(2,1)S(1)}, bf16[2,32,2048]{2,1,0:T(8,128)(2,1)S(1)}, u32[]{:S(2)}, u32[]{:S(2)}) %collective-permute-start.9) | collective-permute-done | bytes 262176 | tf_op jit(solution)/shard_map/ppermute | solution.py:27
  41.9 2.4 %fusion.87 = (f16[128,2432]{1,0:T(8,128)(2,1)}, f32[128,2432]{1,0:T(8,128)S(1)}) fusion(f32[128,2432]{1,0:T(8,128)S(1)} %collective-permute-done.10, bf16[2048,2432]{1,0:T(8,128)(2,1)S(1)} %bitcast.142, f32[128]{0:T(128)S(1)} %get-tuple-element.160, f32[2048]{0:T(1024)S(1)} %bitcast.160, f32[2048]{0:T(1024)S(1)} %bitcast.154, ...), kind=kOutput, calls=%fused_computation.309 | convolution fusion | flops 1278836736 | bytes 13615616 | tf_op jit(solution)/shard_map/dot_general | solution.py:277
  44.3 11.1 %collective-permute-done.11 = f16[128,2432]{1,0:T(8,128)(2,1)S(1)} collective-permute-done((f16[128,2432]{1,0:T(8,128)(2,1)S(1)}, f16[128,2432]{1,0:T(8,128)(2,1)S(1)}, u32[]{:S(2)}, u32[]{:S(2)}) %collective-permute-start.11) | collective-permute-done | bytes 622624 | tf_op jit(solution)/shard_map/ppermute | solution.py:27
  59.6 4.7 %shard_map.78 = (bf16[2,256,2432]{2,1,0:T(8,128)(2,1)}, f32[8,256]{1,0:T(8,128)}) custom-call(s32[8]{0:T(128)} %pad_add_fusion.2.at, f32[128,2432]{1,0:T(8,128)} %copy-done.2, f32[128,2432]{1,0:T(8,128)} %copy-done.5, f32[1,2432]{1,0:T(1,128)} %add.596.row, f32[8,128]{1,0:T(8,128)} %get-tuple-element.165.sums_a, f32[8,128]{1,0:T(8,128)} %get-tuple-element.164.sums_b), custom_call_target="tpu_custom_call" | custom-call | tf_op jit(solution)/shard_map/pallas_call | solution.py:135
  65.0 12.1 %shard_map.79 = f32[512,2048]{1,0:T(8,128)} custom-call(bf16[512,2432]{1,0:T(8,128)(2,1)} %bitcast.150, bf16[2048,2432]{1,0:T(8,128)(2,1)} %head.5), custom_call_target="tpu_custom_call" | custom-call | tf_op jit(solution)/shard_map/pallas_call | solution.py:196
  78.8 3.2 %collective-permute-done.15 = f32[4,256]{1,0:T(4,128)S(1)} collective-permute-done((f32[4,256]{1,0:T(4,128)S(1)}, f32[4,256]{1,0:T(4,128)S(1)}, u32[]{:S(2)}, u32[]{:S(2)}) %collective-permute-start.15) | collective-permute-done | bytes 4128 | tf_op jit(solution)/shard_map/ppermute | solution.py:27
  85.9 2.7 %collective-permute-start.17 = (f32[4,256]{1,0:T(4,128)S(1)}, f32[4,256]{1,0:T(4,128)S(1)}, u32[]{:S(2)}, u32[]{:S(2)}) collective-permute-start(f32[4,256]{1,0:T(4,128)S(1)} %pad_maximum_fusion.12), channel_id=1, source_target_pairs={{0,4},{1,5},{2,6},{3,7},{4,0},{5,1},{6,2},{7,3},{8,12},{9,13},{10,... | collective-permute-start | bytes 12296 | tf_op jit(solution)/shard_map/ppermute | solution.py:27
  90.5 2.5 %multiply_add_fusion.1 = f32[256,2048]{1,0:T(8,128)S(1)} fusion(f32[512,2048]{1,0:T(8,128)} %shard_map.79, f32[256]{0:T(256)S(1)} %get-tuple-element.120, f32[256]{0:T(256)S(1)} %get-tuple-element.121), kind=kLoop, calls=%fused_computation.8 | loop fusion | flops 1572864 | bytes 6293504 | tf_op jit(solution)/shard_map/add | solution.py:320
  96.3 4.6 %shard_map.80 = (bf16[2,256,2432]{2,1,0:T(8,128)(2,1)}, f32[8,256]{1,0:T(8,128)}) custom-call(s32[8]{0:T(128)} %pad_add_fusion.1.at, f32[128,2432]{1,0:T(8,128)} %copy-done.3, f32[128,2432]{1,0:T(8,128)} %collective-permute-done.14.second, f32[1,2432]{1,0:T(1,128)} %add.596.row, f32[8,128]{1,0:T(8,128)} %get-tuple-element.52.sums_a, f32[8,128]{1,0:T(8,128)} %copy-done.26), custom_call_target="tpu_custom_call" | custom-call | tf_op jit(solution)/shard_map/pallas_call | solution.py:135
  103.8 11.9 %shard_map.81 = f32[512,2048]{1,0:T(8,128)} custom-call(bf16[512,2432]{1,0:T(8,128)(2,1)} %bitcast.149, bf16[2048,2432]{1,0:T(8,128)(2,1)} %head.5), custom_call_target="tpu_custom_call" | custom-call | tf_op jit(solution)/shard_map/pallas_call | solution.py:196
  120.2 2.6 %collective-permute-start.25 = (f32[3,256]{1,0:T(4,128)S(1)}, f32[3,256]{1,0:T(4,128)S(1)}, u32[]{:S(2)}, u32[]{:S(2)}) collective-permute-start(f32[3,256]{1,0:T(4,128)S(1)} %pad_maximum_fusion.14), channel_id=1, source_target_pairs={{0,4},{1,5},{2,6},{3,7},{4,0},{5,1},{6,2},{7,3},{8,12},{9,13},{10,... | collective-permute-start | bytes 9224 | tf_op jit(solution)/shard_map/ppermute | solution.py:27
  125.4 2.5 %multiply_add_fusion = f32[256,2048]{1,0:T(8,128)S(1)} fusion(f32[512,2048]{1,0:T(8,128)} %shard_map.81, f32[256]{0:T(256)S(1)} %get-tuple-element.108, f32[256]{0:T(256)S(1)} %get-tuple-element.109), kind=kLoop, calls=%fused_computation.7 | loop fusion | flops 1572864 | bytes 6293504 | tf_op jit(solution)/shard_map/add | solution.py:320
  131.5 3.4 %shard_map.82 = (bf16[512,2432]{1,0:T(8,128)(2,1)}, f32[512,128]{1,0:T(8,128)}) custom-call(s32[16]{0:T(128)} %pad_add_fusion.3.at, bf16[128,2432]{1,0:T(8,128)(2,1)} %refs_0_, bf16[128,2432]{1,0:T(8,128)(2,1)} %collective-permute-done.20.refs_1_, bf16[128,2432]{1,0:T(8,128)(2,1)} %collective-permute-done.21.refs_2_, bf16[128,2432]{1,0:T(8,128)(2,1)} %copy-done.6, ...), custom_call_target="tpu_custom_call" | custom-call | tf_op jit(solution)/shard_map/pallas_call | solution.py:167
  136.0 12.0 %shard_map.83 = f32[512,2048]{1,0:T(8,128)} custom-call(bf16[512,2432]{1,0:T(8,128)(2,1)} %get-tuple-element.84.cotangent, bf16[2048,2432]{1,0:T(8,128)(2,1)} %head.5), custom_call_target="tpu_custom_call" | custom-call | tf_op jit(solution)/shard_map/pallas_call | solution.py:196
  148.0 4.1 %fusion.69 = (bf16[256,2048]{1,0:T(8,128)(2,1)S(1)}, f32[256,2048]{1,0:T(8,128)S(1)}, bf16[256,2048]{1,0:T(8,128)(2,1)S(1)}, f32[256,2048]{1,0:T(8,128)S(1)}) fusion(f32[512,2048]{1,0:T(8,128)} %shard_map.83, f32[256]{0:T(256)S(1)} %get-tuple-element.100, f32[512,2048]{1,0:T(8,128)} %shard_map.81, f32[256]{0:T(256)S(1)} %get-tuple-element.109, ...), kind=kLoop, calls=%fused_computation.295 | loop fusion | flops 4194304 | bytes 14684160 | tf_op jit(solution)/shard_map/convert.7
  158.6 9.5 %collective-permute-done.28 = bf16[2,64,2048]{2,1,0:T(8,128)(2,1)S(1)} collective-permute-done((bf16[2,64,2048]{2,1,0:T(8,128)(2,1)S(1)}, bf16[2,64,2048]{2,1,0:T(8,128)(2,1)S(1)}, u32[]{:S(2)}, u32[]{:S(2)}) %collective-permute-start.28) | collective-permute-done | bytes 524320 | tf_op jit(solution)/shard_map/ppermute | solution.py:27
  172.9 9.2 %collective-permute-done.30 = bf16[1,64,2048]{2,1,0:T(8,128)(2,1)S(1)} collective-permute-done((bf16[1,64,2048]{2,1,0:T(8,128)(2,1)S(1)}, bf16[1,64,2048]{2,1,0:T(8,128)(2,1)S(1)}, u32[]{:S(2)}, u32[]{:S(2)}) %collective-permute-start.30) | collective-permute-done | bytes 262176 | tf_op jit(solution)/shard_map/ppermute | solution.py:27
  185.7 5.2 %collective-permute-done.33 = bf16[1,64,1024]{2,1,0:T(8,128)(2,1)S(1)} collective-permute-done((bf16[1,64,1024]{2,1,0:T(8,128)(2,1)S(1)}, bf16[1,64,1024]{2,1,0:T(8,128)(2,1)S(1)}, u32[]{:S(2)}, u32[]{:S(2)}) %collective-permute-start.33) | collective-permute-done | bytes 131104 | tf_op jit(solution)/shard_map/ppermute | solution.py:27
  194.5 5.8 %collective-permute-done.35 = bf16[1,64,1024]{2,1,0:T(8,128)(2,1)S(1)} collective-permute-done((bf16[1,64,1024]{2,1,0:T(8,128)(2,1)S(1)}, bf16[1,64,1024]{2,1,0:T(8,128)(2,1)S(1)}, u32[]{:S(2)}, u32[]{:S(2)}) %collective-permute-start.35) | collective-permute-done | bytes 131104 | tf_op jit(solution)/shard_map/ppermute | solution.py:27
  202.5 3.0 %collective-permute-done.37 = f32[2,64]{1,0:T(2,128)S(1)} collective-permute-done((f32[2,64]{1,0:T(2,128)S(1)}, f32[2,64]{1,0:T(2,128)S(1)}, u32[]{:S(2)}, u32[]{:S(2)}) %collective-permute-start.37) | collective-permute-done | bytes 544 | tf_op jit(solution)/shard_map/ppermute | solution.py:27
  (225 shorter events, 73.9 us)
Async XLA Ops:
  7.1 21.0 %collective-permute-start.3 = (bf16[64,2048]{1,0:T(8,128)(2,1)}, bf16[64,2048]{1,0:T(8,128)(2,1)S(1)}, u32[]{:S(2)}, u32[]{:S(2)}) collective-permute-start(bf16[64,2048]{1,0:T(8,128)(2,1)} %get-tuple-element.56), channel_id=1, source_target_pairs={{0,16},{8,24},{16,0},{24,8},{1,17},{9,25},{17,1},{25,9},{2,18},{10... | collective-permute-start | bytes 786440 | tf_op jit(solution)/shard_map/ppermute | solution.py:27
  9.7 18.5 %collective-permute-start.4 = (bf16[64,2048]{1,0:T(8,128)(2,1)}, bf16[64,2048]{1,0:T(8,128)(2,1)S(1)}, u32[]{:S(2)}, u32[]{:S(2)}) collective-permute-start(bf16[64,2048]{1,0:T(8,128)(2,1)} %get-tuple-element.57), channel_id=1, source_target_pairs={{0,24},{8,16},{16,8},{24,0},{1,25},{9,17},{17,9},{25,1},{2,26},{10... | collective-permute-start | bytes 786440 | tf_op jit(solution)/shard_map/ppermute | solution.py:27
  17.6 7.8 %collective-permute-start.2 = (f32[128,2432]{1,0:T(8,128)S(1)}, f32[128,2432]{1,0:T(8,128)S(1)}, u32[]{:S(2)}, u32[]{:S(2)}) collective-permute-start(f32[128,2432]{1,0:T(8,128)S(1)} %fusion.2), channel_id=1, source_target_pairs={{0,8},{8,0},{16,24},{24,16},{1,9},{9,1},{17,25},{25,17},{2,10},{10... | collective-permute-start | bytes 3735560 | tf_op jit(solution)/shard_map/ppermute | solution.py:27
  22.9 5.3 %collective-permute-start.5 = (f32[2,8,128]{2,1,0:T(8,128)S(1)}, f32[2,8,128]{2,1,0:T(8,128)S(1)}, u32[]{:S(2)}, u32[]{:S(2)}) collective-permute-start(f32[2,8,128]{2,1,0:T(8,128)S(1)} %pad_maximum_fusion.8), channel_id=1, source_target_pairs={{0,16},{8,24},{16,0},{24,8},{1,17},{9,25},{17,1},{25,9},{2,18},{10... | collective-permute-start | bytes 24584 | tf_op jit(solution)/shard_map/ppermute | solution.py:27
  28.3 7.5 %collective-permute-start.9 = (bf16[2,32,2048]{2,1,0:T(8,128)(2,1)S(1)}, bf16[2,32,2048]{2,1,0:T(8,128)(2,1)S(1)}, u32[]{:S(2)}, u32[]{:S(2)}) collective-permute-start(bf16[2,32,2048]{2,1,0:T(8,128)(2,1)S(1)} %pad_maximum_fusion.5), channel_id=1, source_target_pairs={{0,1},{1,0},{2,3},{3,2},{4,5},{5,4},{6,7},{7,6},{8,9},{9,8},{10,11... | collective-permute-start | bytes 786440 | tf_op jit(solution)/shard_map/ppermute | solution.py:27
  30.1 7.1 %collective-permute-start.8 = (bf16[2,32,2048]{2,1,0:T(8,128)(2,1)S(1)}, bf16[2,32,2048]{2,1,0:T(8,128)(2,1)S(1)}, u32[]{:S(2)}, u32[]{:S(2)}) collective-permute-start(bf16[2,32,2048]{2,1,0:T(8,128)(2,1)S(1)} %pad_maximum_fusion.5), channel_id=1, source_target_pairs={{0,2},{1,3},{2,0},{3,1},{4,6},{5,7},{6,4},{7,5},{8,10},{9,11},{10,... | collective-permute-start | bytes 786440 | tf_op jit(solution)/shard_map/ppermute | solution.py:27
  39.0 16.4 %collective-permute-start.11 = (f16[128,2432]{1,0:T(8,128)(2,1)S(1)}, f16[128,2432]{1,0:T(8,128)(2,1)S(1)}, u32[]{:S(2)}, u32[]{:S(2)}) collective-permute-start(f16[128,2432]{1,0:T(8,128)(2,1)S(1)} %get-tuple-element.62), channel_id=1, source_target_pairs={{0,16},{8,24},{16,0},{24,8},{1,17},{9,25},{17,1},{25,9},{2,18},{10... | collective-permute-start | bytes 1867784 | tf_op jit(solution)/shard_map/ppermute | solution.py:27
  55.6 21.5 %collective-permute-start.12 = (f16[128,2432]{1,0:T(8,128)(2,1)}, f16[128,2432]{1,0:T(8,128)(2,1)S(1)}, u32[]{:S(2)}, u32[]{:S(2)}) collective-permute-start(f16[128,2432]{1,0:T(8,128)(2,1)} %get-tuple-element.63), channel_id=1, source_target_pairs={{0,16},{8,24},{16,0},{24,8},{1,17},{9,25},{17,1},{25,9},{2,18},{10... | collective-permute-start | bytes 1867784 | tf_op jit(solution)/shard_map/ppermute | solution.py:27
  84.4 31.4 %collective-permute-start.21 = (bf16[128,2432]{1,0:T(8,128)(2,1)}, bf16[128,2432]{1,0:T(8,128)(2,1)}, u32[]{:S(2)}, u32[]{:S(2)}) collective-permute-start(bf16[128,2432]{1,0:T(8,128)(2,1)} %refs_0_), channel_id=1, source_target_pairs={{0,16},{8,24},{16,0},{24,8},{1,17},{9,25},{17,1},{25,9},{2,18},{10... | collective-permute-start | bytes 1867784 | tf_op jit(solution)/shard_map/ppermute | solution.py:27
  85.8 29.9 %collective-permute-start.20 = (bf16[128,2432]{1,0:T(8,128)(2,1)}, bf16[128,2432]{1,0:T(8,128)(2,1)}, u32[]{:S(2)}, u32[]{:S(2)}) collective-permute-start(bf16[128,2432]{1,0:T(8,128)(2,1)} %refs_0_), channel_id=1, source_target_pairs={{0,8},{8,0},{16,24},{24,16},{1,9},{9,1},{17,25},{25,17},{2,10},{10... | collective-permute-start | bytes 1867784 | tf_op jit(solution)/shard_map/ppermute | solution.py:27
  88.7 7.6 %collective-permute-start.14 = (f32[128,2432]{1,0:T(8,128)S(1)}, f32[128,2432]{1,0:T(8,128)}, u32[]{:S(2)}, u32[]{:S(2)}) collective-permute-start(f32[128,2432]{1,0:T(8,128)S(1)} %convert_add_fusion.first), channel_id=1, source_target_pairs={{0,8},{8,0},{16,24},{24,16},{1,9},{9,1},{17,25},{25,17},{2,10},{10... | collective-permute-start | bytes 3735560 | tf_op jit(solution)/shard_map/ppermute | solution.py:27
  93.1 22.6 %collective-permute-start.19 = (bf16[128,2048]{1,0:T(8,128)(2,1)S(1)}, bf16[128,2048]{1,0:T(8,128)(2,1)S(1)}, u32[]{:S(2)}, u32[]{:S(2)}) collective-permute-start(bf16[128,2048]{1,0:T(8,128)(2,1)S(1)} %slice.440), channel_id=1, source_target_pairs={{0,1},{1,0},{2,3},{3,2},{4,5},{5,4},{6,7},{7,6},{8,9},{9,8},{10,11... | collective-permute-start | bytes 1572872 | tf_op jit(solution)/shard_map/ppermute | solution.py:27
  94.9 20.9 %collective-permute-start.23 = (f32[2,8,128]{2,1,0:T(8,128)S(1)}, f32[2,8,128]{2,1,0:T(8,128)S(1)}, u32[]{:S(2)}, u32[]{:S(2)}) collective-permute-start(f32[2,8,128]{2,1,0:T(8,128)S(1)} %pad_maximum_fusion.9), channel_id=1, source_target_pairs={{0,16},{8,24},{16,0},{24,8},{1,17},{9,25},{17,1},{25,9},{2,18},{10... | collective-permute-start | bytes 24584 | tf_op jit(solution)/shard_map/ppermute | solution.py:27
  101.6 14.1 %collective-permute-start.18 = (f32[3,256]{1,0:T(4,128)S(1)}, f32[3,256]{1,0:T(4,128)S(1)}, u32[]{:S(2)}, u32[]{:S(2)}) collective-permute-start(f32[3,256]{1,0:T(4,128)S(1)} %slice.284), channel_id=1, source_target_pairs={{0,1},{1,0},{2,3},{3,2},{4,5},{5,4},{6,7},{7,6},{8,9},{9,8},{10,11... | collective-permute-start | bytes 9224 | tf_op jit(solution)/shard_map/ppermute | solution.py:27
  123.4 7.3 %collective-permute-start.26 = (bf16[128,2432]{1,0:T(8,128)(2,1)}, bf16[128,2432]{1,0:T(8,128)(2,1)S(1)}, u32[]{:S(2)}, u32[]{:S(2)}) collective-permute-start(bf16[128,2432]{1,0:T(8,128)(2,1)} %collective-permute-done.21.refs_2_), channel_id=1, source_target_pairs={{0,8},{8,0},{16,24},{24,16},{1,9},{9,1},{17,25},{25,17},{2,10},{10... | collective-permute-start | bytes 1867784 | tf_op jit(solution)/shard_map/ppermute | solution.py:27
  130.2 22.1 %collective-permute-start.27 = (bf16[128,2048]{1,0:T(8,128)(2,1)}, bf16[128,2048]{1,0:T(8,128)(2,1)}, u32[]{:S(2)}, u32[]{:S(2)}) collective-permute-start(bf16[128,2048]{1,0:T(8,128)(2,1)} %slice.439), channel_id=1, source_target_pairs={{0,1},{1,0},{2,3},{3,2},{4,5},{5,4},{6,7},{7,6},{8,9},{9,8},{10,11... | collective-permute-start | bytes 1572872 | tf_op jit(solution)/shard_map/ppermute | solution.py:27
  155.3 12.8 %collective-permute-start.28 = (bf16[2,64,2048]{2,1,0:T(8,128)(2,1)S(1)}, bf16[2,64,2048]{2,1,0:T(8,128)(2,1)S(1)}, u32[]{:S(2)}, u32[]{:S(2)}) collective-permute-start(bf16[2,64,2048]{2,1,0:T(8,128)(2,1)S(1)} %fusion.4), channel_id=1, source_target_pairs={{0,2},{1,3},{2,0},{3,1},{4,6},{5,7},{6,4},{7,5},{8,10},{9,11},{10,... | collective-permute-start | bytes 1572872 | tf_op jit(solution)/shard_map/ppermute | solution.py:27
  156.9 12.5 %collective-permute-start.29 = (bf16[256,1024]{1,0:T(8,128)(2,1)S(1)}, bf16[256,1024]{1,0:T(8,128)(2,1)S(1)}, u32[]{:S(2)}, u32[]{:S(2)}) collective-permute-start(bf16[256,1024]{1,0:T(8,128)(2,1)S(1)} %pad_maximum_fusion.3), channel_id=1, source_target_pairs={{0,1},{1,0},{2,3},{3,2},{4,5},{5,4},{6,7},{7,6},{8,9},{9,8},{10,11... | collective-permute-start | bytes 1572872 | tf_op jit(solution)/shard_map/ppermute | solution.py:27
  169.6 12.6 %collective-permute-start.30 = (bf16[1,64,2048]{2,1,0:T(8,128)(2,1)S(1)}, bf16[1,64,2048]{2,1,0:T(8,128)(2,1)S(1)}, u32[]{:S(2)}, u32[]{:S(2)}) collective-permute-start(bf16[1,64,2048]{2,1,0:T(8,128)(2,1)S(1)} %dynamic-slice_convert_fusion), channel_id=1, source_target_pairs={{0,4},{1,5},{2,6},{3,7},{4,0},{5,1},{6,2},{7,3},{8,12},{9,13},{10,... | collective-permute-start | bytes 786440 | tf_op jit(solution)/shard_map/ppermute | solution.py:27
  170.3 12.6 %collective-permute-start.32 = (bf16[256,1024]{1,0:T(8,128)(2,1)S(1)}, bf16[256,1024]{1,0:T(8,128)(2,1)S(1)}, u32[]{:S(2)}, u32[]{:S(2)}) collective-permute-start(bf16[256,1024]{1,0:T(8,128)(2,1)S(1)} %pad_maximum_fusion.4), channel_id=1, source_target_pairs={{0,1},{1,0},{2,3},{3,2},{4,5},{5,4},{6,7},{7,6},{8,9},{9,8},{10,11... | collective-permute-start | bytes 1572872 | tf_op jit(solution)/shard_map/ppermute | solution.py:27
  172.1 10.8 %collective-permute-start.31 = (bf16[2,64,1024]{2,1,0:T(8,128)(2,1)S(1)}, bf16[2,64,1024]{2,1,0:T(8,128)(2,1)S(1)}, u32[]{:S(2)}, u32[]{:S(2)}) collective-permute-start(bf16[2,64,1024]{2,1,0:T(8,128)(2,1)S(1)} %fusion.17), channel_id=1, source_target_pairs={{0,2},{1,3},{2,0},{3,1},{4,6},{5,7},{6,4},{7,5},{8,10},{9,11},{10,... | collective-permute-start | bytes 786440 | tf_op jit(solution)/shard_map/ppermute | solution.py:27
  183.2 9.9 %collective-permute-start.34 = (bf16[2,64,1024]{2,1,0:T(8,128)(2,1)S(1)}, bf16[2,64,1024]{2,1,0:T(8,128)(2,1)S(1)}, u32[]{:S(2)}, u32[]{:S(2)}) collective-permute-start(bf16[2,64,1024]{2,1,0:T(8,128)(2,1)S(1)} %fusion.18), channel_id=1, source_target_pairs={{0,2},{1,3},{2,0},{3,1},{4,6},{5,7},{6,4},{7,5},{8,10},{9,11},{10,... | collective-permute-start | bytes 786440 | tf_op jit(solution)/shard_map/ppermute | solution.py:27
  183.3 7.6 %collective-permute-start.33 = (bf16[1,64,1024]{2,1,0:T(8,128)(2,1)S(1)}, bf16[1,64,1024]{2,1,0:T(8,128)(2,1)S(1)}, u32[]{:S(2)}, u32[]{:S(2)}) collective-permute-start(bf16[1,64,1024]{2,1,0:T(8,128)(2,1)S(1)} %dynamic-slice_convert_fusion.2), channel_id=1, source_target_pairs={{0,4},{1,5},{2,6},{3,7},{4,0},{5,1},{6,2},{7,3},{8,12},{9,13},{10,... | collective-permute-start | bytes 393224 | tf_op jit(solution)/shard_map/ppermute | solution.py:27
  193.2 7.1 %collective-permute-start.35 = (bf16[1,64,1024]{2,1,0:T(8,128)(2,1)S(1)}, bf16[1,64,1024]{2,1,0:T(8,128)(2,1)S(1)}, u32[]{:S(2)}, u32[]{:S(2)}) collective-permute-start(bf16[1,64,1024]{2,1,0:T(8,128)(2,1)S(1)} %dynamic-slice_convert_fusion.1), channel_id=1, source_target_pairs={{0,4},{1,5},{2,6},{3,7},{4,0},{5,1},{6,2},{7,3},{8,12},{9,13},{10,... | collective-permute-start | bytes 393224 | tf_op jit(solution)/shard_map/ppermute | solution.py:27
  (48 other events, 306.1 us)

commit v5 on v4

--- a/solution.py
+++ b/solution.py
@@ -15,6 +15,10 @@
 F32, BF16 = jnp.float32, jnp.bfloat16
 
 
+def params(mebibytes):
+    return pltpu.CompilerParams(vmem_limit_bytes=mebibytes * 1024 * 1024)
+
+
 def whole_spec():
     return pl.BlockSpec(memory_space=pltpu.VMEM)
 
@@ -39,28 +43,21 @@
     return jnp.concatenate([rows8, jnp.zeros((120, 128), F32)], axis=0).T
 
 
-def cut_kernel(width, seq_size, at, hidden, vectors, *outs):
-    own, mate, over_2, over_3, sums, parts, two = outs
-    seq_index, group = at[0], at[1]
+def cut_kernel(width, at, hidden, vectors, *outs):
+    blocks, (sums, parts, two) = outs[:4], outs[4:]
+    seq_index = at[0]
     rows = hidden.shape[0]
     size = rows // QUARTERS
 
-    def quarter(place):
-        return pl.ds(pl.multiple_of((place ^ group) * size, size), size)
-
     def features(bit):
         return pl.ds(pl.multiple_of((seq_index ^ bit) * width, width), width)
 
-    for out, bit in ((over_2, 2), (over_3, 3)):
-        out[0:size, :] = hidden[quarter(0), features(bit)]
-        out[size:, :] = hidden[quarter(3), features(bit)]
+    for bit, block in enumerate(blocks):
+        block[...] = hidden[:, features(bit)]
     steer, tangent = vectors[0:1, :], vectors[1:2, :]
     columns = []
-    for place in range(QUARTERS):
-        spot = pl.ds(place * size, size)
-        own[spot, :] = hidden[quarter(place), features(0)]
-        mate[spot, :] = hidden[quarter(place), features(1)]
-        inputs = hidden[quarter(place), :].astype(F32) + steer
+    for begin in range(0, rows, size):
+        inputs = hidden[begin : begin + size, :].astype(F32) + steer
         columns.append(
             lanes(
                 [
@@ -80,23 +77,23 @@
     ).astype(BF16)
 
 
-def cut(at, hidden, vectors, width, seq_size):
+def cut(at, hidden, vectors, width):
     rows = hidden.shape[0]
-    piece = jax.ShapeDtypeStruct((2 * (rows // QUARTERS), width), BF16)
     block = jax.ShapeDtypeStruct((rows, width), BF16)
     return pl.pallas_call(
-        functools.partial(cut_kernel, width, seq_size),
+        functools.partial(cut_kernel, width),
         in_specs=[smem_spec(), whole_spec(), whole_spec()],
         out_specs=[whole_spec()] * 7,
         out_shape=[
             block,
             block,
-            piece,
-            piece,
+            block,
+            block,
             jax.ShapeDtypeStruct((8, rows), F32),
             jax.ShapeDtypeStruct((vectors.shape[0], width), F32),
             jax.ShapeDtypeStruct((16, width), BF16),
         ],
+        compiler_params=params(12),
         cost_estimate=LIGHT,
     )(at, hidden, vectors)
 
@@ -141,6 +138,7 @@
             jax.ShapeDtypeStruct((8, rows), F32),
         ],
         scratch_shapes=[pltpu.VMEM((rows, 128), F32)],
+        compiler_params=params(16),
         cost_estimate=LIGHT,
     )(at, first, second, row, sums_a, sums_b)
 
@@ -172,6 +170,7 @@
             jax.ShapeDtypeStruct((rows, width), BF16),
             jax.ShapeDtypeStruct((rows, 128), F32),
         ],
+        compiler_params=params(12),
         cost_estimate=LIGHT,
     )(at, *blocks, *totals)
 
@@ -202,6 +201,7 @@
         ],
         out_specs=pl.BlockSpec((rows, tile), lambda i: (0, i)),
         out_shape=jax.ShapeDtypeStruct((rows, features), F32),
+        compiler_params=params(20),
         cost_estimate=LIGHT,
     )(cotangent, head)
 
@@ -216,9 +216,11 @@
 
 
 def exchange(value, size, beside):
-    half = value.shape[1] // 2
     other, beside = lax.optimization_barrier((swap(value, "vocab", 1, size), beside))
-    aligned = jnp.concatenate([other[:3, half:], other[:3, :half]], axis=1)
+    part = value.shape[1] // 4
+    aligned = jnp.concatenate(
+        [other[:3, i * part : (i + 1) * part] for i in (1, 0, 3, 2)], axis=1
+    )
     value = merge(value, jnp.concatenate([aligned, other[3:]], axis=0))
     bit = PAIR
     while bit < size:
@@ -241,7 +243,6 @@
     y, z = vocab_index % PAIR, vocab_index // PAIR
     length = vocab_size // PAIR
     chip = seq_index // 2
-    group = 2 * y + z % 2
 
     def destination(block, begin):
         row = (block % 2) * tokens + begin
@@ -249,20 +250,19 @@
         return ((owner % PAIR) ^ y) * tokens + owner // PAIR * share + inside
 
     starts = jnp.arange(tokens // size) * size
-    turned = ((starts // quarter) ^ group) * quarter + starts % quarter
 
     def places(bits, begins):
         return jnp.concatenate(
             [destination(seq_index ^ bit, begins) for bit in bits]
         ).astype(jnp.int32)
 
-    own_places, other_places = places((0, 1), turned), places((2, 3), turned)
+    own_places, other_places = places((0, 1), starts), places((2, 3), starts)
     target_places = places((0, 1, 2, 3), starts)
 
-    at = jnp.stack([seq_index, group]).astype(jnp.int32)
+    at = seq_index.astype(jnp.int32)[None]
     vectors = jnp.stack([steer, tangent, gain])
     own, mate, over_2, over_3, sums_0, parts, two = cut(
-        at, hidden, vectors, width, seq_size
+        at, hidden, vectors, width
     )
     mate = swap(mate, "seq", 1, seq_size)
     sums_1 = swap(sums_0, "seq", 1, seq_size)
@@ -284,20 +284,12 @@
     tangent_row = row + swap(row, "seq", 2, seq_size)
     summed_0 = partial_logits(own, sums_0) + given
     send_0 = summed_0.astype(jnp.float16)
-    over_2, over_3, both, send_0, tangent_row = lax.optimization_barrier(
-        (over_2, over_3, both, send_0, tangent_row)
-    )
+    both, send_0, tangent_row = lax.optimization_barrier((both, send_0, tangent_row))
     got_2 = swap(send_0, "seq", 2, seq_size)
-    near = jnp.stack([over_2[:quarter], over_3[:quarter]])
-    by_y = swap(near, "vocab", 2, vocab_size)
-    by_z = swap(near, "vocab", 1, vocab_size)
     sums = [sums_0, sums_1, both[0], both[1]]
     denominators = [s[0] / feature_count + EPSILON for s in sums]
 
-    blocks = [own, mate] + [
-        jnp.concatenate([over[:quarter], by_y[i], by_z[i], over[quarter:]], axis=0)
-        for i, over in enumerate((over_2, over_3))
-    ]
+    blocks = [own, mate, over_2, over_3]
     given = swap(partial_logits(blocks[3], sums[3]), "seq", 1, seq_size)
     summed_2 = partial_logits(blocks[2], sums[2]) + given
     send_2, got_2 = lax.optimization_barrier((summed_2.astype(jnp.float16), got_2))
@@ -326,29 +318,22 @@
         (got_0, target, raw_other, stats_other)
     )
     target_2 = swap(target, "seq", 2, seq_size)
+    target_1 = swap(target, "seq", 1, seq_size)
+    both_own, stats_own = soften_of(0, summed_0, got_0, own_places)
     own_total = jnp.sum(target.astype(F32), axis=1)
-    joint_other, raw_other = exchange(
-        jnp.concatenate([stats_other, jnp.concatenate([own_total, own_total])[None]]),
+    stats = jnp.concatenate([stats_own, stats_other], axis=1)
+    joint, (raw_own, target_1, target_2) = exchange(
+        jnp.concatenate([stats, jnp.concatenate([own_total] * seq_size)[None]]),
         vocab_size,
-        raw_other,
-    )
-    plain_other, theirs_other, kept_other = scaled_of(raw_other, stats_other, joint_other)
+        (back(both_own, head), target_1, target_2),
+    )
+    plain_own, theirs_own, kept_own = scaled_of(raw_own, stats_own, joint[:, :half])
+    plain_other, theirs_other, kept_other = scaled_of(raw_other, stats_other, joint[:, half:])
+    got_own = swap(theirs_own, "vocab", 1, vocab_size)
     got_other = swap(theirs_other, "vocab", 1, vocab_size)
-
-    target_1 = swap(target, "seq", 1, seq_size)
-    total_0 = jnp.broadcast_to(joint_other[3, :tokens], (8, tokens))
+    total_0 = jnp.broadcast_to(joint[3, :tokens], (8, tokens))
     total_1 = swap(total_0, "seq", 1, seq_size)
     both_totals = swap(jnp.stack([total_0, total_1]), "seq", 2, seq_size)
-
-    both_own, stats_own = soften_of(0, summed_0, got_0, own_places)
-    stats_own, theirs_other = lax.optimization_barrier((stats_own, theirs_other))
-    joint, (raw_own, got_other, target_1, target_2, both_totals) = exchange(
-        stats_own,
-        vocab_size,
-        (back(both_own, head), got_other, target_1, target_2, both_totals),
-    )
-    plain_own, theirs_own, kept_own = scaled_of(raw_own, stats_own, joint)
-    got_own = swap(theirs_own, "vocab", 1, vocab_size)
 
     target_3 = swap(target_2, "seq", 1, seq_size)
     ordered, columns = order(
@@ -356,7 +341,7 @@
         [target, target_1, target_2, target_3],
         [total_0, total_1, both_totals[0], both_totals[1]],
     )
-    ordered, _ = lax.optimization_barrier((ordered, theirs_own))
+    ordered, _, _ = lax.optimization_barrier((ordered, theirs_own, theirs_other))
     weighed = back(ordered, head)
     inverse = columns[:, 0:1]
     gradients = [
@@ -431,9 +416,8 @@
         pieces = []
         for begin in range(0, share, size):
             inside = first_row % tokens + begin
-            place = ((inside // quarter) ^ group) * quarter + inside % quarter
             pieces.append(
-                choose([lax.dynamic_slice_in_dim(o, place, size, 0) for o in options])
+                choose([lax.dynamic_slice_in_dim(o, inside, size, 0) for o in options])
             )
         return jnp.concatenate(pieces, axis=0)
 

time: 208 us -> 187 us (0.90)
  Pallas kernels: 52.5 us -> 28.4 us
  waiting for transfers between devices: 67.3 us -> 79.4 us
  other arithmetic: 22.9 us -> 12.3 us
  local copies, waits for them, and re-layouts: 11.5 us -> 19.3 us
  starting transfers between devices: 37.2 us -> 31.7 us
    pallas_call x3, Pallas kernels: 36 us -> 21.5 us  [back(): pl.pallas_call(functools.partial(back_kernel, deep), grid=(features // ti...]
    ppermute x38 -> x33, waiting for transfers between devices: 67.3 us -> 79.4 us  [swap(): return lax.ppermute(value, axis, [(i, i ^ bit) for i in range(size)])]
    unnamed x68 -> x42, local copies, waits for them, and re-layouts: 5.43 us -> 17.1 us
    ppermute x38 -> x33, starting transfers between devices: 37.2 us -> 31.7 us  [swap(): return lax.ppermute(value, axis, [(i, i ^ bit) for i in range(size)])]
    pallas_call x2, Pallas kernels: 9.3 us -> 4.41 us  [soften(): pl.pallas_call(functools.partial(soften_kernel, feature_count), in_specs=...]
    another operation x3 -> x1, other arithmetic: 4.79 us -> 0.63 us
    pallas_call x1, Pallas kernels: 3.8 us -> 1.08 us  [cut(): pl.pallas_call(functools.partial(cut_kernel, width), in_specs=[smem_spec(...]
  transfers between devices with their start and end apart: 38 -> 33, of which waited for: 22 -> 18; matrix products, arithmetic and copies ran while one was open for 16% -> 10% of each run, Pallas kernels for 24% -> 15%
where the time goes in v5:
time: 187 us; the launch traced here: 186 us
  waiting for transfers between devices  79.4 us (42%)
  starting transfers between devices  31.7 us (17%)
  Pallas kernels  28.4 us (15%)
  local copies, waits for them, and re-layouts  19.3 us (10%)
  matrix products  13.8 us (7%)
  other arithmetic  12.3 us (7%)
    ppermute x33, waiting for transfers between devices, swap(): return lax.ppermute(value, axis, [(i, i ^ bit) for i in range(size)])  79.4 us
    ppermute x33, starting transfers between devices, swap(): return lax.ppermute(value, axis, [(i, i ^ bit) for i in range(size)])  31.7 us
    pallas_call x3, Pallas kernels, back(): pl.pallas_call(functools.partial(back_kernel, deep), grid=(features // ti...  21.5 us
    unnamed x42, local copies, waits for them, and re-layouts  17.1 us
    dot_general x4, matrix products, partial_logits(): return jnp.dot(normed, head, preferred_element_type=F32)  12.3 us
    pallas_call x2, Pallas kernels, soften(): pl.pallas_call(functools.partial(soften_kernel, feature_count), in_specs=...  4.41 us
  transfers between devices with their start and end apart: 33, of which 18 were waited for; matrix products, arithmetic and copies ran while one was open for 10% of the time, Pallas kernels for 15%

profile of v5, /device:TPU:0, one launch (start us, length us, event | category | flops | bytes accessed | tf_op | source)
XLA Modules:
  0.0 186.3 jit_solution(1215988627589677945)
XLA Ops:
  4.8 2.6 %collective-permute-start.7 = (bf16[128,2048]{1,0:T(8,128)(2,1)S(1)}, bf16[128,2048]{1,0:T(8,128)(2,1)S(1)}, u32[]{:S(2)}, u32[]{:S(2)}) collective-permute-start(bf16[128,2048]{1,0:T(8,128)(2,1)S(1)} %get-tuple-element.52), channel_id=1, source_target_pairs={{0,24},{8,16},{16,8},{24,0},{1,25},{9,17},{17,9},{25,1},{2,26},{10... | collective-permute-start | bytes 1572872 | tf_op jit(solution)/shard_map/ppermute | solution.py:31
  7.5 5.6 %fusion.2 = f32[128,2432]{1,0:T(8,128)S(1)} fusion(bf16[2048,2432]{1,0:T(8,128)(2,1)} %head.5, bf16[128,2048]{1,0:T(8,128)(2,1)S(1)} %collective-permute-done, f32[128]{0:T(128)S(1)} %get-tuple-element.142, f32[2048]{0:T(1024)S(1)} %bitcast.127, f32[2048]{0:T(1024)S(1)} %bitcast.121), kind=kOutput, calls=%fused_computation.25 | convolution fusion | flops 1276379136 | bytes 11747840 | tf_op jit(solution)/shard_map/dot_general | solution.py:277
  20.1 2.7 %fusion.69 = (f16[128,2432]{1,0:T(8,128)(2,1)S(1)}, f32[128,2432]{1,0:T(8,128)}) fusion(f32[128,2432]{1,0:T(8,128)S(1)} %collective-permute-done.2, bf16[2048,2432]{1,0:T(8,128)(2,1)S(1)} %bitcast.109, bf16[128,2048]{1,0:T(8,128)(2,1)S(1)} %get-tuple-element.44, f32[128]{0:T(128)S(1)} %get-tuple-element.140, f32[2048]{0:T(1024)S(1)} %bitcast.128, ...), kind=kOutput, calls=%fused_computation.218 | convolution fusion | flops 1277001728 | bytes 13615616 | tf_op jit(solution)/shard_map/dot_general | solution.py:277
  24.5 2.2 %collective-permute-start.3 = (bf16[128,2048]{1,0:T(8,128)(2,1)S(1)}, bf16[128,2048]{1,0:T(8,128)(2,1)S(1)}, u32[]{:S(2)}, u32[]{:S(2)}) collective-permute-start(bf16[128,2048]{1,0:T(8,128)(2,1)S(1)} %get-tuple-element.49), channel_id=1, source_target_pairs={{0,16},{8,24},{16,0},{24,8},{1,17},{9,25},{17,1},{25,9},{2,18},{10... | collective-permute-start | bytes 1572872 | tf_op jit(solution)/shard_map/ppermute | solution.py:31
  26.8 12.7 %collective-permute-done.3 = bf16[128,2048]{1,0:T(8,128)(2,1)S(1)} collective-permute-done((bf16[128,2048]{1,0:T(8,128)(2,1)S(1)}, bf16[128,2048]{1,0:T(8,128)(2,1)S(1)}, u32[]{:S(2)}, u32[]{:S(2)}) %collective-permute-start.3) | collective-permute-done | bytes 524320 | tf_op jit(solution)/shard_map/ppermute | solution.py:31
  39.5 2.4 %fusion.70 = (f16[128,2432]{1,0:T(8,128)(2,1)}, f32[128,2432]{1,0:T(8,128)S(1)}) fusion(f32[128,2432]{1,0:T(8,128)S(1)} %collective-permute-done.8, bf16[2048,2432]{1,0:T(8,128)(2,1)S(1)} %bitcast.109, bf16[128,2048]{1,0:T(8,128)(2,1)S(1)} %collective-permute-done.3, f32[128]{0:T(128)S(1)} %get-tuple-element.123, f32[2048]{0:T(1024)S(1)} %bitcast.130, ...), kind=kOutput, calls=%fused_computation.219 | convolution fusion | flops 1277001728 | bytes 13615616 | tf_op jit(solution)/shard_map/dot_general | solution.py:277
  42.0 10.6 %collective-permute-done.9 = f16[128,2432]{1,0:T(8,128)(2,1)S(1)} collective-permute-done((f16[128,2432]{1,0:T(8,128)(2,1)S(1)}, f16[128,2432]{1,0:T(8,128)(2,1)S(1)}, u32[]{:S(2)}, u32[]{:S(2)}) %collective-permute-start.9) | collective-permute-done | bytes 622624 | tf_op jit(solution)/shard_map/ppermute | solution.py:31
  55.7 2.2 %shard_map.78 = (bf16[2,256,2432]{2,1,0:T(8,128)(2,1)S(1)}, f32[8,256]{1,0:T(8,128)S(1)}) custom-call(s32[8]{0:T(128)S(1)} %pad_add_fusion.1.at, f32[128,2432]{1,0:T(8,128)S(1)} %convert_add_fusion.1.first, f32[128,2432]{1,0:T(8,128)S(1)} %collective-permute-done.11.second, f32[1,2432]{1,0:T(1,128)S(1)} %add.417.row, ...), custom_call_target="tpu_custom_call" | custom-call | tf_op jit(solution)/shard_map/pallas_call | solution.py:132
  58.0 3.8 %copy-done = bf16[2048,2432]{1,0:T(8,128)(2,1)S(1)} copy-done((bf16[2048,2432]{1,0:T(8,128)(2,1)S(1)}, bf16[2048,2432]{1,0:T(8,128)(2,1)}, u32[]{:S(2)}) %copy-start) | copy-done | bytes 9961496
  61.8 7.2 %shard_map.79 = f32[512,2048]{1,0:T(8,128)S(1)} custom-call(bf16[512,2432]{1,0:T(8,128)(2,1)S(1)} %bitcast.111, bf16[2048,2432]{1,0:T(8,128)(2,1)S(1)} %copy-done), custom_call_target="tpu_custom_call" | custom-call | tf_op jit(solution)/shard_map/pallas_call | solution.py:195
  75.2 2.2 %shard_map.80 = (bf16[2,256,2432]{2,1,0:T(8,128)(2,1)S(1)}, f32[8,256]{1,0:T(8,128)S(1)}) custom-call(s32[8]{0:T(128)S(1)} %pad_add_fusion.at, f32[128,2432]{1,0:T(8,128)S(1)} %convert_add_fusion.first, f32[128,2432]{1,0:T(8,128)S(1)} %collective-permute-done.12.second, f32[1,2432]{1,0:T(1,128)S(1)} %add.417.row, f32[8,128]{1,0:T(8,128)S(1)} %get-tuple-element.45.sums_a, ...), custom_call_target="tpu_custom_call" | custom-call | tf_op jit(solution)/shard_map/pallas_call | solution.py:132
  79.2 3.8 %copy-done.1 = bf16[2048,2432]{1,0:T(8,128)(2,1)S(1)} copy-done((bf16[2048,2432]{1,0:T(8,128)(2,1)S(1)}, bf16[2048,2432]{1,0:T(8,128)(2,1)}, u32[]{:S(2)}) %copy-start.1) | copy-done | bytes 9961496
  83.0 7.1 %shard_map.81 = f32[512,2048]{1,0:T(8,128)S(1)} custom-call(bf16[512,2432]{1,0:T(8,128)(2,1)S(1)} %bitcast.110, bf16[2048,2432]{1,0:T(8,128)(2,1)S(1)} %copy-done.1), custom_call_target="tpu_custom_call" | custom-call | tf_op jit(solution)/shard_map/pallas_call | solution.py:195
  96.1 2.7 %collective-permute-start.17 = (f32[4,512]{1,0:T(4,128)S(1)}, f32[4,512]{1,0:T(4,128)S(1)}, u32[]{:S(2)}, u32[]{:S(2)}) collective-permute-start(f32[4,512]{1,0:T(4,128)S(1)} %pad_maximum_fusion.8), channel_id=1, source_target_pairs={{0,4},{1,5},{2,6},{3,7},{4,0},{5,1},{6,2},{7,3},{8,12},{9,13},{10,... | collective-permute-start | bytes 24584 | tf_op jit(solution)/shard_map/ppermute | solution.py:31
  100.9 2.7 %multiply_add_fusion = f32[256,2048]{1,0:T(8,128)S(1)} fusion(f32[512,2048]{1,0:T(8,128)} %copy-done.3, f32[256]{0:T(256)S(1)} %mul.320, f32[256]{0:T(256)S(1)} %bitcast.140), kind=kLoop, calls=%fused_computation.7 | loop fusion | flops 1572864 | bytes 6293504 | tf_op jit(solution)/shard_map/add | solution.py:312
  109.5 3.8 %copy-done.2 = bf16[2048,2432]{1,0:T(8,128)(2,1)S(1)} copy-done((bf16[2048,2432]{1,0:T(8,128)(2,1)S(1)}, bf16[2048,2432]{1,0:T(8,128)(2,1)}, u32[]{:S(2)}) %copy-start.2) | copy-done | bytes 9961496
  113.4 7.2 %shard_map.83 = f32[512,2048]{1,0:T(8,128)S(1)} custom-call(bf16[512,2432]{1,0:T(8,128)(2,1)S(1)} %get-tuple-element.71.cotangent, bf16[2048,2432]{1,0:T(8,128)(2,1)S(1)} %copy-done.2), custom_call_target="tpu_custom_call" | custom-call | tf_op jit(solution)/shard_map/pallas_call | solution.py:195
  122.2 7.1 %collective-permute-done.21 = bf16[128,2048]{1,0:T(8,128)(2,1)S(1)} collective-permute-done((bf16[128,2048]{1,0:T(8,128)(2,1)S(1)}, bf16[128,2048]{1,0:T(8,128)(2,1)S(1)}, u32[]{:S(2)}, u32[]{:S(2)}) %collective-permute-start.21) | collective-permute-done | bytes 524320 | tf_op jit(solution)/shard_map/ppermute | solution.py:31
  132.2 11.3 %collective-permute-done.23 = bf16[2,64,2048]{2,1,0:T(8,128)(2,1)S(1)} collective-permute-done((bf16[2,64,2048]{2,1,0:T(8,128)(2,1)S(1)}, bf16[2,64,2048]{2,1,0:T(8,128)(2,1)S(1)}, u32[]{:S(2)}, u32[]{:S(2)}) %collective-permute-start.23) | collective-permute-done | bytes 524320 | tf_op jit(solution)/shard_map/ppermute | solution.py:31
  145.6 2.6 %collective-permute-start.25 = (bf16[1,64,2048]{2,1,0:T(8,128)(2,1)}, bf16[1,64,2048]{2,1,0:T(8,128)(2,1)S(1)}, u32[]{:S(2)}, u32[]{:S(2)}) collective-permute-start(bf16[1,64,2048]{2,1,0:T(8,128)(2,1)} %dynamic-slice_convert_fusion), channel_id=1, source_target_pairs={{0,4},{1,5},{2,6},{3,7},{4,0},{5,1},{6,2},{7,3},{8,12},{9,13},{10,... | collective-permute-start | bytes 786440 | tf_op jit(solution)/shard_map/ppermute | solution.py:31
  150.1 9.1 %collective-permute-done.25 = bf16[1,64,2048]{2,1,0:T(8,128)(2,1)S(1)} collective-permute-done((bf16[1,64,2048]{2,1,0:T(8,128)(2,1)}, bf16[1,64,2048]{2,1,0:T(8,128)(2,1)S(1)}, u32[]{:S(2)}, u32[]{:S(2)}) %collective-permute-start.25) | collective-permute-done | bytes 262176 | tf_op jit(solution)/shard_map/ppermute | solution.py:31
  159.2 2.4 %collective-permute-done.26 = bf16[2,64,1024]{2,1,0:T(8,128)(2,1)} collective-permute-done((bf16[2,64,1024]{2,1,0:T(8,128)(2,1)}, bf16[2,64,1024]{2,1,0:T(8,128)(2,1)}, u32[]{:S(2)}, u32[]{:S(2)}) %collective-permute-start.26) | collective-permute-done | bytes 262176 | tf_op jit(solution)/shard_map/ppermute | solution.py:31
  164.9 6.0 %collective-permute-done.28 = bf16[1,64,1024]{2,1,0:T(8,128)(2,1)S(1)} collective-permute-done((bf16[1,64,1024]{2,1,0:T(8,128)(2,1)S(1)}, bf16[1,64,1024]{2,1,0:T(8,128)(2,1)S(1)}, u32[]{:S(2)}, u32[]{:S(2)}) %collective-permute-start.28) | collective-permute-done | bytes 131104 | tf_op jit(solution)/shard_map/ppermute | solution.py:31
  174.4 5.5 %collective-permute-done.30 = bf16[1,64,1024]{2,1,0:T(8,128)(2,1)S(1)} collective-permute-done((bf16[1,64,1024]{2,1,0:T(8,128)(2,1)S(1)}, bf16[1,64,1024]{2,1,0:T(8,128)(2,1)S(1)}, u32[]{:S(2)}, u32[]{:S(2)}) %collective-permute-start.30) | collective-permute-done | bytes 131104 | tf_op jit(solution)/shard_map/ppermute | solution.py:31
  (174 shorter events, 59.4 us)
Async XLA Ops:
  4.8 18.0 %collective-permute-start.7 = (bf16[128,2048]{1,0:T(8,128)(2,1)S(1)}, bf16[128,2048]{1,0:T(8,128)(2,1)S(1)}, u32[]{:S(2)}, u32[]{:S(2)}) collective-permute-start(bf16[128,2048]{1,0:T(8,128)(2,1)S(1)} %get-tuple-element.52), channel_id=1, source_target_pairs={{0,24},{8,16},{16,8},{24,0},{1,25},{9,17},{17,9},{25,1},{2,26},{10... | collective-permute-start | bytes 1572872 | tf_op jit(solution)/shard_map/ppermute | solution.py:31
  13.2 7.0 %collective-permute-start.2 = (f32[128,2432]{1,0:T(8,128)S(1)}, f32[128,2432]{1,0:T(8,128)S(1)}, u32[]{:S(2)}, u32[]{:S(2)}) collective-permute-start(f32[128,2432]{1,0:T(8,128)S(1)} %fusion.2), channel_id=1, source_target_pairs={{0,8},{8,0},{16,24},{24,16},{1,9},{9,1},{17,25},{25,17},{2,10},{10... | collective-permute-start | bytes 3735560 | tf_op jit(solution)/shard_map/ppermute | solution.py:31
  16.4 3.7 %collective-permute-start.6 = (f32[1,2432]{1,0:T(1,128)S(1)}, f32[1,2432]{1,0:T(1,128)S(1)}, u32[]{:S(2)}, u32[]{:S(2)}) collective-permute-start(f32[1,2432]{1,0:T(1,128)S(1)} %reshape_add_fusion), channel_id=1, source_target_pairs={{0,16},{8,24},{16,0},{24,8},{1,17},{9,25},{17,1},{25,9},{2,18},{10... | collective-permute-start | bytes 29192 | tf_op jit(solution)/shard_map/ppermute | solution.py:31
  18.2 4.6 %collective-permute-start.4 = (f32[2,8,128]{2,1,0:T(8,128)S(1)}, f32[2,8,128]{2,1,0:T(8,128)S(1)}, u32[]{:S(2)}, u32[]{:S(2)}) collective-permute-start(f32[2,8,128]{2,1,0:T(8,128)S(1)} %pad_maximum_fusion.5), channel_id=1, source_target_pairs={{0,16},{8,24},{16,0},{24,8},{1,17},{9,25},{17,1},{25,9},{2,18},{10... | collective-permute-start | bytes 24584 | tf_op jit(solution)/shard_map/ppermute | solution.py:31
  24.5 15.1 %collective-permute-start.8 = (f32[128,2432]{1,0:T(8,128)S(1)}, f32[128,2432]{1,0:T(8,128)S(1)}, u32[]{:S(2)}, u32[]{:S(2)}) collective-permute-start(f32[128,2432]{1,0:T(8,128)S(1)} %fusion.3), channel_id=1, source_target_pairs={{0,8},{8,0},{16,24},{24,16},{1,9},{9,1},{17,25},{25,17},{2,10},{10... | collective-permute-start | bytes 3735560 | tf_op jit(solution)/shard_map/ppermute | solution.py:31
  24.5 15.0 %collective-permute-start.3 = (bf16[128,2048]{1,0:T(8,128)(2,1)S(1)}, bf16[128,2048]{1,0:T(8,128)(2,1)S(1)}, u32[]{:S(2)}, u32[]{:S(2)}) collective-permute-start(bf16[128,2048]{1,0:T(8,128)(2,1)S(1)} %get-tuple-element.49), channel_id=1, source_target_pairs={{0,16},{8,24},{16,0},{24,8},{1,17},{9,25},{17,1},{25,9},{2,18},{10... | collective-permute-start | bytes 1572872 | tf_op jit(solution)/shard_map/ppermute | solution.py:31
  26.7 25.9 %collective-permute-start.9 = (f16[128,2432]{1,0:T(8,128)(2,1)S(1)}, f16[128,2432]{1,0:T(8,128)(2,1)S(1)}, u32[]{:S(2)}, u32[]{:S(2)}) collective-permute-start(f16[128,2432]{1,0:T(8,128)(2,1)S(1)} %get-tuple-element.53), channel_id=1, source_target_pairs={{0,16},{8,24},{16,0},{24,8},{1,17},{9,25},{17,1},{25,9},{2,18},{10... | collective-permute-start | bytes 1867784 | tf_op jit(solution)/shard_map/ppermute | solution.py:31
  52.8 18.1 %collective-permute-start.10 = (f16[128,2432]{1,0:T(8,128)(2,1)}, f16[128,2432]{1,0:T(8,128)(2,1)}, u32[]{:S(2)}, u32[]{:S(2)}) collective-permute-start(f16[128,2432]{1,0:T(8,128)(2,1)} %get-tuple-element.54), channel_id=1, source_target_pairs={{0,16},{8,24},{16,0},{24,8},{1,17},{9,25},{17,1},{25,9},{2,18},{10... | collective-permute-start | bytes 1867784 | tf_op jit(solution)/shard_map/ppermute | solution.py:31
  72.4 19.8 %collective-permute-start.15 = (bf16[128,2432]{1,0:T(8,128)(2,1)S(1)}, bf16[128,2432]{1,0:T(8,128)(2,1)}, u32[]{:S(2)}, u32[]{:S(2)}) collective-permute-start(bf16[128,2432]{1,0:T(8,128)(2,1)S(1)} %copy-done.7), channel_id=1, source_target_pairs={{0,16},{8,24},{16,0},{24,8},{1,17},{9,25},{17,1},{25,9},{2,18},{10... | collective-permute-start | bytes 1867784 | tf_op jit(solution)/shard_map/ppermute | solution.py:31
  74.2 18.0 %collective-permute-start.14 = (bf16[128,2432]{1,0:T(8,128)(2,1)S(1)}, bf16[128,2432]{1,0:T(8,128)(2,1)}, u32[]{:S(2)}, u32[]{:S(2)}) collective-permute-start(bf16[128,2432]{1,0:T(8,128)(2,1)S(1)} %copy-done.7), channel_id=1, source_target_pairs={{0,8},{8,0},{16,24},{24,16},{1,9},{9,1},{17,25},{25,17},{2,10},{10... | collective-permute-start | bytes 1867784 | tf_op jit(solution)/shard_map/ppermute | solution.py:31
  77.5 14.8 %collective-permute-start.13 = (f32[4,512]{1,0:T(4,128)S(1)}, f32[4,512]{1,0:T(4,128)S(1)}, u32[]{:S(2)}, u32[]{:S(2)}) collective-permute-start(f32[4,512]{1,0:T(4,128)S(1)} %pad_maximum_fusion.6), channel_id=1, source_target_pairs={{0,1},{1,0},{2,3},{3,2},{4,5},{5,4},{6,7},{7,6},{8,9},{9,8},{10,11... | collective-permute-start | bytes 24584 | tf_op jit(solution)/shard_map/ppermute | solution.py:31
  96.1 4.6 %collective-permute-start.17 = (f32[4,512]{1,0:T(4,128)S(1)}, f32[4,512]{1,0:T(4,128)S(1)}, u32[]{:S(2)}, u32[]{:S(2)}) collective-permute-start(f32[4,512]{1,0:T(4,128)S(1)} %pad_maximum_fusion.8), channel_id=1, source_target_pairs={{0,4},{1,5},{2,6},{3,7},{4,0},{5,1},{6,2},{7,3},{8,12},{9,13},{10,... | collective-permute-start | bytes 24584 | tf_op jit(solution)/shard_map/ppermute | solution.py:31
  98.9 9.0 %collective-permute-start.18 = (bf16[128,2432]{1,0:T(8,128)(2,1)}, bf16[128,2432]{1,0:T(8,128)(2,1)S(1)}, u32[]{:S(2)}, u32[]{:S(2)}) collective-permute-start(bf16[128,2432]{1,0:T(8,128)(2,1)} %collective-permute-done.15.refs_2_), channel_id=1, source_target_pairs={{0,8},{8,0},{16,24},{24,16},{1,9},{9,1},{17,25},{25,17},{2,10},{10... | collective-permute-start | bytes 1867784 | tf_op jit(solution)/shard_map/ppermute | solution.py:31
  103.7 18.5 %collective-permute-start.22 = (bf16[128,2048]{1,0:T(8,128)(2,1)S(1)}, bf16[128,2048]{1,0:T(8,128)(2,1)S(1)}, u32[]{:S(2)}, u32[]{:S(2)}) collective-permute-start(bf16[128,2048]{1,0:T(8,128)(2,1)S(1)} %slice.415), channel_id=1, source_target_pairs={{0,1},{1,0},{2,3},{3,2},{4,5},{5,4},{6,7},{7,6},{8,9},{9,8},{10,11... | collective-permute-start | bytes 1572872 | tf_op jit(solution)/shard_map/ppermute | solution.py:31
  104.1 3.8 %collective-permute-start.20 = (f32[2,8,128]{2,1,0:T(8,128)S(1)}, f32[2,8,128]{2,1,0:T(8,128)S(1)}, u32[]{:S(2)}, u32[]{:S(2)}) collective-permute-start(f32[2,8,128]{2,1,0:T(8,128)S(1)} %pad_maximum_fusion.9), channel_id=1, source_target_pairs={{0,16},{8,24},{16,0},{24,8},{1,17},{9,25},{17,1},{25,9},{2,18},{10... | collective-permute-start | bytes 24584 | tf_op jit(solution)/shard_map/ppermute | solution.py:31
  106.3 23.0 %collective-permute-start.21 = (bf16[128,2048]{1,0:T(8,128)(2,1)S(1)}, bf16[128,2048]{1,0:T(8,128)(2,1)S(1)}, u32[]{:S(2)}, u32[]{:S(2)}) collective-permute-start(bf16[128,2048]{1,0:T(8,128)(2,1)S(1)} %slice.416), channel_id=1, source_target_pairs={{0,1},{1,0},{2,3},{3,2},{4,5},{5,4},{6,7},{7,6},{8,9},{9,8},{10,11... | collective-permute-start | bytes 1572872 | tf_op jit(solution)/shard_map/ppermute | solution.py:31
  129.9 13.6 %collective-permute-start.23 = (bf16[2,64,2048]{2,1,0:T(8,128)(2,1)S(1)}, bf16[2,64,2048]{2,1,0:T(8,128)(2,1)S(1)}, u32[]{:S(2)}, u32[]{:S(2)}) collective-permute-start(bf16[2,64,2048]{2,1,0:T(8,128)(2,1)S(1)} %fusion.4), channel_id=1, source_target_pairs={{0,2},{1,3},{2,0},{3,1},{4,6},{5,7},{6,4},{7,5},{8,10},{9,11},{10,... | collective-permute-start | bytes 1572872 | tf_op jit(solution)/shard_map/ppermute | solution.py:31
  131.5 13.3 %collective-permute-start.24 = (bf16[256,1024]{1,0:T(8,128)(2,1)S(1)}, bf16[256,1024]{1,0:T(8,128)(2,1)S(1)}, u32[]{:S(2)}, u32[]{:S(2)}) collective-permute-start(bf16[256,1024]{1,0:T(8,128)(2,1)S(1)} %pad_maximum_fusion.1), channel_id=1, source_target_pairs={{0,1},{1,0},{2,3},{3,2},{4,5},{5,4},{6,7},{7,6},{8,9},{9,8},{10,11... | collective-permute-start | bytes 1572872 | tf_op jit(solution)/shard_map/ppermute | solution.py:31
  145.6 13.6 %collective-permute-start.25 = (bf16[1,64,2048]{2,1,0:T(8,128)(2,1)}, bf16[1,64,2048]{2,1,0:T(8,128)(2,1)S(1)}, u32[]{:S(2)}, u32[]{:S(2)}) collective-permute-start(bf16[1,64,2048]{2,1,0:T(8,128)(2,1)} %dynamic-slice_convert_fusion), channel_id=1, source_target_pairs={{0,4},{1,5},{2,6},{3,7},{4,0},{5,1},{6,2},{7,3},{8,12},{9,13},{10,... | collective-permute-start | bytes 786440 | tf_op jit(solution)/shard_map/ppermute | solution.py:31
  148.2 13.4 %collective-permute-start.27 = (bf16[256,1024]{1,0:T(8,128)(2,1)}, bf16[256,1024]{1,0:T(8,128)(2,1)}, u32[]{:S(2)}, u32[]{:S(2)}) collective-permute-start(bf16[256,1024]{1,0:T(8,128)(2,1)} %pad_maximum_fusion.2), channel_id=1, source_target_pairs={{0,1},{1,0},{2,3},{3,2},{4,5},{5,4},{6,7},{7,6},{8,9},{9,8},{10,11... | collective-permute-start | bytes 1572872 | tf_op jit(solution)/shard_map/ppermute | solution.py:31
  149.6 12.0 %collective-permute-start.26 = (bf16[2,64,1024]{2,1,0:T(8,128)(2,1)}, bf16[2,64,1024]{2,1,0:T(8,128)(2,1)}, u32[]{:S(2)}, u32[]{:S(2)}) collective-permute-start(bf16[2,64,1024]{2,1,0:T(8,128)(2,1)} %fusion.17), channel_id=1, source_target_pairs={{0,2},{1,3},{2,0},{3,1},{4,6},{5,7},{6,4},{7,5},{8,10},{9,11},{10,... | collective-permute-start | bytes 786440 | tf_op jit(solution)/shard_map/ppermute | solution.py:31
  163.9 9.2 %collective-permute-start.29 = (bf16[2,64,1024]{2,1,0:T(8,128)(2,1)S(1)}, bf16[2,64,1024]{2,1,0:T(8,128)(2,1)S(1)}, u32[]{:S(2)}, u32[]{:S(2)}) collective-permute-start(bf16[2,64,1024]{2,1,0:T(8,128)(2,1)S(1)} %fusion.18), channel_id=1, source_target_pairs={{0,2},{1,3},{2,0},{3,1},{4,6},{5,7},{6,4},{7,5},{8,10},{9,11},{10,... | collective-permute-start | bytes 786440 | tf_op jit(solution)/shard_map/ppermute | solution.py:31
  164.0 6.8 %collective-permute-start.28 = (bf16[1,64,1024]{2,1,0:T(8,128)(2,1)S(1)}, bf16[1,64,1024]{2,1,0:T(8,128)(2,1)S(1)}, u32[]{:S(2)}, u32[]{:S(2)}) collective-permute-start(bf16[1,64,1024]{2,1,0:T(8,128)(2,1)S(1)} %dynamic-slice_convert_fusion.2), channel_id=1, source_target_pairs={{0,4},{1,5},{2,6},{3,7},{4,0},{5,1},{6,2},{7,3},{8,12},{9,13},{10,... | collective-permute-start | bytes 393224 | tf_op jit(solution)/shard_map/ppermute | solution.py:31
  173.1 6.7 %collective-permute-start.30 = (bf16[1,64,1024]{2,1,0:T(8,128)(2,1)S(1)}, bf16[1,64,1024]{2,1,0:T(8,128)(2,1)S(1)}, u32[]{:S(2)}, u32[]{:S(2)}) collective-permute-start(bf16[1,64,1024]{2,1,0:T(8,128)(2,1)S(1)} %dynamic-slice_convert_fusion.1), channel_id=1, source_target_pairs={{0,4},{1,5},{2,6},{3,7},{4,0},{5,1},{6,2},{7,3},{8,12},{9,13},{10,... | collective-permute-start | bytes 393224 | tf_op jit(solution)/shard_map/ppermute | solution.py:31
  (30 other events, 172.1 us)

commit v6 on v5

--- a/solution.py
+++ b/solution.py
@@ -44,7 +44,7 @@
 
 
 def cut_kernel(width, at, hidden, vectors, *outs):
-    blocks, (sums, parts, two) = outs[:4], outs[4:]
+    own, mate, over, sums, parts, two = outs
     seq_index = at[0]
     rows = hidden.shape[0]
     size = rows // QUARTERS
@@ -52,8 +52,10 @@
     def features(bit):
         return pl.ds(pl.multiple_of((seq_index ^ bit) * width, width), width)
 
-    for bit, block in enumerate(blocks):
-        block[...] = hidden[:, features(bit)]
+    own[...] = hidden[:, features(0)]
+    mate[...] = hidden[:, features(1)]
+    over[0] = hidden[:, features(2)]
+    over[1] = hidden[:, features(3)]
     steer, tangent = vectors[0:1, :], vectors[1:2, :]
     columns = []
     for begin in range(0, rows, size):
@@ -83,12 +85,11 @@
     return pl.pallas_call(
         functools.partial(cut_kernel, width),
         in_specs=[smem_spec(), whole_spec(), whole_spec()],
-        out_specs=[whole_spec()] * 7,
+        out_specs=[whole_spec()] * 6,
         out_shape=[
             block,
             block,
-            block,
-            block,
+            jax.ShapeDtypeStruct((2, rows, width), BF16),
             jax.ShapeDtypeStruct((8, rows), F32),
             jax.ShapeDtypeStruct((vectors.shape[0], width), F32),
             jax.ShapeDtypeStruct((16, width), BF16),
@@ -261,12 +262,13 @@
 
     at = seq_index.astype(jnp.int32)[None]
     vectors = jnp.stack([steer, tangent, gain])
-    own, mate, over_2, over_3, sums_0, parts, two = cut(
+    own, mate, over, sums_0, parts, two = cut(
         at, hidden, vectors, width
     )
     mate = swap(mate, "seq", 1, seq_size)
     sums_1 = swap(sums_0, "seq", 1, seq_size)
-    over_2, over_3 = swap(over_2, "seq", 2, seq_size), swap(over_3, "seq", 3, seq_size)
+    over = swap(over, "seq", 2, seq_size)
+    over_2, over_3 = over[0], swap(over[1], "seq", 1, seq_size)
     both = swap(jnp.stack([sums_0, sums_1]), "seq", 2, seq_size)
     steer_part, gain_part = parts[0], parts[2]
 

time: 187 us -> 187 us (level)
    unnamed x42 -> x40, local copies, waits for them, and re-layouts: 17.1 us -> 17.1 us
  transfers between devices with their start and end apart: 33 -> 33, of which waited for: 18 -> 18; matrix products, arithmetic and copies ran while one was open for 10% -> 11% of each run, Pallas kernels for 15% -> 15%
where the time goes in v6:
time: 187 us
  waiting for transfers between devices  79.2 us (42%)
  starting transfers between devices  31.8 us (17%)
  Pallas kernels  28.4 us (15%)
  local copies, waits for them, and re-layouts  20.2 us (11%)
  matrix products  13.7 us (7%)
  other arithmetic  12.3 us (7%)
    ppermute x33, waiting for transfers between devices, swap(): return lax.ppermute(value, axis, [(i, i ^ bit) for i in range(size)])  79.2 us
    ppermute x33, starting transfers between devices, swap(): return lax.ppermute(value, axis, [(i, i ^ bit) for i in range(size)])  31.8 us
    pallas_call x3, Pallas kernels, back(): pl.pallas_call(functools.partial(back_kernel, deep), grid=(features // ti...  21.5 us
    unnamed x40, local copies, waits for them, and re-layouts  17.1 us
    dot_general x4, matrix products, partial_logits(): return jnp.dot(normed, head, preferred_element_type=F32)  12.3 us
    pallas_call x2, Pallas kernels, soften(): pl.pallas_call(functools.partial(soften_kernel, feature_count), in_specs=...  4.41 us
  transfers between devices with their start and end apart: 33, of which 18 were waited for; matrix products, arithmetic and copies ran while one was open for 11% of the time, Pallas kernels for 15%

profile of v6, /device:TPU:0, one launch (start us, length us, event | category | flops | bytes accessed | tf_op | source)
XLA Modules:
  0.0 187.0 jit_solution(6155840177368218319)
XLA Ops:
  4.8 2.9 %collective-permute-start.3 = (bf16[2,128,2048]{2,1,0:T(8,128)(2,1)S(1)}, bf16[2,128,2048]{2,1,0:T(8,128)(2,1)S(1)}, u32[]{:S(2)}, u32[]{:S(2)}) collective-permute-start(bf16[2,128,2048]{2,1,0:T(8,128)(2,1)S(1)} %get-tuple-element.48), channel_id=1, source_target_pairs={{0,16},{8,24},{16,0},{24,8},{1,17},{9,25},{17,1},{25,9},{2,18},{10... | collective-permute-start | bytes 3145736 | tf_op jit(solution)/shard_map/ppermute | solution.py:31
  7.8 5.6 %fusion.5 = f32[128,2432]{1,0:T(8,128)S(1)} fusion(bf16[2048,2432]{1,0:T(8,128)(2,1)} %head.5, bf16[128,2048]{1,0:T(8,128)(2,1)S(1)} %collective-permute-done, f32[128]{0:T(128)S(1)} %get-tuple-element.142, f32[2048]{0:T(1024)S(1)} %bitcast.145, f32[2048]{0:T(1024)S(1)} %bitcast.139), kind=kOutput, calls=%fused_computation.28 | convolution fusion | flops 1276379136 | bytes 11747840 | tf_op jit(solution)/shard_map/dot_general | solution.py:279
  18.3 13.1 %collective-permute-done.6 = f32[1,2432]{1,0:T(1,128)S(1)} collective-permute-done((f32[1,2432]{1,0:T(1,128)S(1)}, f32[1,2432]{1,0:T(1,128)S(1)}, u32[]{:S(2)}, u32[]{:S(2)}) %collective-permute-start.6) | collective-permute-done | bytes 9760 | tf_op jit(solution)/shard_map/ppermute | solution.py:31
  32.3 2.7 %fusion.78 = (f16[128,2432]{1,0:T(8,128)(2,1)S(1)}, f32[128,2432]{1,0:T(8,128)}) fusion(f32[128,2432]{1,0:T(8,128)S(1)} %collective-permute-done.2, bf16[2048,2432]{1,0:T(8,128)(2,1)S(1)} %bitcast.127, bf16[128,2048]{1,0:T(8,128)(2,1)S(1)} %get-tuple-element.43, f32[128]{0:T(128)S(1)} %get-tuple-element.140, f32[2048]{0:T(1024)S(1)} %bitcast.146, ...), kind=kOutput, calls=%fused_computation.227 | convolution fusion | flops 1277001728 | bytes 13615616 | tf_op jit(solution)/shard_map/dot_general | solution.py:279
  39.8 2.4 %fusion.79 = (f16[128,2432]{1,0:T(8,128)(2,1)}, f32[128,2432]{1,0:T(8,128)S(1)}) fusion(f32[128,2432]{1,0:T(8,128)S(1)} %collective-permute-done.8, bf16[2048,2432]{1,0:T(8,128)(2,1)S(1)} %bitcast.127, f32[128]{0:T(128)S(1)} %get-tuple-element.123, f32[2048]{0:T(1024)S(1)} %bitcast.148, f32[2048]{0:T(1024)S(1)} %bitcast.142, ...), kind=kOutput, calls=%fused_computation.228 | convolution fusion | flops 1277001728 | bytes 13615616 | tf_op jit(solution)/shard_map/dot_general | solution.py:279
  42.2 11.0 %collective-permute-done.9 = f16[128,2432]{1,0:T(8,128)(2,1)S(1)} collective-permute-done((f16[128,2432]{1,0:T(8,128)(2,1)S(1)}, f16[128,2432]{1,0:T(8,128)(2,1)S(1)}, u32[]{:S(2)}, u32[]{:S(2)}) %collective-permute-start.9) | collective-permute-done | bytes 622624 | tf_op jit(solution)/shard_map/ppermute | solution.py:31
  56.4 2.2 %shard_map.78 = (bf16[2,256,2432]{2,1,0:T(8,128)(2,1)S(1)}, f32[8,256]{1,0:T(8,128)S(1)}) custom-call(s32[8]{0:T(128)S(1)} %pad_add_fusion.1.at, f32[128,2432]{1,0:T(8,128)S(1)} %convert_add_fusion.1.first, f32[128,2432]{1,0:T(8,128)S(1)} %collective-permute-done.11.second, f32[1,2432]{1,0:T(1,128)S(1)} %add.417.row, ...), custom_call_target="tpu_custom_call" | custom-call | tf_op jit(solution)/shard_map/pallas_call | solution.py:133
  58.6 3.8 %copy-done = bf16[2048,2432]{1,0:T(8,128)(2,1)S(1)} copy-done((bf16[2048,2432]{1,0:T(8,128)(2,1)S(1)}, bf16[2048,2432]{1,0:T(8,128)(2,1)}, u32[]{:S(2)}) %copy-start) | copy-done | bytes 9961496
  62.4 7.1 %shard_map.79 = f32[512,2048]{1,0:T(8,128)S(1)} custom-call(bf16[512,2432]{1,0:T(8,128)(2,1)S(1)} %bitcast.129, bf16[2048,2432]{1,0:T(8,128)(2,1)S(1)} %copy-done), custom_call_target="tpu_custom_call" | custom-call | tf_op jit(solution)/shard_map/pallas_call | solution.py:196
  75.9 2.2 %shard_map.80 = (bf16[2,256,2432]{2,1,0:T(8,128)(2,1)S(1)}, f32[8,256]{1,0:T(8,128)S(1)}) custom-call(s32[8]{0:T(128)S(1)} %pad_add_fusion.at, f32[128,2432]{1,0:T(8,128)S(1)} %convert_add_fusion.first, f32[128,2432]{1,0:T(8,128)S(1)} %collective-permute-done.12.second, f32[1,2432]{1,0:T(1,128)S(1)} %add.417.row, f32[8,128]{1,0:T(8,128)S(1)} %get-tuple-element.44.sums_a, ...), custom_call_target="tpu_custom_call" | custom-call | tf_op jit(solution)/shard_map/pallas_call | solution.py:133
  79.9 3.8 %copy-done.1 = bf16[2048,2432]{1,0:T(8,128)(2,1)S(1)} copy-done((bf16[2048,2432]{1,0:T(8,128)(2,1)S(1)}, bf16[2048,2432]{1,0:T(8,128)(2,1)}, u32[]{:S(2)}) %copy-start.1) | copy-done | bytes 9961496
  83.8 7.1 %shard_map.81 = f32[512,2048]{1,0:T(8,128)S(1)} custom-call(bf16[512,2432]{1,0:T(8,128)(2,1)S(1)} %bitcast.128, bf16[2048,2432]{1,0:T(8,128)(2,1)S(1)} %copy-done.1), custom_call_target="tpu_custom_call" | custom-call | tf_op jit(solution)/shard_map/pallas_call | solution.py:196
  96.8 2.7 %collective-permute-start.17 = (f32[4,512]{1,0:T(4,128)S(1)}, f32[4,512]{1,0:T(4,128)S(1)}, u32[]{:S(2)}, u32[]{:S(2)}) collective-permute-start(f32[4,512]{1,0:T(4,128)S(1)} %pad_maximum_fusion.8), channel_id=1, source_target_pairs={{0,4},{1,5},{2,6},{3,7},{4,0},{5,1},{6,2},{7,3},{8,12},{9,13},{10,... | collective-permute-start | bytes 24584 | tf_op jit(solution)/shard_map/ppermute | solution.py:31
  101.7 2.7 %multiply_add_fusion = f32[256,2048]{1,0:T(8,128)S(1)} fusion(f32[512,2048]{1,0:T(8,128)} %copy-done.3, f32[256]{0:T(256)S(1)} %mul.320, f32[256]{0:T(256)S(1)} %bitcast.158), kind=kLoop, calls=%fused_computation.7 | loop fusion | flops 1572864 | bytes 6293504 | tf_op jit(solution)/shard_map/add | solution.py:314
  110.2 3.8 %copy-done.2 = bf16[2048,2432]{1,0:T(8,128)(2,1)S(1)} copy-done((bf16[2048,2432]{1,0:T(8,128)(2,1)S(1)}, bf16[2048,2432]{1,0:T(8,128)(2,1)}, u32[]{:S(2)}) %copy-start.2) | copy-done | bytes 9961496
  114.0 7.2 %shard_map.83 = f32[512,2048]{1,0:T(8,128)S(1)} custom-call(bf16[512,2432]{1,0:T(8,128)(2,1)S(1)} %get-tuple-element.69.cotangent, bf16[2048,2432]{1,0:T(8,128)(2,1)S(1)} %copy-done.2), custom_call_target="tpu_custom_call" | custom-call | tf_op jit(solution)/shard_map/pallas_call | solution.py:196
  122.8 7.2 %collective-permute-done.21 = bf16[128,2048]{1,0:T(8,128)(2,1)S(1)} collective-permute-done((bf16[128,2048]{1,0:T(8,128)(2,1)S(1)}, bf16[128,2048]{1,0:T(8,128)(2,1)S(1)}, u32[]{:S(2)}, u32[]{:S(2)}) %collective-permute-start.21) | collective-permute-done | bytes 524320 | tf_op jit(solution)/shard_map/ppermute | solution.py:31
  132.9 11.3 %collective-permute-done.23 = bf16[2,64,2048]{2,1,0:T(8,128)(2,1)S(1)} collective-permute-done((bf16[2,64,2048]{2,1,0:T(8,128)(2,1)S(1)}, bf16[2,64,2048]{2,1,0:T(8,128)(2,1)S(1)}, u32[]{:S(2)}, u32[]{:S(2)}) %collective-permute-start.23) | collective-permute-done | bytes 524320 | tf_op jit(solution)/shard_map/ppermute | solution.py:31
  146.3 2.6 %collective-permute-start.25 = (bf16[1,64,2048]{2,1,0:T(8,128)(2,1)}, bf16[1,64,2048]{2,1,0:T(8,128)(2,1)S(1)}, u32[]{:S(2)}, u32[]{:S(2)}) collective-permute-start(bf16[1,64,2048]{2,1,0:T(8,128)(2,1)} %dynamic-slice_convert_fusion), channel_id=1, source_target_pairs={{0,4},{1,5},{2,6},{3,7},{4,0},{5,1},{6,2},{7,3},{8,12},{9,13},{10,... | collective-permute-start | bytes 786440 | tf_op jit(solution)/shard_map/ppermute | solution.py:31
  150.8 9.1 %collective-permute-done.25 = bf16[1,64,2048]{2,1,0:T(8,128)(2,1)S(1)} collective-permute-done((bf16[1,64,2048]{2,1,0:T(8,128)(2,1)}, bf16[1,64,2048]{2,1,0:T(8,128)(2,1)S(1)}, u32[]{:S(2)}, u32[]{:S(2)}) %collective-permute-start.25) | collective-permute-done | bytes 262176 | tf_op jit(solution)/shard_map/ppermute | solution.py:31
  159.9 2.4 %collective-permute-done.26 = bf16[2,64,1024]{2,1,0:T(8,128)(2,1)} collective-permute-done((bf16[2,64,1024]{2,1,0:T(8,128)(2,1)}, bf16[2,64,1024]{2,1,0:T(8,128)(2,1)}, u32[]{:S(2)}, u32[]{:S(2)}) %collective-permute-start.26) | collective-permute-done | bytes 262176 | tf_op jit(solution)/shard_map/ppermute | solution.py:31
  165.6 6.0 %collective-permute-done.28 = bf16[1,64,1024]{2,1,0:T(8,128)(2,1)S(1)} collective-permute-done((bf16[1,64,1024]{2,1,0:T(8,128)(2,1)S(1)}, bf16[1,64,1024]{2,1,0:T(8,128)(2,1)S(1)}, u32[]{:S(2)}, u32[]{:S(2)}) %collective-permute-start.28) | collective-permute-done | bytes 131104 | tf_op jit(solution)/shard_map/ppermute | solution.py:31
  171.5 2.2 %collective-permute-done.29 = bf16[2,64,1024]{2,1,0:T(8,128)(2,1)S(1)} collective-permute-done((bf16[2,64,1024]{2,1,0:T(8,128)(2,1)S(1)}, bf16[2,64,1024]{2,1,0:T(8,128)(2,1)S(1)}, u32[]{:S(2)}, u32[]{:S(2)}) %collective-permute-start.29) | collective-permute-done | bytes 262176 | tf_op jit(solution)/shard_map/ppermute | solution.py:31
  175.1 5.5 %collective-permute-done.30 = bf16[1,64,1024]{2,1,0:T(8,128)(2,1)S(1)} collective-permute-done((bf16[1,64,1024]{2,1,0:T(8,128)(2,1)S(1)}, bf16[1,64,1024]{2,1,0:T(8,128)(2,1)S(1)}, u32[]{:S(2)}, u32[]{:S(2)}) %collective-permute-start.30) | collective-permute-done | bytes 131104 | tf_op jit(solution)/shard_map/ppermute | solution.py:31
  (173 shorter events, 59.0 us)
Async XLA Ops:
  4.8 26.6 %collective-permute-start.3 = (bf16[2,128,2048]{2,1,0:T(8,128)(2,1)S(1)}, bf16[2,128,2048]{2,1,0:T(8,128)(2,1)S(1)}, u32[]{:S(2)}, u32[]{:S(2)}) collective-permute-start(bf16[2,128,2048]{2,1,0:T(8,128)(2,1)S(1)} %get-tuple-element.48), channel_id=1, source_target_pairs={{0,16},{8,24},{16,0},{24,8},{1,17},{9,25},{17,1},{25,9},{2,18},{10... | collective-permute-start | bytes 3145736 | tf_op jit(solution)/shard_map/ppermute | solution.py:31
  15.0 17.3 %collective-permute-start.2 = (f32[128,2432]{1,0:T(8,128)S(1)}, f32[128,2432]{1,0:T(8,128)S(1)}, u32[]{:S(2)}, u32[]{:S(2)}) collective-permute-start(f32[128,2432]{1,0:T(8,128)S(1)} %fusion.5), channel_id=1, source_target_pairs={{0,8},{8,0},{16,24},{24,16},{1,9},{9,1},{17,25},{25,17},{2,10},{10... | collective-permute-start | bytes 3735560 | tf_op jit(solution)/shard_map/ppermute | solution.py:31
  16.2 15.2 %collective-permute-start.6 = (f32[1,2432]{1,0:T(1,128)S(1)}, f32[1,2432]{1,0:T(1,128)S(1)}, u32[]{:S(2)}, u32[]{:S(2)}) collective-permute-start(f32[1,2432]{1,0:T(1,128)S(1)} %reshape_add_fusion), channel_id=1, source_target_pairs={{0,16},{8,24},{16,0},{24,8},{1,17},{9,25},{17,1},{25,9},{2,18},{10... | collective-permute-start | bytes 29192 | tf_op jit(solution)/shard_map/ppermute | solution.py:31
  17.8 17.3 %collective-permute-start.4 = (f32[2,8,128]{2,1,0:T(8,128)S(1)}, f32[2,8,128]{2,1,0:T(8,128)S(1)}, u32[]{:S(2)}, u32[]{:S(2)}) collective-permute-start(f32[2,8,128]{2,1,0:T(8,128)S(1)} %pad_maximum_fusion.5), channel_id=1, source_target_pairs={{0,16},{8,24},{16,0},{24,8},{1,17},{9,25},{17,1},{25,9},{2,18},{10... | collective-permute-start | bytes 24584 | tf_op jit(solution)/shard_map/ppermute | solution.py:31
  37.2 16.0 %collective-permute-start.9 = (f16[128,2432]{1,0:T(8,128)(2,1)S(1)}, f16[128,2432]{1,0:T(8,128)(2,1)S(1)}, u32[]{:S(2)}, u32[]{:S(2)}) collective-permute-start(f16[128,2432]{1,0:T(8,128)(2,1)S(1)} %get-tuple-element.51), channel_id=1, source_target_pairs={{0,16},{8,24},{16,0},{24,8},{1,17},{9,25},{17,1},{25,9},{2,18},{10... | collective-permute-start | bytes 1867784 | tf_op jit(solution)/shard_map/ppermute | solution.py:31
  53.5 18.1 %collective-permute-start.10 = (f16[128,2432]{1,0:T(8,128)(2,1)}, f16[128,2432]{1,0:T(8,128)(2,1)}, u32[]{:S(2)}, u32[]{:S(2)}) collective-permute-start(f16[128,2432]{1,0:T(8,128)(2,1)} %get-tuple-element.52), channel_id=1, source_target_pairs={{0,16},{8,24},{16,0},{24,8},{1,17},{9,25},{17,1},{25,9},{2,18},{10... | collective-permute-start | bytes 1867784 | tf_op jit(solution)/shard_map/ppermute | solution.py:31
  73.1 19.9 %collective-permute-start.15 = (bf16[128,2432]{1,0:T(8,128)(2,1)S(1)}, bf16[128,2432]{1,0:T(8,128)(2,1)}, u32[]{:S(2)}, u32[]{:S(2)}) collective-permute-start(bf16[128,2432]{1,0:T(8,128)(2,1)S(1)} %copy-done.7), channel_id=1, source_target_pairs={{0,16},{8,24},{16,0},{24,8},{1,17},{9,25},{17,1},{25,9},{2,18},{10... | collective-permute-start | bytes 1867784 | tf_op jit(solution)/shard_map/ppermute | solution.py:31
  74.8 18.1 %collective-permute-start.14 = (bf16[128,2432]{1,0:T(8,128)(2,1)S(1)}, bf16[128,2432]{1,0:T(8,128)(2,1)}, u32[]{:S(2)}, u32[]{:S(2)}) collective-permute-start(bf16[128,2432]{1,0:T(8,128)(2,1)S(1)} %copy-done.7), channel_id=1, source_target_pairs={{0,8},{8,0},{16,24},{24,16},{1,9},{9,1},{17,25},{25,17},{2,10},{10... | collective-permute-start | bytes 1867784 | tf_op jit(solution)/shard_map/ppermute | solution.py:31
  78.1 14.9 %collective-permute-start.13 = (f32[4,512]{1,0:T(4,128)S(1)}, f32[4,512]{1,0:T(4,128)S(1)}, u32[]{:S(2)}, u32[]{:S(2)}) collective-permute-start(f32[4,512]{1,0:T(4,128)S(1)} %pad_maximum_fusion.6), channel_id=1, source_target_pairs={{0,1},{1,0},{2,3},{3,2},{4,5},{5,4},{6,7},{7,6},{8,9},{9,8},{10,11... | collective-permute-start | bytes 24584 | tf_op jit(solution)/shard_map/ppermute | solution.py:31
  93.1 3.7 %collective-permute-start.16 = (f32[4,512]{1,0:T(4,128)S(1)}, f32[4,512]{1,0:T(4,128)S(1)}, u32[]{:S(2)}, u32[]{:S(2)}) collective-permute-start(f32[4,512]{1,0:T(4,128)S(1)} %pad_maximum_fusion.7), channel_id=1, source_target_pairs={{0,2},{1,3},{2,0},{3,1},{4,6},{5,7},{6,4},{7,5},{8,10},{9,11},{10,... | collective-permute-start | bytes 24584 | tf_op jit(solution)/shard_map/ppermute | solution.py:31
  96.8 4.6 %collective-permute-start.17 = (f32[4,512]{1,0:T(4,128)S(1)}, f32[4,512]{1,0:T(4,128)S(1)}, u32[]{:S(2)}, u32[]{:S(2)}) collective-permute-start(f32[4,512]{1,0:T(4,128)S(1)} %pad_maximum_fusion.8), channel_id=1, source_target_pairs={{0,4},{1,5},{2,6},{3,7},{4,0},{5,1},{6,2},{7,3},{8,12},{9,13},{10,... | collective-permute-start | bytes 24584 | tf_op jit(solution)/shard_map/ppermute | solution.py:31
  99.6 8.9 %collective-permute-start.18 = (bf16[128,2432]{1,0:T(8,128)(2,1)}, bf16[128,2432]{1,0:T(8,128)(2,1)S(1)}, u32[]{:S(2)}, u32[]{:S(2)}) collective-permute-start(bf16[128,2432]{1,0:T(8,128)(2,1)} %collective-permute-done.15.refs_2_), channel_id=1, source_target_pairs={{0,8},{8,0},{16,24},{24,16},{1,9},{9,1},{17,25},{25,17},{2,10},{10... | collective-permute-start | bytes 1867784 | tf_op jit(solution)/shard_map/ppermute | solution.py:31
  104.4 18.4 %collective-permute-start.22 = (bf16[128,2048]{1,0:T(8,128)(2,1)S(1)}, bf16[128,2048]{1,0:T(8,128)(2,1)S(1)}, u32[]{:S(2)}, u32[]{:S(2)}) collective-permute-start(bf16[128,2048]{1,0:T(8,128)(2,1)S(1)} %slice.430), channel_id=1, source_target_pairs={{0,1},{1,0},{2,3},{3,2},{4,5},{5,4},{6,7},{7,6},{8,9},{9,8},{10,11... | collective-permute-start | bytes 1572872 | tf_op jit(solution)/shard_map/ppermute | solution.py:31
  104.7 3.8 %collective-permute-start.20 = (f32[2,8,128]{2,1,0:T(8,128)S(1)}, f32[2,8,128]{2,1,0:T(8,128)S(1)}, u32[]{:S(2)}, u32[]{:S(2)}) collective-permute-start(f32[2,8,128]{2,1,0:T(8,128)S(1)} %pad_maximum_fusion.9), channel_id=1, source_target_pairs={{0,16},{8,24},{16,0},{24,8},{1,17},{9,25},{17,1},{25,9},{2,18},{10... | collective-permute-start | bytes 24584 | tf_op jit(solution)/shard_map/ppermute | solution.py:31
  106.9 23.1 %collective-permute-start.21 = (bf16[128,2048]{1,0:T(8,128)(2,1)S(1)}, bf16[128,2048]{1,0:T(8,128)(2,1)S(1)}, u32[]{:S(2)}, u32[]{:S(2)}) collective-permute-start(bf16[128,2048]{1,0:T(8,128)(2,1)S(1)} %slice.431), channel_id=1, source_target_pairs={{0,1},{1,0},{2,3},{3,2},{4,5},{5,4},{6,7},{7,6},{8,9},{9,8},{10,11... | collective-permute-start | bytes 1572872 | tf_op jit(solution)/shard_map/ppermute | solution.py:31
  130.6 13.6 %collective-permute-start.23 = (bf16[2,64,2048]{2,1,0:T(8,128)(2,1)S(1)}, bf16[2,64,2048]{2,1,0:T(8,128)(2,1)S(1)}, u32[]{:S(2)}, u32[]{:S(2)}) collective-permute-start(bf16[2,64,2048]{2,1,0:T(8,128)(2,1)S(1)} %fusion.8), channel_id=1, source_target_pairs={{0,2},{1,3},{2,0},{3,1},{4,6},{5,7},{6,4},{7,5},{8,10},{9,11},{10,... | collective-permute-start | bytes 1572872 | tf_op jit(solution)/shard_map/ppermute | solution.py:31
  132.2 13.3 %collective-permute-start.24 = (bf16[256,1024]{1,0:T(8,128)(2,1)S(1)}, bf16[256,1024]{1,0:T(8,128)(2,1)S(1)}, u32[]{:S(2)}, u32[]{:S(2)}) collective-permute-start(bf16[256,1024]{1,0:T(8,128)(2,1)S(1)} %pad_maximum_fusion.1), channel_id=1, source_target_pairs={{0,1},{1,0},{2,3},{3,2},{4,5},{5,4},{6,7},{7,6},{8,9},{9,8},{10,11... | collective-permute-start | bytes 1572872 | tf_op jit(solution)/shard_map/ppermute | solution.py:31
  146.3 13.6 %collective-permute-start.25 = (bf16[1,64,2048]{2,1,0:T(8,128)(2,1)}, bf16[1,64,2048]{2,1,0:T(8,128)(2,1)S(1)}, u32[]{:S(2)}, u32[]{:S(2)}) collective-permute-start(bf16[1,64,2048]{2,1,0:T(8,128)(2,1)} %dynamic-slice_convert_fusion), channel_id=1, source_target_pairs={{0,4},{1,5},{2,6},{3,7},{4,0},{5,1},{6,2},{7,3},{8,12},{9,13},{10,... | collective-permute-start | bytes 786440 | tf_op jit(solution)/shard_map/ppermute | solution.py:31
  148.9 13.4 %collective-permute-start.27 = (bf16[256,1024]{1,0:T(8,128)(2,1)}, bf16[256,1024]{1,0:T(8,128)(2,1)}, u32[]{:S(2)}, u32[]{:S(2)}) collective-permute-start(bf16[256,1024]{1,0:T(8,128)(2,1)} %pad_maximum_fusion.2), channel_id=1, source_target_pairs={{0,1},{1,0},{2,3},{3,2},{4,5},{5,4},{6,7},{7,6},{8,9},{9,8},{10,11... | collective-permute-start | bytes 1572872 | tf_op jit(solution)/shard_map/ppermute | solution.py:31
  150.3 12.0 %collective-permute-start.26 = (bf16[2,64,1024]{2,1,0:T(8,128)(2,1)}, bf16[2,64,1024]{2,1,0:T(8,128)(2,1)}, u32[]{:S(2)}, u32[]{:S(2)}) collective-permute-start(bf16[2,64,1024]{2,1,0:T(8,128)(2,1)} %fusion.22), channel_id=1, source_target_pairs={{0,2},{1,3},{2,0},{3,1},{4,6},{5,7},{6,4},{7,5},{8,10},{9,11},{10,... | collective-permute-start | bytes 786440 | tf_op jit(solution)/shard_map/ppermute | solution.py:31
  164.6 9.2 %collective-permute-start.29 = (bf16[2,64,1024]{2,1,0:T(8,128)(2,1)S(1)}, bf16[2,64,1024]{2,1,0:T(8,128)(2,1)S(1)}, u32[]{:S(2)}, u32[]{:S(2)}) collective-permute-start(bf16[2,64,1024]{2,1,0:T(8,128)(2,1)S(1)} %fusion.23), channel_id=1, source_target_pairs={{0,2},{1,3},{2,0},{3,1},{4,6},{5,7},{6,4},{7,5},{8,10},{9,11},{10,... | collective-permute-start | bytes 786440 | tf_op jit(solution)/shard_map/ppermute | solution.py:31
  164.7 6.8 %collective-permute-start.28 = (bf16[1,64,1024]{2,1,0:T(8,128)(2,1)S(1)}, bf16[1,64,1024]{2,1,0:T(8,128)(2,1)S(1)}, u32[]{:S(2)}, u32[]{:S(2)}) collective-permute-start(bf16[1,64,1024]{2,1,0:T(8,128)(2,1)S(1)} %dynamic-slice_convert_fusion.2), channel_id=1, source_target_pairs={{0,4},{1,5},{2,6},{3,7},{4,0},{5,1},{6,2},{7,3},{8,12},{9,13},{10,... | collective-permute-start | bytes 393224 | tf_op jit(solution)/shard_map/ppermute | solution.py:31
  173.8 6.7 %collective-permute-start.30 = (bf16[1,64,1024]{2,1,0:T(8,128)(2,1)S(1)}, bf16[1,64,1024]{2,1,0:T(8,128)(2,1)S(1)}, u32[]{:S(2)}, u32[]{:S(2)}) collective-permute-start(bf16[1,64,1024]{2,1,0:T(8,128)(2,1)S(1)} %dynamic-slice_convert_fusion.1), channel_id=1, source_target_pairs={{0,4},{1,5},{2,6},{3,7},{4,0},{5,1},{6,2},{7,3},{8,12},{9,13},{10,... | collective-permute-start | bytes 393224 | tf_op jit(solution)/shard_map/ppermute | solution.py:31
  182.1 3.6 %collective-permute-start.32 = (f32[2,64]{1,0:T(2,128)S(1)}, f32[2,64]{1,0:T(2,128)S(1)}, u32[]{:S(2)}, u32[]{:S(2)}) collective-permute-start(f32[2,64]{1,0:T(2,128)S(1)} %fusion.60), channel_id=1, source_target_pairs={{0,16},{8,24},{16,0},{24,8},{1,17},{9,25},{17,1},{25,9},{2,18},{10... | collective-permute-start | bytes 1544 | tf_op jit(solution)/shard_map/ppermute | solution.py:31
  (29 other events, 179.6 us)

commit v7 on v6

--- a/solution.py
+++ b/solution.py
@@ -283,10 +283,10 @@
     given = swap(given, "seq", 1, seq_size)
     row = jnp.sum(jnp.dot(two, head, preferred_element_type=F32), axis=0, keepdims=True)
     row = row + swap(row, "seq", 1, seq_size)
-    tangent_row = row + swap(row, "seq", 2, seq_size)
     summed_0 = partial_logits(own, sums_0) + given
     send_0 = summed_0.astype(jnp.float16)
-    both, send_0, tangent_row = lax.optimization_barrier((both, send_0, tangent_row))
+    both, send_0, row = lax.optimization_barrier((both, send_0, row))
+    tangent_row = row + swap(row, "seq", 2, seq_size)
     got_2 = swap(send_0, "seq", 2, seq_size)
     sums = [sums_0, sums_1, both[0], both[1]]
     denominators = [s[0] / feature_count + EPSILON for s in sums]
@@ -294,7 +294,9 @@
     blocks = [own, mate, over_2, over_3]
     given = swap(partial_logits(blocks[3], sums[3]), "seq", 1, seq_size)
     summed_2 = partial_logits(blocks[2], sums[2]) + given
-    send_2, got_2 = lax.optimization_barrier((summed_2.astype(jnp.float16), got_2))
+    send_2, got_2, tangent_row = lax.optimization_barrier(
+        (summed_2.astype(jnp.float16), got_2, tangent_row)
+    )
     got_0 = swap(send_2, "seq", 2, seq_size)
 
     half = rows // 2

time: 187 us -> 188 us (level)
  waiting for transfers between devices: 79.2 us -> 85 us
  starting transfers between devices: 31.8 us -> 27 us
    ppermute x33, waiting for transfers between devices: 79.2 us -> 85 us  [swap(): return lax.ppermute(value, axis, [(i, i ^ bit) for i in range(size)])]
    ppermute x33, starting transfers between devices: 31.8 us -> 27 us  [swap(): return lax.ppermute(value, axis, [(i, i ^ bit) for i in range(size)])]
where the time goes in v7:
time: 188 us
  waiting for transfers between devices  85 us (45%)
  Pallas kernels  28.4 us (15%)
  starting transfers between devices  27 us (14%)
  local copies, waits for them, and re-layouts  20.2 us (11%)
  matrix products  13.8 us (7%)
  other arithmetic  12.3 us (7%)
    ppermute x33, waiting for transfers between devices, swap(): return lax.ppermute(value, axis, [(i, i ^ bit) for i in range(size)])  85 us
    ppermute x33, starting transfers between devices, swap(): return lax.ppermute(value, axis, [(i, i ^ bit) for i in range(size)])  27 us
    pallas_call x3, Pallas kernels, back(): pl.pallas_call(functools.partial(back_kernel, deep), grid=(features // ti...  21.5 us
    unnamed x40, local copies, waits for them, and re-layouts  17.1 us
    dot_general x4, matrix products, partial_logits(): return jnp.dot(normed, head, preferred_element_type=F32)  12.3 us
    pallas_call x2, Pallas kernels, soften(): pl.pallas_call(functools.partial(soften_kernel, feature_count), in_specs=...  4.41 us
  transfers between devices with their start and end apart: 33, of which 18 were waited for; matrix products, arithmetic and copies ran while one was open for 11% of the time, Pallas kernels for 15%

profile of v7, /device:TPU:0, one launch (start us, length us, event | category | flops | bytes accessed | tf_op | source)
XLA Modules:
  0.0 188.0 jit_solution(3973684454104663400)
XLA Ops:
  4.8 2.9 %collective-permute-start.3 = (bf16[2,128,2048]{2,1,0:T(8,128)(2,1)S(1)}, bf16[2,128,2048]{2,1,0:T(8,128)(2,1)S(1)}, u32[]{:S(2)}, u32[]{:S(2)}) collective-permute-start(bf16[2,128,2048]{2,1,0:T(8,128)(2,1)S(1)} %get-tuple-element.49), channel_id=1, source_target_pairs={{0,16},{8,24},{16,0},{24,8},{1,17},{9,25},{17,1},{25,9},{2,18},{10... | collective-permute-start | bytes 3145736 | tf_op jit(solution)/shard_map/ppermute | solution.py:31
  7.8 5.6 %fusion.5 = f32[128,2432]{1,0:T(8,128)S(1)} fusion(bf16[2048,2432]{1,0:T(8,128)(2,1)} %head.5, bf16[128,2048]{1,0:T(8,128)(2,1)S(1)} %collective-permute-done, f32[128]{0:T(128)S(1)} %get-tuple-element.144, f32[2048]{0:T(1024)S(1)} %bitcast.145, f32[2048]{0:T(1024)S(1)} %bitcast.139), kind=kOutput, calls=%fused_computation.28 | convolution fusion | flops 1276379136 | bytes 11747840 | tf_op jit(solution)/shard_map/dot_general | solution.py:279
  17.0 14.2 %collective-permute-done.3 = bf16[2,128,2048]{2,1,0:T(8,128)(2,1)S(1)} collective-permute-done((bf16[2,128,2048]{2,1,0:T(8,128)(2,1)S(1)}, bf16[2,128,2048]{2,1,0:T(8,128)(2,1)S(1)}, u32[]{:S(2)}, u32[]{:S(2)}) %collective-permute-start.3) | collective-permute-done | bytes 1048608 | tf_op jit(solution)/shard_map/ppermute | solution.py:31
  32.1 2.7 %fusion.78 = (f16[128,2432]{1,0:T(8,128)(2,1)S(1)}, f32[128,2432]{1,0:T(8,128)}) fusion(f32[128,2432]{1,0:T(8,128)S(1)} %collective-permute-done.2, bf16[2048,2432]{1,0:T(8,128)(2,1)S(1)} %bitcast.127, bf16[128,2048]{1,0:T(8,128)(2,1)S(1)} %get-tuple-element.44, f32[128]{0:T(128)S(1)} %get-tuple-element.142, f32[2048]{0:T(1024)S(1)} %bitcast.146, ...), kind=kOutput, calls=%fused_computation.227 | convolution fusion | flops 1277001728 | bytes 13615616 | tf_op jit(solution)/shard_map/dot_general | solution.py:279
  40.7 2.4 %fusion.79 = (f16[128,2432]{1,0:T(8,128)(2,1)}, f32[128,2432]{1,0:T(8,128)S(1)}) fusion(f32[128,2432]{1,0:T(8,128)S(1)} %collective-permute-done.7, bf16[2048,2432]{1,0:T(8,128)(2,1)S(1)} %bitcast.127, f32[128]{0:T(128)S(1)} %get-tuple-element.125, f32[2048]{0:T(1024)S(1)} %bitcast.148, f32[2048]{0:T(1024)S(1)} %bitcast.142, ...), kind=kOutput, calls=%fused_computation.228 | convolution fusion | flops 1277001728 | bytes 13615616 | tf_op jit(solution)/shard_map/dot_general | solution.py:279
  43.1 11.4 %collective-permute-done.8 = f16[128,2432]{1,0:T(8,128)(2,1)S(1)} collective-permute-done((f16[128,2432]{1,0:T(8,128)(2,1)S(1)}, f16[128,2432]{1,0:T(8,128)(2,1)S(1)}, u32[]{:S(2)}, u32[]{:S(2)}) %collective-permute-start.8) | collective-permute-done | bytes 622624 | tf_op jit(solution)/shard_map/ppermute | solution.py:31
  55.3 2.3 %collective-permute-done.11.second = f32[128,2432]{1,0:T(8,128)S(1)} collective-permute-done((f32[128,2432]{1,0:T(8,128)S(1)}, f32[128,2432]{1,0:T(8,128)S(1)}, u32[]{:S(2)}, u32[]{:S(2)}) %collective-permute-start.11) | collective-permute-done | bytes 1245216 | tf_op jit(solution)/shard_map/ppermute | solution.py:31
  57.6 2.2 %shard_map.78 = (bf16[2,256,2432]{2,1,0:T(8,128)(2,1)S(1)}, f32[8,256]{1,0:T(8,128)S(1)}) custom-call(s32[8]{0:T(128)S(1)} %pad_add_fusion.1.at, f32[128,2432]{1,0:T(8,128)S(1)} %convert_add_fusion.1.first, f32[128,2432]{1,0:T(8,128)S(1)} %collective-permute-done.11.second, f32[1,2432]{1,0:T(1,128)S(1)} %add.421.row, ...), custom_call_target="tpu_custom_call" | custom-call | tf_op jit(solution)/shard_map/pallas_call | solution.py:133
  59.8 3.8 %copy-done = bf16[2048,2432]{1,0:T(8,128)(2,1)S(1)} copy-done((bf16[2048,2432]{1,0:T(8,128)(2,1)S(1)}, bf16[2048,2432]{1,0:T(8,128)(2,1)}, u32[]{:S(2)}) %copy-start) | copy-done | bytes 9961496
  63.7 7.2 %shard_map.79 = f32[512,2048]{1,0:T(8,128)S(1)} custom-call(bf16[512,2432]{1,0:T(8,128)(2,1)S(1)} %bitcast.129, bf16[2048,2432]{1,0:T(8,128)(2,1)S(1)} %copy-done), custom_call_target="tpu_custom_call" | custom-call | tf_op jit(solution)/shard_map/pallas_call | solution.py:196
  80.9 3.8 %copy-done.1 = bf16[2048,2432]{1,0:T(8,128)(2,1)S(1)} copy-done((bf16[2048,2432]{1,0:T(8,128)(2,1)S(1)}, bf16[2048,2432]{1,0:T(8,128)(2,1)}, u32[]{:S(2)}) %copy-start.1) | copy-done | bytes 9961496
  84.7 7.1 %shard_map.81 = f32[512,2048]{1,0:T(8,128)S(1)} custom-call(bf16[512,2432]{1,0:T(8,128)(2,1)S(1)} %bitcast.128, bf16[2048,2432]{1,0:T(8,128)(2,1)S(1)} %copy-done.1), custom_call_target="tpu_custom_call" | custom-call | tf_op jit(solution)/shard_map/pallas_call | solution.py:196
  97.8 2.6 %collective-permute-start.17 = (f32[4,512]{1,0:T(4,128)S(1)}, f32[4,512]{1,0:T(4,128)S(1)}, u32[]{:S(2)}, u32[]{:S(2)}) collective-permute-start(f32[4,512]{1,0:T(4,128)S(1)} %pad_maximum_fusion.8), channel_id=1, source_target_pairs={{0,4},{1,5},{2,6},{3,7},{4,0},{5,1},{6,2},{7,3},{8,12},{9,13},{10,... | collective-permute-start | bytes 24584 | tf_op jit(solution)/shard_map/ppermute | solution.py:31
  102.6 2.7 %multiply_add_fusion = f32[256,2048]{1,0:T(8,128)S(1)} fusion(f32[512,2048]{1,0:T(8,128)} %copy-done.3, f32[256]{0:T(256)S(1)} %mul.320, f32[256]{0:T(256)S(1)} %bitcast.158), kind=kLoop, calls=%fused_computation.7 | loop fusion | flops 1572864 | bytes 6293504 | tf_op jit(solution)/shard_map/add | solution.py:316
  111.3 3.8 %copy-done.2 = bf16[2048,2432]{1,0:T(8,128)(2,1)S(1)} copy-done((bf16[2048,2432]{1,0:T(8,128)(2,1)S(1)}, bf16[2048,2432]{1,0:T(8,128)(2,1)}, u32[]{:S(2)}) %copy-start.2) | copy-done | bytes 9961496
  115.2 7.2 %shard_map.83 = f32[512,2048]{1,0:T(8,128)S(1)} custom-call(bf16[512,2432]{1,0:T(8,128)(2,1)S(1)} %get-tuple-element.71.cotangent, bf16[2048,2432]{1,0:T(8,128)(2,1)S(1)} %copy-done.2), custom_call_target="tpu_custom_call" | custom-call | tf_op jit(solution)/shard_map/pallas_call | solution.py:196
  123.9 7.1 %collective-permute-done.21 = bf16[128,2048]{1,0:T(8,128)(2,1)S(1)} collective-permute-done((bf16[128,2048]{1,0:T(8,128)(2,1)S(1)}, bf16[128,2048]{1,0:T(8,128)(2,1)S(1)}, u32[]{:S(2)}, u32[]{:S(2)}) %collective-permute-start.21) | collective-permute-done | bytes 524320 | tf_op jit(solution)/shard_map/ppermute | solution.py:31
  133.9 11.3 %collective-permute-done.23 = bf16[2,64,2048]{2,1,0:T(8,128)(2,1)S(1)} collective-permute-done((bf16[2,64,2048]{2,1,0:T(8,128)(2,1)S(1)}, bf16[2,64,2048]{2,1,0:T(8,128)(2,1)S(1)}, u32[]{:S(2)}, u32[]{:S(2)}) %collective-permute-start.23) | collective-permute-done | bytes 524320 | tf_op jit(solution)/shard_map/ppermute | solution.py:31
  147.3 2.6 %collective-permute-start.25 = (bf16[1,64,2048]{2,1,0:T(8,128)(2,1)}, bf16[1,64,2048]{2,1,0:T(8,128)(2,1)S(1)}, u32[]{:S(2)}, u32[]{:S(2)}) collective-permute-start(bf16[1,64,2048]{2,1,0:T(8,128)(2,1)} %dynamic-slice_convert_fusion), channel_id=1, source_target_pairs={{0,4},{1,5},{2,6},{3,7},{4,0},{5,1},{6,2},{7,3},{8,12},{9,13},{10,... | collective-permute-start | bytes 786440 | tf_op jit(solution)/shard_map/ppermute | solution.py:31
  151.8 9.1 %collective-permute-done.25 = bf16[1,64,2048]{2,1,0:T(8,128)(2,1)S(1)} collective-permute-done((bf16[1,64,2048]{2,1,0:T(8,128)(2,1)}, bf16[1,64,2048]{2,1,0:T(8,128)(2,1)S(1)}, u32[]{:S(2)}, u32[]{:S(2)}) %collective-permute-start.25) | collective-permute-done | bytes 262176 | tf_op jit(solution)/shard_map/ppermute | solution.py:31
  160.9 2.4 %collective-permute-done.26 = bf16[2,64,1024]{2,1,0:T(8,128)(2,1)} collective-permute-done((bf16[2,64,1024]{2,1,0:T(8,128)(2,1)}, bf16[2,64,1024]{2,1,0:T(8,128)(2,1)}, u32[]{:S(2)}, u32[]{:S(2)}) %collective-permute-start.26) | collective-permute-done | bytes 262176 | tf_op jit(solution)/shard_map/ppermute | solution.py:31
  166.5 6.0 %collective-permute-done.28 = bf16[1,64,1024]{2,1,0:T(8,128)(2,1)S(1)} collective-permute-done((bf16[1,64,1024]{2,1,0:T(8,128)(2,1)S(1)}, bf16[1,64,1024]{2,1,0:T(8,128)(2,1)S(1)}, u32[]{:S(2)}, u32[]{:S(2)}) %collective-permute-start.28) | collective-permute-done | bytes 131104 | tf_op jit(solution)/shard_map/ppermute | solution.py:31
  176.1 5.5 %collective-permute-done.30 = bf16[1,64,1024]{2,1,0:T(8,128)(2,1)S(1)} collective-permute-done((bf16[1,64,1024]{2,1,0:T(8,128)(2,1)S(1)}, bf16[1,64,1024]{2,1,0:T(8,128)(2,1)S(1)}, u32[]{:S(2)}, u32[]{:S(2)}) %collective-permute-start.30) | collective-permute-done | bytes 131104 | tf_op jit(solution)/shard_map/ppermute | solution.py:31
  183.9 2.9 %collective-permute-done.32 = f32[2,64]{1,0:T(2,128)S(1)} collective-permute-done((f32[2,64]{1,0:T(2,128)S(1)}, f32[2,64]{1,0:T(2,128)S(1)}, u32[]{:S(2)}, u32[]{:S(2)}) %collective-permute-start.32) | collective-permute-done | bytes 544 | tf_op jit(solution)/shard_map/ppermute | solution.py:31
  (173 shorter events, 58.0 us)
Async XLA Ops:
  4.8 26.4 %collective-permute-start.3 = (bf16[2,128,2048]{2,1,0:T(8,128)(2,1)S(1)}, bf16[2,128,2048]{2,1,0:T(8,128)(2,1)S(1)}, u32[]{:S(2)}, u32[]{:S(2)}) collective-permute-start(bf16[2,128,2048]{2,1,0:T(8,128)(2,1)S(1)} %get-tuple-element.49), channel_id=1, source_target_pairs={{0,16},{8,24},{16,0},{24,8},{1,17},{9,25},{17,1},{25,9},{2,18},{10... | collective-permute-start | bytes 3145736 | tf_op jit(solution)/shard_map/ppermute | solution.py:31
  15.0 17.1 %collective-permute-start.2 = (f32[128,2432]{1,0:T(8,128)S(1)}, f32[128,2432]{1,0:T(8,128)S(1)}, u32[]{:S(2)}, u32[]{:S(2)}) collective-permute-start(f32[128,2432]{1,0:T(8,128)S(1)} %fusion.5), channel_id=1, source_target_pairs={{0,8},{8,0},{16,24},{24,16},{1,9},{9,1},{17,25},{25,17},{2,10},{10... | collective-permute-start | bytes 3735560 | tf_op jit(solution)/shard_map/ppermute | solution.py:31
  15.5 19.3 %collective-permute-start.4 = (f32[2,8,128]{2,1,0:T(8,128)S(1)}, f32[2,8,128]{2,1,0:T(8,128)S(1)}, u32[]{:S(2)}, u32[]{:S(2)}) collective-permute-start(f32[2,8,128]{2,1,0:T(8,128)S(1)} %pad_maximum_fusion.5), channel_id=1, source_target_pairs={{0,16},{8,24},{16,0},{24,8},{1,17},{9,25},{17,1},{25,9},{2,18},{10... | collective-permute-start | bytes 24584 | tf_op jit(solution)/shard_map/ppermute | solution.py:31
  36.4 4.2 %collective-permute-start.7 = (f32[128,2432]{1,0:T(8,128)S(1)}, f32[128,2432]{1,0:T(8,128)S(1)}, u32[]{:S(2)}, u32[]{:S(2)}) collective-permute-start(f32[128,2432]{1,0:T(8,128)S(1)} %fusion.6), channel_id=1, source_target_pairs={{0,8},{8,0},{16,24},{24,16},{1,9},{9,1},{17,25},{25,17},{2,10},{10... | collective-permute-start | bytes 3735560 | tf_op jit(solution)/shard_map/ppermute | solution.py:31
  37.0 3.7 %collective-permute-start.9 = (f32[1,2432]{1,0:T(1,128)S(1)}, f32[1,2432]{1,0:T(1,128)S(1)}, u32[]{:S(2)}, u32[]{:S(2)}) collective-permute-start(f32[1,2432]{1,0:T(1,128)S(1)} %reshape_add_fusion), channel_id=1, source_target_pairs={{0,16},{8,24},{16,0},{24,8},{1,17},{9,25},{17,1},{25,9},{2,18},{10... | collective-permute-start | bytes 29192 | tf_op jit(solution)/shard_map/ppermute | solution.py:31
  38.7 15.7 %collective-permute-start.8 = (f16[128,2432]{1,0:T(8,128)(2,1)S(1)}, f16[128,2432]{1,0:T(8,128)(2,1)S(1)}, u32[]{:S(2)}, u32[]{:S(2)}) collective-permute-start(f16[128,2432]{1,0:T(8,128)(2,1)S(1)} %get-tuple-element.52), channel_id=1, source_target_pairs={{0,16},{8,24},{16,0},{24,8},{1,17},{9,25},{17,1},{25,9},{2,18},{10... | collective-permute-start | bytes 1867784 | tf_op jit(solution)/shard_map/ppermute | solution.py:31
  54.7 18.1 %collective-permute-start.10 = (f16[128,2432]{1,0:T(8,128)(2,1)}, f16[128,2432]{1,0:T(8,128)(2,1)}, u32[]{:S(2)}, u32[]{:S(2)}) collective-permute-start(f16[128,2432]{1,0:T(8,128)(2,1)} %get-tuple-element.54), channel_id=1, source_target_pairs={{0,16},{8,24},{16,0},{24,8},{1,17},{9,25},{17,1},{25,9},{2,18},{10... | collective-permute-start | bytes 1867784 | tf_op jit(solution)/shard_map/ppermute | solution.py:31
  74.3 19.6 %collective-permute-start.15 = (bf16[128,2432]{1,0:T(8,128)(2,1)S(1)}, bf16[128,2432]{1,0:T(8,128)(2,1)}, u32[]{:S(2)}, u32[]{:S(2)}) collective-permute-start(bf16[128,2432]{1,0:T(8,128)(2,1)S(1)} %copy-done.7), channel_id=1, source_target_pairs={{0,16},{8,24},{16,0},{24,8},{1,17},{9,25},{17,1},{25,9},{2,18},{10... | collective-permute-start | bytes 1867784 | tf_op jit(solution)/shard_map/ppermute | solution.py:31
  74.8 19.1 %collective-permute-start.14 = (bf16[128,2432]{1,0:T(8,128)(2,1)S(1)}, bf16[128,2432]{1,0:T(8,128)(2,1)}, u32[]{:S(2)}, u32[]{:S(2)}) collective-permute-start(bf16[128,2432]{1,0:T(8,128)(2,1)S(1)} %copy-done.7), channel_id=1, source_target_pairs={{0,8},{8,0},{16,24},{24,16},{1,9},{9,1},{17,25},{25,17},{2,10},{10... | collective-permute-start | bytes 1867784 | tf_op jit(solution)/shard_map/ppermute | solution.py:31
  79.3 14.6 %collective-permute-start.13 = (f32[4,512]{1,0:T(4,128)S(1)}, f32[4,512]{1,0:T(4,128)S(1)}, u32[]{:S(2)}, u32[]{:S(2)}) collective-permute-start(f32[4,512]{1,0:T(4,128)S(1)} %pad_maximum_fusion.6), channel_id=1, source_target_pairs={{0,1},{1,0},{2,3},{3,2},{4,5},{5,4},{6,7},{7,6},{8,9},{9,8},{10,11... | collective-permute-start | bytes 24584 | tf_op jit(solution)/shard_map/ppermute | solution.py:31
  94.0 3.7 %collective-permute-start.16 = (f32[4,512]{1,0:T(4,128)S(1)}, f32[4,512]{1,0:T(4,128)S(1)}, u32[]{:S(2)}, u32[]{:S(2)}) collective-permute-start(f32[4,512]{1,0:T(4,128)S(1)} %pad_maximum_fusion.7), channel_id=1, source_target_pairs={{0,2},{1,3},{2,0},{3,1},{4,6},{5,7},{6,4},{7,5},{8,10},{9,11},{10,... | collective-permute-start | bytes 24584 | tf_op jit(solution)/shard_map/ppermute | solution.py:31
  97.8 4.6 %collective-permute-start.17 = (f32[4,512]{1,0:T(4,128)S(1)}, f32[4,512]{1,0:T(4,128)S(1)}, u32[]{:S(2)}, u32[]{:S(2)}) collective-permute-start(f32[4,512]{1,0:T(4,128)S(1)} %pad_maximum_fusion.8), channel_id=1, source_target_pairs={{0,4},{1,5},{2,6},{3,7},{4,0},{5,1},{6,2},{7,3},{8,12},{9,13},{10,... | collective-permute-start | bytes 24584 | tf_op jit(solution)/shard_map/ppermute | solution.py:31
  100.6 9.1 %collective-permute-start.18 = (bf16[128,2432]{1,0:T(8,128)(2,1)}, bf16[128,2432]{1,0:T(8,128)(2,1)S(1)}, u32[]{:S(2)}, u32[]{:S(2)}) collective-permute-start(bf16[128,2432]{1,0:T(8,128)(2,1)} %collective-permute-done.15.refs_2_), channel_id=1, source_target_pairs={{0,8},{8,0},{16,24},{24,16},{1,9},{9,1},{17,25},{25,17},{2,10},{10... | collective-permute-start | bytes 1867784 | tf_op jit(solution)/shard_map/ppermute | solution.py:31
  105.4 18.6 %collective-permute-start.22 = (bf16[128,2048]{1,0:T(8,128)(2,1)S(1)}, bf16[128,2048]{1,0:T(8,128)(2,1)S(1)}, u32[]{:S(2)}, u32[]{:S(2)}) collective-permute-start(bf16[128,2048]{1,0:T(8,128)(2,1)S(1)} %slice.430), channel_id=1, source_target_pairs={{0,1},{1,0},{2,3},{3,2},{4,5},{5,4},{6,7},{7,6},{8,9},{9,8},{10,11... | collective-permute-start | bytes 1572872 | tf_op jit(solution)/shard_map/ppermute | solution.py:31
  106.0 3.7 %collective-permute-start.20 = (f32[2,8,128]{2,1,0:T(8,128)S(1)}, f32[2,8,128]{2,1,0:T(8,128)S(1)}, u32[]{:S(2)}, u32[]{:S(2)}) collective-permute-start(f32[2,8,128]{2,1,0:T(8,128)S(1)} %pad_maximum_fusion.9), channel_id=1, source_target_pairs={{0,16},{8,24},{16,0},{24,8},{1,17},{9,25},{17,1},{25,9},{2,18},{10... | collective-permute-start | bytes 24584 | tf_op jit(solution)/shard_map/ppermute | solution.py:31
  106.9 24.1 %collective-permute-start.21 = (bf16[128,2048]{1,0:T(8,128)(2,1)S(1)}, bf16[128,2048]{1,0:T(8,128)(2,1)S(1)}, u32[]{:S(2)}, u32[]{:S(2)}) collective-permute-start(bf16[128,2048]{1,0:T(8,128)(2,1)S(1)} %slice.431), channel_id=1, source_target_pairs={{0,1},{1,0},{2,3},{3,2},{4,5},{5,4},{6,7},{7,6},{8,9},{9,8},{10,11... | collective-permute-start | bytes 1572872 | tf_op jit(solution)/shard_map/ppermute | solution.py:31
  131.5 13.6 %collective-permute-start.23 = (bf16[2,64,2048]{2,1,0:T(8,128)(2,1)S(1)}, bf16[2,64,2048]{2,1,0:T(8,128)(2,1)S(1)}, u32[]{:S(2)}, u32[]{:S(2)}) collective-permute-start(bf16[2,64,2048]{2,1,0:T(8,128)(2,1)S(1)} %fusion.8), channel_id=1, source_target_pairs={{0,2},{1,3},{2,0},{3,1},{4,6},{5,7},{6,4},{7,5},{8,10},{9,11},{10,... | collective-permute-start | bytes 1572872 | tf_op jit(solution)/shard_map/ppermute | solution.py:31
  133.2 13.3 %collective-permute-start.24 = (bf16[256,1024]{1,0:T(8,128)(2,1)S(1)}, bf16[256,1024]{1,0:T(8,128)(2,1)S(1)}, u32[]{:S(2)}, u32[]{:S(2)}) collective-permute-start(bf16[256,1024]{1,0:T(8,128)(2,1)S(1)} %pad_maximum_fusion.1), channel_id=1, source_target_pairs={{0,1},{1,0},{2,3},{3,2},{4,5},{5,4},{6,7},{7,6},{8,9},{9,8},{10,11... | collective-permute-start | bytes 1572872 | tf_op jit(solution)/shard_map/ppermute | solution.py:31
  147.3 13.6 %collective-permute-start.25 = (bf16[1,64,2048]{2,1,0:T(8,128)(2,1)}, bf16[1,64,2048]{2,1,0:T(8,128)(2,1)S(1)}, u32[]{:S(2)}, u32[]{:S(2)}) collective-permute-start(bf16[1,64,2048]{2,1,0:T(8,128)(2,1)} %dynamic-slice_convert_fusion), channel_id=1, source_target_pairs={{0,4},{1,5},{2,6},{3,7},{4,0},{5,1},{6,2},{7,3},{8,12},{9,13},{10,... | collective-permute-start | bytes 786440 | tf_op jit(solution)/shard_map/ppermute | solution.py:31
  149.9 13.4 %collective-permute-start.27 = (bf16[256,1024]{1,0:T(8,128)(2,1)}, bf16[256,1024]{1,0:T(8,128)(2,1)}, u32[]{:S(2)}, u32[]{:S(2)}) collective-permute-start(bf16[256,1024]{1,0:T(8,128)(2,1)} %pad_maximum_fusion.2), channel_id=1, source_target_pairs={{0,1},{1,0},{2,3},{3,2},{4,5},{5,4},{6,7},{7,6},{8,9},{9,8},{10,11... | collective-permute-start | bytes 1572872 | tf_op jit(solution)/shard_map/ppermute | solution.py:31
  151.3 12.0 %collective-permute-start.26 = (bf16[2,64,1024]{2,1,0:T(8,128)(2,1)}, bf16[2,64,1024]{2,1,0:T(8,128)(2,1)}, u32[]{:S(2)}, u32[]{:S(2)}) collective-permute-start(bf16[2,64,1024]{2,1,0:T(8,128)(2,1)} %fusion.22), channel_id=1, source_target_pairs={{0,2},{1,3},{2,0},{3,1},{4,6},{5,7},{6,4},{7,5},{8,10},{9,11},{10,... | collective-permute-start | bytes 786440 | tf_op jit(solution)/shard_map/ppermute | solution.py:31
  165.5 9.2 %collective-permute-start.29 = (bf16[2,64,1024]{2,1,0:T(8,128)(2,1)S(1)}, bf16[2,64,1024]{2,1,0:T(8,128)(2,1)S(1)}, u32[]{:S(2)}, u32[]{:S(2)}) collective-permute-start(bf16[2,64,1024]{2,1,0:T(8,128)(2,1)S(1)} %fusion.23), channel_id=1, source_target_pairs={{0,2},{1,3},{2,0},{3,1},{4,6},{5,7},{6,4},{7,5},{8,10},{9,11},{10,... | collective-permute-start | bytes 786440 | tf_op jit(solution)/shard_map/ppermute | solution.py:31
  165.7 6.8 %collective-permute-start.28 = (bf16[1,64,1024]{2,1,0:T(8,128)(2,1)S(1)}, bf16[1,64,1024]{2,1,0:T(8,128)(2,1)S(1)}, u32[]{:S(2)}, u32[]{:S(2)}) collective-permute-start(bf16[1,64,1024]{2,1,0:T(8,128)(2,1)S(1)} %dynamic-slice_convert_fusion.2), channel_id=1, source_target_pairs={{0,4},{1,5},{2,6},{3,7},{4,0},{5,1},{6,2},{7,3},{8,12},{9,13},{10,... | collective-permute-start | bytes 393224 | tf_op jit(solution)/shard_map/ppermute | solution.py:31
  174.8 6.7 %collective-permute-start.30 = (bf16[1,64,1024]{2,1,0:T(8,128)(2,1)S(1)}, bf16[1,64,1024]{2,1,0:T(8,128)(2,1)S(1)}, u32[]{:S(2)}, u32[]{:S(2)}) collective-permute-start(bf16[1,64,1024]{2,1,0:T(8,128)(2,1)S(1)} %dynamic-slice_convert_fusion.1), channel_id=1, source_target_pairs={{0,4},{1,5},{2,6},{3,7},{4,0},{5,1},{6,2},{7,3},{8,12},{9,13},{10,... | collective-permute-start | bytes 393224 | tf_op jit(solution)/shard_map/ppermute | solution.py:31
  (29 other events, 180.0 us)

commit v8 on v5

--- a/solution.py
+++ b/solution.py
@@ -325,7 +325,11 @@
     joint, (raw_own, target_1, target_2) = exchange(
         jnp.concatenate([stats, jnp.concatenate([own_total] * seq_size)[None]]),
         vocab_size,
-        (back(both_own, head), target_1, target_2),
+        (
+            lax.dot_general(both_own, head, NT, preferred_element_type=F32),
+            target_1,
+            target_2,
+        ),
     )
     plain_own, theirs_own, kept_own = scaled_of(raw_own, stats_own, joint[:, :half])
     plain_other, theirs_other, kept_other = scaled_of(raw_other, stats_other, joint[:, half:])

time: 187 us -> 186 us (level)
  matrix products: 13.8 us -> 23.5 us
  Pallas kernels: 28.4 us -> 20.5 us
  local copies, waits for them, and re-layouts: 19.3 us -> 15.2 us
  starting transfers between devices: 31.7 us -> 33.6 us
    dot_general x0 -> x1, matrix products: none -> 9.71 us  [body(): lax.dot_general(both_own, head, NT, preferred_element_type=F32)]
    pallas_call x3 -> x2, Pallas kernels: 21.5 us -> 14.3 us  [back(): pl.pallas_call(functools.partial(back_kernel, deep), grid=(features // ti...]
    unnamed x42 -> x46, local copies, waits for them, and re-layouts: 17.1 us -> 13 us
    ppermute x33, starting transfers between devices: 31.7 us -> 33.6 us  [swap(): return lax.ppermute(value, axis, [(i, i ^ bit) for i in range(size)])]
  transfers between devices with their start and end apart: 33 -> 33, of which waited for: 18 -> 19; matrix products, arithmetic and copies ran while one was open for 10% -> 15% of each run, Pallas kernels for 15% -> 10%
where the time goes in v8:
time: 186 us
  waiting for transfers between devices  79.7 us (43%)
  starting transfers between devices  33.6 us (18%)
  matrix products  23.5 us (13%)
  Pallas kernels  20.5 us (11%)
  local copies, waits for them, and re-layouts  15.2 us (8%)
  other arithmetic  12.3 us (7%)
    ppermute x33, waiting for transfers between devices, swap(): return lax.ppermute(value, axis, [(i, i ^ bit) for i in range(size)])  79.7 us
    ppermute x33, starting transfers between devices, swap(): return lax.ppermute(value, axis, [(i, i ^ bit) for i in range(size)])  33.6 us
    pallas_call x2, Pallas kernels, back(): pl.pallas_call(functools.partial(back_kernel, deep), grid=(features // ti...  14.3 us
    unnamed x46, local copies, waits for them, and re-layouts  13 us
    dot_general x4, matrix products, partial_logits(): return jnp.dot(normed, head, preferred_element_type=F32)  12.3 us
    dot_general x1, matrix products, body(): lax.dot_general(both_own, head, NT, preferred_element_type=F32)  9.71 us
    pallas_call x2, Pallas kernels, soften(): pl.pallas_call(functools.partial(soften_kernel, feature_count), in_specs=...  4.41 us
  transfers between devices with their start and end apart: 33, of which 19 were waited for; matrix products, arithmetic and copies ran while one was open for 15% of the time, Pallas kernels for 10%

profile of v8, /device:TPU:0, one launch (start us, length us, event | category | flops | bytes accessed | tf_op | source)
XLA Modules:
  0.0 186.1 jit_solution(1344661097247765043)
XLA Ops:
  4.7 2.6 %collective-permute-start.7 = (bf16[128,2048]{1,0:T(8,128)(2,1)S(1)}, bf16[128,2048]{1,0:T(8,128)(2,1)S(1)}, u32[]{:S(2)}, u32[]{:S(2)}) collective-permute-start(bf16[128,2048]{1,0:T(8,128)(2,1)S(1)} %get-tuple-element.52), channel_id=1, source_target_pairs={{0,24},{8,16},{16,8},{24,0},{1,25},{9,17},{17,9},{25,1},{2,26},{10... | collective-permute-start | bytes 1572872 | tf_op jit(solution)/shard_map/ppermute | solution.py:31
  7.4 5.7 %fusion.2 = f32[128,2432]{1,0:T(8,128)S(1)} fusion(bf16[2048,2432]{1,0:T(8,128)(2,1)} %head.3, bf16[128,2048]{1,0:T(8,128)(2,1)S(1)} %collective-permute-done, f32[128]{0:T(128)S(1)} %get-tuple-element.142, f32[2048]{0:T(1024)S(1)} %bitcast.129, f32[2048]{0:T(1024)S(1)} %bitcast.123), kind=kOutput, calls=%fused_computation.25 | convolution fusion | flops 1276379136 | bytes 11747840 | tf_op jit(solution)/shard_map/dot_general | solution.py:277
  20.1 2.7 %fusion.69 = (f16[128,2432]{1,0:T(8,128)(2,1)S(1)}, f32[128,2432]{1,0:T(8,128)}) fusion(f32[128,2432]{1,0:T(8,128)S(1)} %collective-permute-done.2, bf16[2048,2432]{1,0:T(8,128)(2,1)S(1)} %bitcast.111, bf16[128,2048]{1,0:T(8,128)(2,1)S(1)} %get-tuple-element.44, f32[128]{0:T(128)S(1)} %get-tuple-element.140, f32[2048]{0:T(1024)S(1)} %bitcast.130, ...), kind=kOutput, calls=%fused_computation.218 | convolution fusion | flops 1277001728 | bytes 13615616 | tf_op jit(solution)/shard_map/dot_general | solution.py:277
  24.5 2.2 %collective-permute-start.3 = (bf16[128,2048]{1,0:T(8,128)(2,1)S(1)}, bf16[128,2048]{1,0:T(8,128)(2,1)S(1)}, u32[]{:S(2)}, u32[]{:S(2)}) collective-permute-start(bf16[128,2048]{1,0:T(8,128)(2,1)S(1)} %get-tuple-element.49), channel_id=1, source_target_pairs={{0,16},{8,24},{16,0},{24,8},{1,17},{9,25},{17,1},{25,9},{2,18},{10... | collective-permute-start | bytes 1572872 | tf_op jit(solution)/shard_map/ppermute | solution.py:31
  26.8 12.7 %collective-permute-done.3 = bf16[128,2048]{1,0:T(8,128)(2,1)S(1)} collective-permute-done((bf16[128,2048]{1,0:T(8,128)(2,1)S(1)}, bf16[128,2048]{1,0:T(8,128)(2,1)S(1)}, u32[]{:S(2)}, u32[]{:S(2)}) %collective-permute-start.3) | collective-permute-done | bytes 524320 | tf_op jit(solution)/shard_map/ppermute | solution.py:31
  39.4 2.4 %fusion.70 = (f16[128,2432]{1,0:T(8,128)(2,1)}, f32[128,2432]{1,0:T(8,128)S(1)}) fusion(f32[128,2432]{1,0:T(8,128)S(1)} %collective-permute-done.8, bf16[2048,2432]{1,0:T(8,128)(2,1)S(1)} %bitcast.111, bf16[128,2048]{1,0:T(8,128)(2,1)S(1)} %collective-permute-done.3, f32[128]{0:T(128)S(1)} %get-tuple-element.123, f32[2048]{0:T(1024)S(1)} %bitcast.132, ...), kind=kOutput, calls=%fused_computation.219 | convolution fusion | flops 1277001728 | bytes 13615616 | tf_op jit(solution)/shard_map/dot_general | solution.py:277
  41.9 10.7 %collective-permute-done.9 = f16[128,2432]{1,0:T(8,128)(2,1)S(1)} collective-permute-done((f16[128,2432]{1,0:T(8,128)(2,1)S(1)}, f16[128,2432]{1,0:T(8,128)(2,1)S(1)}, u32[]{:S(2)}, u32[]{:S(2)}) %collective-permute-start.9) | collective-permute-done | bytes 622624 | tf_op jit(solution)/shard_map/ppermute | solution.py:31
  55.7 2.2 %shard_map.78 = (bf16[2,256,2432]{2,1,0:T(8,128)(2,1)S(1)}, f32[8,256]{1,0:T(8,128)S(1)}) custom-call(s32[8]{0:T(128)S(1)} %pad_add_fusion.1.at, f32[128,2432]{1,0:T(8,128)S(1)} %convert_add_fusion.1.first, f32[128,2432]{1,0:T(8,128)S(1)} %collective-permute-done.11.second, f32[1,2432]{1,0:T(1,128)S(1)} %add.417.row, ...), custom_call_target="tpu_custom_call" | custom-call | tf_op jit(solution)/shard_map/pallas_call | solution.py:132
  57.9 3.8 %copy-done = bf16[2048,2432]{1,0:T(8,128)(2,1)S(1)} copy-done((bf16[2048,2432]{1,0:T(8,128)(2,1)S(1)}, bf16[2048,2432]{1,0:T(8,128)(2,1)}, u32[]{:S(2)}) %copy-start) | copy-done | bytes 9961496
  61.7 7.2 %shard_map.79 = f32[512,2048]{1,0:T(8,128)S(1)} custom-call(bf16[512,2432]{1,0:T(8,128)(2,1)S(1)} %bitcast.112, bf16[2048,2432]{1,0:T(8,128)(2,1)S(1)} %copy-done), custom_call_target="tpu_custom_call" | custom-call | tf_op jit(solution)/shard_map/pallas_call | solution.py:195
  75.2 2.2 %shard_map.80 = (bf16[2,256,2432]{2,1,0:T(8,128)(2,1)S(1)}, f32[8,256]{1,0:T(8,128)S(1)}) custom-call(s32[8]{0:T(128)S(1)} %pad_add_fusion.at, f32[128,2432]{1,0:T(8,128)S(1)} %convert_add_fusion.first, f32[128,2432]{1,0:T(8,128)S(1)} %collective-permute-done.12.second, f32[1,2432]{1,0:T(1,128)S(1)} %add.417.row, f32[8,128]{1,0:T(8,128)S(1)} %get-tuple-element.45.sums_a, ...), custom_call_target="tpu_custom_call" | custom-call | tf_op jit(solution)/shard_map/pallas_call | solution.py:132
  79.1 9.7 %fusion.71 = f32[512,2048]{1,0:T(8,128)} fusion(bf16[512,2432]{1,0:T(8,128)(2,1)S(1)} %bitcast.116, bf16[2048,2432]{1,0:T(8,128)(2,1)} %head.3), kind=kOutput, calls=%fused_computation.220 | convolution fusion | flops 5100273664 | bytes 16646144 | tf_op jit(solution)/shard_map/dot_general | solution.py:329
  92.4 2.0 %collective-permute-done.16 = f32[4,512]{1,0:T(4,128)S(1)} collective-permute-done((f32[4,512]{1,0:T(4,128)S(1)}, f32[4,512]{1,0:T(4,128)S(1)}, u32[]{:S(2)}, u32[]{:S(2)}) %collective-permute-start.16) | collective-permute-done | bytes 8224 | tf_op jit(solution)/shard_map/ppermute | solution.py:31
  94.4 2.8 %collective-permute-start.17 = (f32[4,512]{1,0:T(4,128)S(1)}, f32[4,512]{1,0:T(4,128)S(1)}, u32[]{:S(2)}, u32[]{:S(2)}) collective-permute-start(f32[4,512]{1,0:T(4,128)S(1)} %pad_maximum_fusion.8), channel_id=1, source_target_pairs={{0,4},{1,5},{2,6},{3,7},{4,0},{5,1},{6,2},{7,3},{8,12},{9,13},{10,... | collective-permute-start | bytes 24584 | tf_op jit(solution)/shard_map/ppermute | solution.py:31
  99.2 2.7 %multiply_add_fusion = f32[256,2048]{1,0:T(8,128)S(1)} fusion(f32[512,2048]{1,0:T(8,128)} %copy-done.2, f32[256]{0:T(256)S(1)} %mul.320, f32[256]{0:T(256)S(1)} %bitcast.142), kind=kLoop, calls=%fused_computation.7 | loop fusion | flops 1572864 | bytes 6293504 | tf_op jit(solution)/shard_map/add | solution.py:312
  108.3 3.8 %copy-done.1 = bf16[2048,2432]{1,0:T(8,128)(2,1)S(1)} copy-done((bf16[2048,2432]{1,0:T(8,128)(2,1)S(1)}, bf16[2048,2432]{1,0:T(8,128)(2,1)}, u32[]{:S(2)}) %copy-start.1) | copy-done | bytes 9961496
  112.2 7.1 %shard_map.82 = f32[512,2048]{1,0:T(8,128)S(1)} custom-call(bf16[512,2432]{1,0:T(8,128)(2,1)S(1)} %get-tuple-element.71.cotangent, bf16[2048,2432]{1,0:T(8,128)(2,1)S(1)} %copy-done.1), custom_call_target="tpu_custom_call" | custom-call | tf_op jit(solution)/shard_map/pallas_call | solution.py:195
  121.0 6.6 %collective-permute-done.21 = bf16[128,2048]{1,0:T(8,128)(2,1)S(1)} collective-permute-done((bf16[128,2048]{1,0:T(8,128)(2,1)S(1)}, bf16[128,2048]{1,0:T(8,128)(2,1)S(1)}, u32[]{:S(2)}, u32[]{:S(2)}) %collective-permute-start.21) | collective-permute-done | bytes 524320 | tf_op jit(solution)/shard_map/ppermute | solution.py:31
  131.6 10.2 %collective-permute-done.23 = bf16[2,64,2048]{2,1,0:T(8,128)(2,1)S(1)} collective-permute-done((bf16[2,64,2048]{2,1,0:T(8,128)(2,1)S(1)}, bf16[2,64,2048]{2,1,0:T(8,128)(2,1)S(1)}, u32[]{:S(2)}, u32[]{:S(2)}) %collective-permute-start.23) | collective-permute-done | bytes 524320 | tf_op jit(solution)/shard_map/ppermute | solution.py:31
  144.0 2.6 %collective-permute-start.25 = (bf16[1,64,2048]{2,1,0:T(8,128)(2,1)}, bf16[1,64,2048]{2,1,0:T(8,128)(2,1)S(1)}, u32[]{:S(2)}, u32[]{:S(2)}) collective-permute-start(bf16[1,64,2048]{2,1,0:T(8,128)(2,1)} %dynamic-slice_convert_fusion), channel_id=1, source_target_pairs={{0,4},{1,5},{2,6},{3,7},{4,0},{5,1},{6,2},{7,3},{8,12},{9,13},{10,... | collective-permute-start | bytes 786440 | tf_op jit(solution)/shard_map/ppermute | solution.py:31
  149.5 8.1 %collective-permute-done.25 = bf16[1,64,2048]{2,1,0:T(8,128)(2,1)S(1)} collective-permute-done((bf16[1,64,2048]{2,1,0:T(8,128)(2,1)}, bf16[1,64,2048]{2,1,0:T(8,128)(2,1)S(1)}, u32[]{:S(2)}, u32[]{:S(2)}) %collective-permute-start.25) | collective-permute-done | bytes 262176 | tf_op jit(solution)/shard_map/ppermute | solution.py:31
  157.6 3.4 %collective-permute-done.26 = bf16[2,64,1024]{2,1,0:T(8,128)(2,1)} collective-permute-done((bf16[2,64,1024]{2,1,0:T(8,128)(2,1)}, bf16[2,64,1024]{2,1,0:T(8,128)(2,1)}, u32[]{:S(2)}, u32[]{:S(2)}) %collective-permute-start.26) | collective-permute-done | bytes 262176 | tf_op jit(solution)/shard_map/ppermute | solution.py:31
  163.7 7.9 %collective-permute-done.28 = bf16[1,64,1024]{2,1,0:T(8,128)(2,1)S(1)} collective-permute-done((bf16[1,64,1024]{2,1,0:T(8,128)(2,1)S(1)}, bf16[1,64,1024]{2,1,0:T(8,128)(2,1)S(1)}, u32[]{:S(2)}, u32[]{:S(2)}) %collective-permute-start.28) | collective-permute-done | bytes 131104 | tf_op jit(solution)/shard_map/ppermute | solution.py:31
  174.4 5.3 %collective-permute-done.30 = bf16[1,64,1024]{2,1,0:T(8,128)(2,1)S(1)} collective-permute-done((bf16[1,64,1024]{2,1,0:T(8,128)(2,1)S(1)}, bf16[1,64,1024]{2,1,0:T(8,128)(2,1)S(1)}, u32[]{:S(2)}, u32[]{:S(2)}) %collective-permute-start.30) | collective-permute-done | bytes 131104 | tf_op jit(solution)/shard_map/ppermute | solution.py:31
  (178 shorter events, 58.3 us)
Async XLA Ops:
  4.7 18.0 %collective-permute-start.7 = (bf16[128,2048]{1,0:T(8,128)(2,1)S(1)}, bf16[128,2048]{1,0:T(8,128)(2,1)S(1)}, u32[]{:S(2)}, u32[]{:S(2)}) collective-permute-start(bf16[128,2048]{1,0:T(8,128)(2,1)S(1)} %get-tuple-element.52), channel_id=1, source_target_pairs={{0,24},{8,16},{16,8},{24,0},{1,25},{9,17},{17,9},{25,1},{2,26},{10... | collective-permute-start | bytes 1572872 | tf_op jit(solution)/shard_map/ppermute | solution.py:31
  13.1 7.0 %collective-permute-start.2 = (f32[128,2432]{1,0:T(8,128)S(1)}, f32[128,2432]{1,0:T(8,128)S(1)}, u32[]{:S(2)}, u32[]{:S(2)}) collective-permute-start(f32[128,2432]{1,0:T(8,128)S(1)} %fusion.2), channel_id=1, source_target_pairs={{0,8},{8,0},{16,24},{24,16},{1,9},{9,1},{17,25},{25,17},{2,10},{10... | collective-permute-start | bytes 3735560 | tf_op jit(solution)/shard_map/ppermute | solution.py:31
  16.3 3.7 %collective-permute-start.6 = (f32[1,2432]{1,0:T(1,128)S(1)}, f32[1,2432]{1,0:T(1,128)S(1)}, u32[]{:S(2)}, u32[]{:S(2)}) collective-permute-start(f32[1,2432]{1,0:T(1,128)S(1)} %reshape_add_fusion), channel_id=1, source_target_pairs={{0,16},{8,24},{16,0},{24,8},{1,17},{9,25},{17,1},{25,9},{2,18},{10... | collective-permute-start | bytes 29192 | tf_op jit(solution)/shard_map/ppermute | solution.py:31
  18.1 4.6 %collective-permute-start.4 = (f32[2,8,128]{2,1,0:T(8,128)S(1)}, f32[2,8,128]{2,1,0:T(8,128)S(1)}, u32[]{:S(2)}, u32[]{:S(2)}) collective-permute-start(f32[2,8,128]{2,1,0:T(8,128)S(1)} %pad_maximum_fusion.5), channel_id=1, source_target_pairs={{0,16},{8,24},{16,0},{24,8},{1,17},{9,25},{17,1},{25,9},{2,18},{10... | collective-permute-start | bytes 24584 | tf_op jit(solution)/shard_map/ppermute | solution.py:31
  24.4 15.1 %collective-permute-start.8 = (f32[128,2432]{1,0:T(8,128)S(1)}, f32[128,2432]{1,0:T(8,128)S(1)}, u32[]{:S(2)}, u32[]{:S(2)}) collective-permute-start(f32[128,2432]{1,0:T(8,128)S(1)} %fusion.3), channel_id=1, source_target_pairs={{0,8},{8,0},{16,24},{24,16},{1,9},{9,1},{17,25},{25,17},{2,10},{10... | collective-permute-start | bytes 3735560 | tf_op jit(solution)/shard_map/ppermute | solution.py:31
  24.5 15.0 %collective-permute-start.3 = (bf16[128,2048]{1,0:T(8,128)(2,1)S(1)}, bf16[128,2048]{1,0:T(8,128)(2,1)S(1)}, u32[]{:S(2)}, u32[]{:S(2)}) collective-permute-start(bf16[128,2048]{1,0:T(8,128)(2,1)S(1)} %get-tuple-element.49), channel_id=1, source_target_pairs={{0,16},{8,24},{16,0},{24,8},{1,17},{9,25},{17,1},{25,9},{2,18},{10... | collective-permute-start | bytes 1572872 | tf_op jit(solution)/shard_map/ppermute | solution.py:31
  26.7 25.9 %collective-permute-start.9 = (f16[128,2432]{1,0:T(8,128)(2,1)S(1)}, f16[128,2432]{1,0:T(8,128)(2,1)S(1)}, u32[]{:S(2)}, u32[]{:S(2)}) collective-permute-start(f16[128,2432]{1,0:T(8,128)(2,1)S(1)} %get-tuple-element.53), channel_id=1, source_target_pairs={{0,16},{8,24},{16,0},{24,8},{1,17},{9,25},{17,1},{25,9},{2,18},{10... | collective-permute-start | bytes 1867784 | tf_op jit(solution)/shard_map/ppermute | solution.py:31
  52.7 18.1 %collective-permute-start.10 = (f16[128,2432]{1,0:T(8,128)(2,1)}, f16[128,2432]{1,0:T(8,128)(2,1)}, u32[]{:S(2)}, u32[]{:S(2)}) collective-permute-start(f16[128,2432]{1,0:T(8,128)(2,1)} %get-tuple-element.54), channel_id=1, source_target_pairs={{0,16},{8,24},{16,0},{24,8},{1,17},{9,25},{17,1},{25,9},{2,18},{10... | collective-permute-start | bytes 1867784 | tf_op jit(solution)/shard_map/ppermute | solution.py:31
  72.5 16.4 %collective-permute-start.15 = (bf16[128,2432]{1,0:T(8,128)(2,1)S(1)}, bf16[128,2432]{1,0:T(8,128)(2,1)S(1)}, u32[]{:S(2)}, u32[]{:S(2)}) collective-permute-start(bf16[128,2432]{1,0:T(8,128)(2,1)S(1)} %copy-done.4), channel_id=1, source_target_pairs={{0,16},{8,24},{16,0},{24,8},{1,17},{9,25},{17,1},{25,9},{2,18},{10... | collective-permute-start | bytes 1867784 | tf_op jit(solution)/shard_map/ppermute | solution.py:31
  74.2 14.6 %collective-permute-start.14 = (bf16[128,2432]{1,0:T(8,128)(2,1)S(1)}, bf16[128,2432]{1,0:T(8,128)(2,1)S(1)}, u32[]{:S(2)}, u32[]{:S(2)}) collective-permute-start(bf16[128,2432]{1,0:T(8,128)(2,1)S(1)} %copy-done.4), channel_id=1, source_target_pairs={{0,8},{8,0},{16,24},{24,16},{1,9},{9,1},{17,25},{25,17},{2,10},{10... | collective-permute-start | bytes 1867784 | tf_op jit(solution)/shard_map/ppermute | solution.py:31
  77.4 13.2 %collective-permute-start.13 = (f32[4,512]{1,0:T(4,128)S(1)}, f32[4,512]{1,0:T(4,128)S(1)}, u32[]{:S(2)}, u32[]{:S(2)}) collective-permute-start(f32[4,512]{1,0:T(4,128)S(1)} %pad_maximum_fusion.6), channel_id=1, source_target_pairs={{0,1},{1,0},{2,3},{3,2},{4,5},{5,4},{6,7},{7,6},{8,9},{9,8},{10,11... | collective-permute-start | bytes 24584 | tf_op jit(solution)/shard_map/ppermute | solution.py:31
  94.4 4.6 %collective-permute-start.17 = (f32[4,512]{1,0:T(4,128)S(1)}, f32[4,512]{1,0:T(4,128)S(1)}, u32[]{:S(2)}, u32[]{:S(2)}) collective-permute-start(f32[4,512]{1,0:T(4,128)S(1)} %pad_maximum_fusion.8), channel_id=1, source_target_pairs={{0,4},{1,5},{2,6},{3,7},{4,0},{5,1},{6,2},{7,3},{8,12},{9,13},{10,... | collective-permute-start | bytes 24584 | tf_op jit(solution)/shard_map/ppermute | solution.py:31
  97.3 10.2 %collective-permute-start.18 = (bf16[128,2432]{1,0:T(8,128)(2,1)}, bf16[128,2432]{1,0:T(8,128)(2,1)S(1)}, u32[]{:S(2)}, u32[]{:S(2)}) collective-permute-start(bf16[128,2432]{1,0:T(8,128)(2,1)} %copy-done.6), channel_id=1, source_target_pairs={{0,8},{8,0},{16,24},{24,16},{1,9},{9,1},{17,25},{25,17},{2,10},{10... | collective-permute-start | bytes 1867784 | tf_op jit(solution)/shard_map/ppermute | solution.py:31
  99.1 4.6 %collective-permute-start.19 = (f32[8,128]{1,0:T(8,128)S(1)}, f32[8,128]{1,0:T(8,128)S(1)}, u32[]{:S(2)}, u32[]{:S(2)}) collective-permute-start(f32[8,128]{1,0:T(8,128)S(1)} %broadcast_in_dim.11.refs_4_), channel_id=1, source_target_pairs={{0,8},{8,0},{16,24},{24,16},{1,9},{9,1},{17,25},{25,17},{2,10},{10... | collective-permute-start | bytes 12296 | tf_op jit(solution)/shard_map/ppermute | solution.py:31
  102.0 19.0 %collective-permute-start.22 = (bf16[128,2048]{1,0:T(8,128)(2,1)S(1)}, bf16[128,2048]{1,0:T(8,128)(2,1)S(1)}, u32[]{:S(2)}, u32[]{:S(2)}) collective-permute-start(bf16[128,2048]{1,0:T(8,128)(2,1)S(1)} %slice.415), channel_id=1, source_target_pairs={{0,1},{1,0},{2,3},{3,2},{4,5},{5,4},{6,7},{7,6},{8,9},{9,8},{10,11... | collective-permute-start | bytes 1572872 | tf_op jit(solution)/shard_map/ppermute | solution.py:31
  105.7 21.9 %collective-permute-start.21 = (bf16[128,2048]{1,0:T(8,128)(2,1)S(1)}, bf16[128,2048]{1,0:T(8,128)(2,1)S(1)}, u32[]{:S(2)}, u32[]{:S(2)}) collective-permute-start(bf16[128,2048]{1,0:T(8,128)(2,1)S(1)} %slice.416), channel_id=1, source_target_pairs={{0,1},{1,0},{2,3},{3,2},{4,5},{5,4},{6,7},{7,6},{8,9},{9,8},{10,11... | collective-permute-start | bytes 1572872 | tf_op jit(solution)/shard_map/ppermute | solution.py:31
  128.1 13.6 %collective-permute-start.23 = (bf16[2,64,2048]{2,1,0:T(8,128)(2,1)S(1)}, bf16[2,64,2048]{2,1,0:T(8,128)(2,1)S(1)}, u32[]{:S(2)}, u32[]{:S(2)}) collective-permute-start(bf16[2,64,2048]{2,1,0:T(8,128)(2,1)S(1)} %fusion.4), channel_id=1, source_target_pairs={{0,2},{1,3},{2,0},{3,1},{4,6},{5,7},{6,4},{7,5},{8,10},{9,11},{10,... | collective-permute-start | bytes 1572872 | tf_op jit(solution)/shard_map/ppermute | solution.py:31
  129.9 13.3 %collective-permute-start.24 = (bf16[256,1024]{1,0:T(8,128)(2,1)S(1)}, bf16[256,1024]{1,0:T(8,128)(2,1)S(1)}, u32[]{:S(2)}, u32[]{:S(2)}) collective-permute-start(bf16[256,1024]{1,0:T(8,128)(2,1)S(1)} %pad_maximum_fusion.1), channel_id=1, source_target_pairs={{0,1},{1,0},{2,3},{3,2},{4,5},{5,4},{6,7},{7,6},{8,9},{9,8},{10,11... | collective-permute-start | bytes 1572872 | tf_op jit(solution)/shard_map/ppermute | solution.py:31
  144.0 13.6 %collective-permute-start.25 = (bf16[1,64,2048]{2,1,0:T(8,128)(2,1)}, bf16[1,64,2048]{2,1,0:T(8,128)(2,1)S(1)}, u32[]{:S(2)}, u32[]{:S(2)}) collective-permute-start(bf16[1,64,2048]{2,1,0:T(8,128)(2,1)} %dynamic-slice_convert_fusion), channel_id=1, source_target_pairs={{0,4},{1,5},{2,6},{3,7},{4,0},{5,1},{6,2},{7,3},{8,12},{9,13},{10,... | collective-permute-start | bytes 786440 | tf_op jit(solution)/shard_map/ppermute | solution.py:31
  146.6 14.4 %collective-permute-start.27 = (bf16[256,1024]{1,0:T(8,128)(2,1)}, bf16[256,1024]{1,0:T(8,128)(2,1)}, u32[]{:S(2)}, u32[]{:S(2)}) collective-permute-start(bf16[256,1024]{1,0:T(8,128)(2,1)} %pad_maximum_fusion.2), channel_id=1, source_target_pairs={{0,1},{1,0},{2,3},{3,2},{4,5},{5,4},{6,7},{7,6},{8,9},{9,8},{10,11... | collective-permute-start | bytes 1572872 | tf_op jit(solution)/shard_map/ppermute | solution.py:31
  149.0 12.0 %collective-permute-start.26 = (bf16[2,64,1024]{2,1,0:T(8,128)(2,1)}, bf16[2,64,1024]{2,1,0:T(8,128)(2,1)}, u32[]{:S(2)}, u32[]{:S(2)}) collective-permute-start(bf16[2,64,1024]{2,1,0:T(8,128)(2,1)} %fusion.17), channel_id=1, source_target_pairs={{0,2},{1,3},{2,0},{3,1},{4,6},{5,7},{6,4},{7,5},{8,10},{9,11},{10,... | collective-permute-start | bytes 786440 | tf_op jit(solution)/shard_map/ppermute | solution.py:31
  163.3 9.6 %collective-permute-start.29 = (bf16[2,64,1024]{2,1,0:T(8,128)(2,1)S(1)}, bf16[2,64,1024]{2,1,0:T(8,128)(2,1)S(1)}, u32[]{:S(2)}, u32[]{:S(2)}) collective-permute-start(bf16[2,64,1024]{2,1,0:T(8,128)(2,1)S(1)} %fusion.18), channel_id=1, source_target_pairs={{0,2},{1,3},{2,0},{3,1},{4,6},{5,7},{6,4},{7,5},{8,10},{9,11},{10,... | collective-permute-start | bytes 786440 | tf_op jit(solution)/shard_map/ppermute | solution.py:31
  163.4 8.2 %collective-permute-start.28 = (bf16[1,64,1024]{2,1,0:T(8,128)(2,1)S(1)}, bf16[1,64,1024]{2,1,0:T(8,128)(2,1)S(1)}, u32[]{:S(2)}, u32[]{:S(2)}) collective-permute-start(bf16[1,64,1024]{2,1,0:T(8,128)(2,1)S(1)} %dynamic-slice_convert_fusion.2), channel_id=1, source_target_pairs={{0,4},{1,5},{2,6},{3,7},{4,0},{5,1},{6,2},{7,3},{8,12},{9,13},{10,... | collective-permute-start | bytes 393224 | tf_op jit(solution)/shard_map/ppermute | solution.py:31
  173.0 6.7 %collective-permute-start.30 = (bf16[1,64,1024]{2,1,0:T(8,128)(2,1)S(1)}, bf16[1,64,1024]{2,1,0:T(8,128)(2,1)S(1)}, u32[]{:S(2)}, u32[]{:S(2)}) collective-permute-start(bf16[1,64,1024]{2,1,0:T(8,128)(2,1)S(1)} %dynamic-slice_convert_fusion.1), channel_id=1, source_target_pairs={{0,4},{1,5},{2,6},{3,7},{4,0},{5,1},{6,2},{7,3},{8,12},{9,13},{10,... | collective-permute-start | bytes 393224 | tf_op jit(solution)/shard_map/ppermute | solution.py:31
  (32 other events, 174.9 us)

commit v9 on v8

--- a/solution.py
+++ b/solution.py
@@ -392,7 +392,9 @@
         ]
         got = [swap(items[i][1], "vocab", bits[items[i][0]], vocab_size) for i in active]
         waiting = [i for i, item in enumerate(items) if i not in active and item[0] == 0]
-        tied = lax.optimization_barrier((got, [items[i][1] for i in waiting]))
+        tied = (got, [])
+        if waiting:
+            tied = lax.optimization_barrier((got, [items[i][1] for i in waiting]))
         for i, value in zip(waiting, tied[1]):
             items[i][1] = value
         for i, value in zip(active, tied[0]):

time: 186 us -> 182 us (0.978)
  other arithmetic: 12.3 us -> 9.59 us
    add x5, other arithmetic: 2.54 us -> 0.61 us  [body(): joined = kept + value.astype(F32)]
  transfers between devices with their start and end apart: 33 -> 33, of which waited for: 19 -> 19; matrix products, arithmetic and copies ran while one was open for 15% -> 15% of each run, Pallas kernels for 10% -> 11%
where the time goes in v9:
time: 182 us; the launch traced here: 181 us
  waiting for transfers between devices  79.5 us (44%)
  starting transfers between devices  33 us (18%)
  matrix products  23.6 us (13%)
  Pallas kernels  20.5 us (11%)
  local copies, waits for them, and re-layouts  13.8 us (8%)
  other arithmetic  9.59 us (5%)
    ppermute x33, waiting for transfers between devices, swap(): return lax.ppermute(value, axis, [(i, i ^ bit) for i in range(size)])  79.5 us
    ppermute x33, starting transfers between devices, swap(): return lax.ppermute(value, axis, [(i, i ^ bit) for i in range(size)])  33 us
    pallas_call x2, Pallas kernels, back(): pl.pallas_call(functools.partial(back_kernel, deep), grid=(features // ti...  14.3 us
    unnamed x46, local copies, waits for them, and re-layouts  13 us
    dot_general x4, matrix products, partial_logits(): return jnp.dot(normed, head, preferred_element_type=F32)  12.4 us
    dot_general x1, matrix products, body(): lax.dot_general(both_own, head, NT, preferred_element_type=F32)  9.86 us
    pallas_call x2, Pallas kernels, soften(): pl.pallas_call(functools.partial(soften_kernel, feature_count), in_specs=...  4.41 us
  transfers between devices with their start and end apart: 33, of which 19 were waited for; matrix products, arithmetic and copies ran while one was open for 15% of the time, Pallas kernels for 11%

profile of v9, /device:TPU:0, one launch (start us, length us, event | category | flops | bytes accessed | tf_op | source)
XLA Modules:
  0.0 181.3 jit_solution(8143530712731125492)
XLA Ops:
  4.7 2.6 %collective-permute-start.7 = (bf16[128,2048]{1,0:T(8,128)(2,1)S(1)}, bf16[128,2048]{1,0:T(8,128)(2,1)S(1)}, u32[]{:S(2)}, u32[]{:S(2)}) collective-permute-start(bf16[128,2048]{1,0:T(8,128)(2,1)S(1)} %get-tuple-element.47), channel_id=1, source_target_pairs={{0,24},{8,16},{16,8},{24,0},{1,25},{9,17},{17,9},{25,1},{2,26},{10... | collective-permute-start | bytes 1572872 | tf_op jit(solution)/shard_map/ppermute | solution.py:31
  7.4 5.6 %fusion.2 = f32[128,2432]{1,0:T(8,128)S(1)} fusion(bf16[2048,2432]{1,0:T(8,128)(2,1)} %head.3, bf16[128,2048]{1,0:T(8,128)(2,1)S(1)} %collective-permute-done, f32[128]{0:T(128)S(1)} %get-tuple-element.132, f32[2048]{0:T(1024)S(1)} %bitcast.129, f32[2048]{0:T(1024)S(1)} %bitcast.123), kind=kOutput, calls=%fused_computation.25 | convolution fusion | flops 1276379136 | bytes 11747840 | tf_op jit(solution)/shard_map/dot_general | solution.py:277
  20.1 2.7 %fusion.69 = (f16[128,2432]{1,0:T(8,128)(2,1)S(1)}, f32[128,2432]{1,0:T(8,128)}) fusion(f32[128,2432]{1,0:T(8,128)S(1)} %collective-permute-done.2, bf16[2048,2432]{1,0:T(8,128)(2,1)S(1)} %bitcast.111, bf16[128,2048]{1,0:T(8,128)(2,1)S(1)} %get-tuple-element.39, f32[128]{0:T(128)S(1)} %get-tuple-element.130, f32[2048]{0:T(1024)S(1)} %bitcast.130, ...), kind=kOutput, calls=%fused_computation.218 | convolution fusion | flops 1277001728 | bytes 13615616 | tf_op jit(solution)/shard_map/dot_general | solution.py:277
  24.5 2.2 %collective-permute-start.3 = (bf16[128,2048]{1,0:T(8,128)(2,1)S(1)}, bf16[128,2048]{1,0:T(8,128)(2,1)S(1)}, u32[]{:S(2)}, u32[]{:S(2)}) collective-permute-start(bf16[128,2048]{1,0:T(8,128)(2,1)S(1)} %get-tuple-element.44), channel_id=1, source_target_pairs={{0,16},{8,24},{16,0},{24,8},{1,17},{9,25},{17,1},{25,9},{2,18},{10... | collective-permute-start | bytes 1572872 | tf_op jit(solution)/shard_map/ppermute | solution.py:31
  26.8 12.7 %collective-permute-done.3 = bf16[128,2048]{1,0:T(8,128)(2,1)S(1)} collective-permute-done((bf16[128,2048]{1,0:T(8,128)(2,1)S(1)}, bf16[128,2048]{1,0:T(8,128)(2,1)S(1)}, u32[]{:S(2)}, u32[]{:S(2)}) %collective-permute-start.3) | collective-permute-done | bytes 524320 | tf_op jit(solution)/shard_map/ppermute | solution.py:31
  39.5 2.4 %fusion.70 = (f16[128,2432]{1,0:T(8,128)(2,1)}, f32[128,2432]{1,0:T(8,128)S(1)}) fusion(f32[128,2432]{1,0:T(8,128)S(1)} %collective-permute-done.8, bf16[2048,2432]{1,0:T(8,128)(2,1)S(1)} %bitcast.111, bf16[128,2048]{1,0:T(8,128)(2,1)S(1)} %collective-permute-done.3, f32[128]{0:T(128)S(1)} %get-tuple-element.113, f32[2048]{0:T(1024)S(1)} %bitcast.132, ...), kind=kOutput, calls=%fused_computation.219 | convolution fusion | flops 1277001728 | bytes 13615616 | tf_op jit(solution)/shard_map/dot_general | solution.py:277
  41.9 10.7 %collective-permute-done.9 = f16[128,2432]{1,0:T(8,128)(2,1)S(1)} collective-permute-done((f16[128,2432]{1,0:T(8,128)(2,1)S(1)}, f16[128,2432]{1,0:T(8,128)(2,1)S(1)}, u32[]{:S(2)}, u32[]{:S(2)}) %collective-permute-start.9) | collective-permute-done | bytes 622624 | tf_op jit(solution)/shard_map/ppermute | solution.py:31
  55.7 2.2 %shard_map.78 = (bf16[2,256,2432]{2,1,0:T(8,128)(2,1)S(1)}, f32[8,256]{1,0:T(8,128)S(1)}) custom-call(s32[8]{0:T(128)S(1)} %pad_add_fusion.1.at, f32[128,2432]{1,0:T(8,128)S(1)} %convert_add_fusion.1.first, f32[128,2432]{1,0:T(8,128)S(1)} %collective-permute-done.11.second, f32[1,2432]{1,0:T(1,128)S(1)} %add.417.row, ...), custom_call_target="tpu_custom_call" | custom-call | tf_op jit(solution)/shard_map/pallas_call | solution.py:132
  57.9 3.8 %copy-done = bf16[2048,2432]{1,0:T(8,128)(2,1)S(1)} copy-done((bf16[2048,2432]{1,0:T(8,128)(2,1)S(1)}, bf16[2048,2432]{1,0:T(8,128)(2,1)}, u32[]{:S(2)}) %copy-start) | copy-done | bytes 9961496
  61.7 7.2 %shard_map.79 = f32[512,2048]{1,0:T(8,128)S(1)} custom-call(bf16[512,2432]{1,0:T(8,128)(2,1)S(1)} %bitcast.112, bf16[2048,2432]{1,0:T(8,128)(2,1)S(1)} %copy-done), custom_call_target="tpu_custom_call" | custom-call | tf_op jit(solution)/shard_map/pallas_call | solution.py:195
  75.2 2.2 %shard_map.80 = (bf16[2,256,2432]{2,1,0:T(8,128)(2,1)S(1)}, f32[8,256]{1,0:T(8,128)S(1)}) custom-call(s32[8]{0:T(128)S(1)} %pad_add_fusion.at, f32[128,2432]{1,0:T(8,128)S(1)} %convert_add_fusion.first, f32[128,2432]{1,0:T(8,128)S(1)} %collective-permute-done.12.second, f32[1,2432]{1,0:T(1,128)S(1)} %add.417.row, f32[8,128]{1,0:T(8,128)S(1)} %get-tuple-element.40.sums_a, ...), custom_call_target="tpu_custom_call" | custom-call | tf_op jit(solution)/shard_map/pallas_call | solution.py:132
  79.2 9.9 %fusion.71 = f32[512,2048]{1,0:T(8,128)} fusion(bf16[512,2432]{1,0:T(8,128)(2,1)S(1)} %bitcast.116, bf16[2048,2432]{1,0:T(8,128)(2,1)} %head.3), kind=kOutput, calls=%fused_computation.220 | convolution fusion | flops 5100273664 | bytes 16646144 | tf_op jit(solution)/shard_map/dot_general | solution.py:329
  94.6 2.6 %collective-permute-start.17 = (f32[4,512]{1,0:T(4,128)S(1)}, f32[4,512]{1,0:T(4,128)S(1)}, u32[]{:S(2)}, u32[]{:S(2)}) collective-permute-start(f32[4,512]{1,0:T(4,128)S(1)} %pad_maximum_fusion.8), channel_id=1, source_target_pairs={{0,4},{1,5},{2,6},{3,7},{4,0},{5,1},{6,2},{7,3},{8,12},{9,13},{10,... | collective-permute-start | bytes 24584 | tf_op jit(solution)/shard_map/ppermute | solution.py:31
  99.4 2.7 %multiply_add_fusion = f32[256,2048]{1,0:T(8,128)S(1)} fusion(f32[512,2048]{1,0:T(8,128)} %copy-done.2, f32[256]{0:T(256)S(1)} %mul.320, f32[256]{0:T(256)S(1)} %bitcast.142), kind=kLoop, calls=%fused_computation.7 | loop fusion | flops 1572864 | bytes 6293504 | tf_op jit(solution)/shard_map/add | solution.py:312
  108.4 3.8 %copy-done.1 = bf16[2048,2432]{1,0:T(8,128)(2,1)S(1)} copy-done((bf16[2048,2432]{1,0:T(8,128)(2,1)S(1)}, bf16[2048,2432]{1,0:T(8,128)(2,1)}, u32[]{:S(2)}) %copy-start.1) | copy-done | bytes 9961496
  112.2 7.1 %shard_map.82 = f32[512,2048]{1,0:T(8,128)S(1)} custom-call(bf16[512,2432]{1,0:T(8,128)(2,1)S(1)} %get-tuple-element.66.cotangent, bf16[2048,2432]{1,0:T(8,128)(2,1)S(1)} %copy-done.1), custom_call_target="tpu_custom_call" | custom-call | tf_op jit(solution)/shard_map/pallas_call | solution.py:195
  120.2 7.6 %collective-permute-done.21 = bf16[128,2048]{1,0:T(8,128)(2,1)S(1)} collective-permute-done((bf16[128,2048]{1,0:T(8,128)(2,1)S(1)}, bf16[128,2048]{1,0:T(8,128)(2,1)S(1)}, u32[]{:S(2)}, u32[]{:S(2)}) %collective-permute-start.21) | collective-permute-done | bytes 524320 | tf_op jit(solution)/shard_map/ppermute | solution.py:31
  131.6 10.4 %collective-permute-done.23 = bf16[2,64,2048]{2,1,0:T(8,128)(2,1)S(1)} collective-permute-done((bf16[2,64,2048]{2,1,0:T(8,128)(2,1)S(1)}, bf16[2,64,2048]{2,1,0:T(8,128)(2,1)S(1)}, u32[]{:S(2)}, u32[]{:S(2)}) %collective-permute-start.23) | collective-permute-done | bytes 524320 | tf_op jit(solution)/shard_map/ppermute | solution.py:31
  144.9 2.7 %collective-permute-start.30 = (bf16[1,64,2048]{2,1,0:T(8,128)(2,1)S(1)}, bf16[1,64,2048]{2,1,0:T(8,128)(2,1)S(1)}, u32[]{:S(2)}, u32[]{:S(2)}) collective-permute-start(bf16[1,64,2048]{2,1,0:T(8,128)(2,1)S(1)} %dynamic-slice_convert_fusion), channel_id=1, source_target_pairs={{0,4},{1,5},{2,6},{3,7},{4,0},{5,1},{6,2},{7,3},{8,12},{9,13},{10,... | collective-permute-start | bytes 786440 | tf_op jit(solution)/shard_map/ppermute | solution.py:31
  148.3 7.3 %collective-permute-done.27 = bf16[256,1024]{1,0:T(8,128)(2,1)S(1)} collective-permute-done((bf16[256,1024]{1,0:T(8,128)(2,1)S(1)}, bf16[256,1024]{1,0:T(8,128)(2,1)S(1)}, u32[]{:S(2)}, u32[]{:S(2)}) %collective-permute-start.27) | collective-permute-done | bytes 524320 | tf_op jit(solution)/shard_map/ppermute | solution.py:31
  156.5 5.8 %collective-permute-done.25 = bf16[2,64,1024]{2,1,0:T(8,128)(2,1)S(1)} collective-permute-done((bf16[2,64,1024]{2,1,0:T(8,128)(2,1)S(1)}, bf16[2,64,1024]{2,1,0:T(8,128)(2,1)S(1)}, u32[]{:S(2)}, u32[]{:S(2)}) %collective-permute-start.25) | collective-permute-done | bytes 262176 | tf_op jit(solution)/shard_map/ppermute | solution.py:31
  162.5 4.0 %collective-permute-done.28 = bf16[2,64,1024]{2,1,0:T(8,128)(2,1)S(1)} collective-permute-done((bf16[2,64,1024]{2,1,0:T(8,128)(2,1)S(1)}, bf16[2,64,1024]{2,1,0:T(8,128)(2,1)S(1)}, u32[]{:S(2)}, u32[]{:S(2)}) %collective-permute-start.28) | collective-permute-done | bytes 262176 | tf_op jit(solution)/shard_map/ppermute | solution.py:31
  167.2 2.4 %collective-permute-done.26 = bf16[1,64,1024]{2,1,0:T(8,128)(2,1)S(1)} collective-permute-done((bf16[1,64,1024]{2,1,0:T(8,128)(2,1)S(1)}, bf16[1,64,1024]{2,1,0:T(8,128)(2,1)S(1)}, u32[]{:S(2)}, u32[]{:S(2)}) %collective-permute-start.26) | collective-permute-done | bytes 131104 | tf_op jit(solution)/shard_map/ppermute | solution.py:31
  169.7 5.2 %collective-permute-done.29 = bf16[1,64,1024]{2,1,0:T(8,128)(2,1)S(1)} collective-permute-done((bf16[1,64,1024]{2,1,0:T(8,128)(2,1)S(1)}, bf16[1,64,1024]{2,1,0:T(8,128)(2,1)S(1)}, u32[]{:S(2)}, u32[]{:S(2)}) %collective-permute-start.29) | collective-permute-done | bytes 131104 | tf_op jit(solution)/shard_map/ppermute | solution.py:31
  (178 shorter events, 54.0 us)
Async XLA Ops:
  4.7 18.1 %collective-permute-start.7 = (bf16[128,2048]{1,0:T(8,128)(2,1)S(1)}, bf16[128,2048]{1,0:T(8,128)(2,1)S(1)}, u32[]{:S(2)}, u32[]{:S(2)}) collective-permute-start(bf16[128,2048]{1,0:T(8,128)(2,1)S(1)} %get-tuple-element.47), channel_id=1, source_target_pairs={{0,24},{8,16},{16,8},{24,0},{1,25},{9,17},{17,9},{25,1},{2,26},{10... | collective-permute-start | bytes 1572872 | tf_op jit(solution)/shard_map/ppermute | solution.py:31
  13.1 7.0 %collective-permute-start.2 = (f32[128,2432]{1,0:T(8,128)S(1)}, f32[128,2432]{1,0:T(8,128)S(1)}, u32[]{:S(2)}, u32[]{:S(2)}) collective-permute-start(f32[128,2432]{1,0:T(8,128)S(1)} %fusion.2), channel_id=1, source_target_pairs={{0,8},{8,0},{16,24},{24,16},{1,9},{9,1},{17,25},{25,17},{2,10},{10... | collective-permute-start | bytes 3735560 | tf_op jit(solution)/shard_map/ppermute | solution.py:31
  16.3 3.7 %collective-permute-start.6 = (f32[1,2432]{1,0:T(1,128)S(1)}, f32[1,2432]{1,0:T(1,128)S(1)}, u32[]{:S(2)}, u32[]{:S(2)}) collective-permute-start(f32[1,2432]{1,0:T(1,128)S(1)} %reshape_add_fusion), channel_id=1, source_target_pairs={{0,16},{8,24},{16,0},{24,8},{1,17},{9,25},{17,1},{25,9},{2,18},{10... | collective-permute-start | bytes 29192 | tf_op jit(solution)/shard_map/ppermute | solution.py:31
  18.1 4.7 %collective-permute-start.4 = (f32[2,8,128]{2,1,0:T(8,128)S(1)}, f32[2,8,128]{2,1,0:T(8,128)S(1)}, u32[]{:S(2)}, u32[]{:S(2)}) collective-permute-start(f32[2,8,128]{2,1,0:T(8,128)S(1)} %pad_maximum_fusion.5), channel_id=1, source_target_pairs={{0,16},{8,24},{16,0},{24,8},{1,17},{9,25},{17,1},{25,9},{2,18},{10... | collective-permute-start | bytes 24584 | tf_op jit(solution)/shard_map/ppermute | solution.py:31
  24.4 15.1 %collective-permute-start.8 = (f32[128,2432]{1,0:T(8,128)S(1)}, f32[128,2432]{1,0:T(8,128)S(1)}, u32[]{:S(2)}, u32[]{:S(2)}) collective-permute-start(f32[128,2432]{1,0:T(8,128)S(1)} %fusion.3), channel_id=1, source_target_pairs={{0,8},{8,0},{16,24},{24,16},{1,9},{9,1},{17,25},{25,17},{2,10},{10... | collective-permute-start | bytes 3735560 | tf_op jit(solution)/shard_map/ppermute | solution.py:31
  24.5 15.0 %collective-permute-start.3 = (bf16[128,2048]{1,0:T(8,128)(2,1)S(1)}, bf16[128,2048]{1,0:T(8,128)(2,1)S(1)}, u32[]{:S(2)}, u32[]{:S(2)}) collective-permute-start(bf16[128,2048]{1,0:T(8,128)(2,1)S(1)} %get-tuple-element.44), channel_id=1, source_target_pairs={{0,16},{8,24},{16,0},{24,8},{1,17},{9,25},{17,1},{25,9},{2,18},{10... | collective-permute-start | bytes 1572872 | tf_op jit(solution)/shard_map/ppermute | solution.py:31
  26.7 25.9 %collective-permute-start.9 = (f16[128,2432]{1,0:T(8,128)(2,1)S(1)}, f16[128,2432]{1,0:T(8,128)(2,1)S(1)}, u32[]{:S(2)}, u32[]{:S(2)}) collective-permute-start(f16[128,2432]{1,0:T(8,128)(2,1)S(1)} %get-tuple-element.48), channel_id=1, source_target_pairs={{0,16},{8,24},{16,0},{24,8},{1,17},{9,25},{17,1},{25,9},{2,18},{10... | collective-permute-start | bytes 1867784 | tf_op jit(solution)/shard_map/ppermute | solution.py:31
  52.8 18.1 %collective-permute-start.10 = (f16[128,2432]{1,0:T(8,128)(2,1)}, f16[128,2432]{1,0:T(8,128)(2,1)}, u32[]{:S(2)}, u32[]{:S(2)}) collective-permute-start(f16[128,2432]{1,0:T(8,128)(2,1)} %get-tuple-element.49), channel_id=1, source_target_pairs={{0,16},{8,24},{16,0},{24,8},{1,17},{9,25},{17,1},{25,9},{2,18},{10... | collective-permute-start | bytes 1867784 | tf_op jit(solution)/shard_map/ppermute | solution.py:31
  72.5 16.6 %collective-permute-start.15 = (bf16[128,2432]{1,0:T(8,128)(2,1)S(1)}, bf16[128,2432]{1,0:T(8,128)(2,1)S(1)}, u32[]{:S(2)}, u32[]{:S(2)}) collective-permute-start(bf16[128,2432]{1,0:T(8,128)(2,1)S(1)} %copy-done.4), channel_id=1, source_target_pairs={{0,16},{8,24},{16,0},{24,8},{1,17},{9,25},{17,1},{25,9},{2,18},{10... | collective-permute-start | bytes 1867784 | tf_op jit(solution)/shard_map/ppermute | solution.py:31
  74.3 14.8 %collective-permute-start.14 = (bf16[128,2432]{1,0:T(8,128)(2,1)S(1)}, bf16[128,2432]{1,0:T(8,128)(2,1)S(1)}, u32[]{:S(2)}, u32[]{:S(2)}) collective-permute-start(bf16[128,2432]{1,0:T(8,128)(2,1)S(1)} %copy-done.4), channel_id=1, source_target_pairs={{0,8},{8,0},{16,24},{24,16},{1,9},{9,1},{17,25},{25,17},{2,10},{10... | collective-permute-start | bytes 1867784 | tf_op jit(solution)/shard_map/ppermute | solution.py:31
  77.4 13.3 %collective-permute-start.13 = (f32[4,512]{1,0:T(4,128)S(1)}, f32[4,512]{1,0:T(4,128)S(1)}, u32[]{:S(2)}, u32[]{:S(2)}) collective-permute-start(f32[4,512]{1,0:T(4,128)S(1)} %pad_maximum_fusion.6), channel_id=1, source_target_pairs={{0,1},{1,0},{2,3},{3,2},{4,5},{5,4},{6,7},{7,6},{8,9},{9,8},{10,11... | collective-permute-start | bytes 24584 | tf_op jit(solution)/shard_map/ppermute | solution.py:31
  94.6 4.6 %collective-permute-start.17 = (f32[4,512]{1,0:T(4,128)S(1)}, f32[4,512]{1,0:T(4,128)S(1)}, u32[]{:S(2)}, u32[]{:S(2)}) collective-permute-start(f32[4,512]{1,0:T(4,128)S(1)} %pad_maximum_fusion.8), channel_id=1, source_target_pairs={{0,4},{1,5},{2,6},{3,7},{4,0},{5,1},{6,2},{7,3},{8,12},{9,13},{10,... | collective-permute-start | bytes 24584 | tf_op jit(solution)/shard_map/ppermute | solution.py:31
  97.4 10.0 %collective-permute-start.18 = (bf16[128,2432]{1,0:T(8,128)(2,1)}, bf16[128,2432]{1,0:T(8,128)(2,1)S(1)}, u32[]{:S(2)}, u32[]{:S(2)}) collective-permute-start(bf16[128,2432]{1,0:T(8,128)(2,1)} %copy-done.6), channel_id=1, source_target_pairs={{0,8},{8,0},{16,24},{24,16},{1,9},{9,1},{17,25},{25,17},{2,10},{10... | collective-permute-start | bytes 1867784 | tf_op jit(solution)/shard_map/ppermute | solution.py:31
  99.3 4.4 %collective-permute-start.19 = (f32[8,128]{1,0:T(8,128)S(1)}, f32[8,128]{1,0:T(8,128)S(1)}, u32[]{:S(2)}, u32[]{:S(2)}) collective-permute-start(f32[8,128]{1,0:T(8,128)S(1)} %broadcast_in_dim.11.refs_4_), channel_id=1, source_target_pairs={{0,8},{8,0},{16,24},{24,16},{1,9},{9,1},{17,25},{25,17},{2,10},{10... | collective-permute-start | bytes 12296 | tf_op jit(solution)/shard_map/ppermute | solution.py:31
  102.2 18.0 %collective-permute-start.22 = (bf16[128,2048]{1,0:T(8,128)(2,1)S(1)}, bf16[128,2048]{1,0:T(8,128)(2,1)S(1)}, u32[]{:S(2)}, u32[]{:S(2)}) collective-permute-start(bf16[128,2048]{1,0:T(8,128)(2,1)S(1)} %slice.415), channel_id=1, source_target_pairs={{0,1},{1,0},{2,3},{3,2},{4,5},{5,4},{6,7},{7,6},{8,9},{9,8},{10,11... | collective-permute-start | bytes 1572872 | tf_op jit(solution)/shard_map/ppermute | solution.py:31
  105.8 22.0 %collective-permute-start.21 = (bf16[128,2048]{1,0:T(8,128)(2,1)S(1)}, bf16[128,2048]{1,0:T(8,128)(2,1)S(1)}, u32[]{:S(2)}, u32[]{:S(2)}) collective-permute-start(bf16[128,2048]{1,0:T(8,128)(2,1)S(1)} %slice.416), channel_id=1, source_target_pairs={{0,1},{1,0},{2,3},{3,2},{4,5},{5,4},{6,7},{7,6},{8,9},{9,8},{10,11... | collective-permute-start | bytes 1572872 | tf_op jit(solution)/shard_map/ppermute | solution.py:31
  128.3 13.6 %collective-permute-start.23 = (bf16[2,64,2048]{2,1,0:T(8,128)(2,1)S(1)}, bf16[2,64,2048]{2,1,0:T(8,128)(2,1)S(1)}, u32[]{:S(2)}, u32[]{:S(2)}) collective-permute-start(bf16[2,64,2048]{2,1,0:T(8,128)(2,1)S(1)} %fusion.4), channel_id=1, source_target_pairs={{0,2},{1,3},{2,0},{3,1},{4,6},{5,7},{6,4},{7,5},{8,10},{9,11},{10,... | collective-permute-start | bytes 1572872 | tf_op jit(solution)/shard_map/ppermute | solution.py:31
  130.0 13.3 %collective-permute-start.24 = (bf16[256,1024]{1,0:T(8,128)(2,1)S(1)}, bf16[256,1024]{1,0:T(8,128)(2,1)S(1)}, u32[]{:S(2)}, u32[]{:S(2)}) collective-permute-start(bf16[256,1024]{1,0:T(8,128)(2,1)S(1)} %pad_maximum_fusion.1), channel_id=1, source_target_pairs={{0,1},{1,0},{2,3},{3,2},{4,5},{5,4},{6,7},{7,6},{8,9},{9,8},{10,11... | collective-permute-start | bytes 1572872 | tf_op jit(solution)/shard_map/ppermute | solution.py:31
  143.2 12.3 %collective-permute-start.27 = (bf16[256,1024]{1,0:T(8,128)(2,1)S(1)}, bf16[256,1024]{1,0:T(8,128)(2,1)S(1)}, u32[]{:S(2)}, u32[]{:S(2)}) collective-permute-start(bf16[256,1024]{1,0:T(8,128)(2,1)S(1)} %pad_maximum_fusion.2), channel_id=1, source_target_pairs={{0,1},{1,0},{2,3},{3,2},{4,5},{5,4},{6,7},{7,6},{8,9},{9,8},{10,11... | collective-permute-start | bytes 1572872 | tf_op jit(solution)/shard_map/ppermute | solution.py:31
  144.9 30.0 %collective-permute-start.30 = (bf16[1,64,2048]{2,1,0:T(8,128)(2,1)S(1)}, bf16[1,64,2048]{2,1,0:T(8,128)(2,1)S(1)}, u32[]{:S(2)}, u32[]{:S(2)}) collective-permute-start(bf16[1,64,2048]{2,1,0:T(8,128)(2,1)S(1)} %dynamic-slice_convert_fusion), channel_id=1, source_target_pairs={{0,4},{1,5},{2,6},{3,7},{4,0},{5,1},{6,2},{7,3},{8,12},{9,13},{10,... | collective-permute-start | bytes 786440 | tf_op jit(solution)/shard_map/ppermute | solution.py:31
  147.8 14.5 %collective-permute-start.25 = (bf16[2,64,1024]{2,1,0:T(8,128)(2,1)S(1)}, bf16[2,64,1024]{2,1,0:T(8,128)(2,1)S(1)}, u32[]{:S(2)}, u32[]{:S(2)}) collective-permute-start(bf16[2,64,1024]{2,1,0:T(8,128)(2,1)S(1)} %fusion.17), channel_id=1, source_target_pairs={{0,2},{1,3},{2,0},{3,1},{4,6},{5,7},{6,4},{7,5},{8,10},{9,11},{10,... | collective-permute-start | bytes 786440 | tf_op jit(solution)/shard_map/ppermute | solution.py:31
  155.8 10.7 %collective-permute-start.28 = (bf16[2,64,1024]{2,1,0:T(8,128)(2,1)S(1)}, bf16[2,64,1024]{2,1,0:T(8,128)(2,1)S(1)}, u32[]{:S(2)}, u32[]{:S(2)}) collective-permute-start(bf16[2,64,1024]{2,1,0:T(8,128)(2,1)S(1)} %fusion.18), channel_id=1, source_target_pairs={{0,2},{1,3},{2,0},{3,1},{4,6},{5,7},{6,4},{7,5},{8,10},{9,11},{10,... | collective-permute-start | bytes 786440 | tf_op jit(solution)/shard_map/ppermute | solution.py:31
  162.4 7.2 %collective-permute-start.26 = (bf16[1,64,1024]{2,1,0:T(8,128)(2,1)S(1)}, bf16[1,64,1024]{2,1,0:T(8,128)(2,1)S(1)}, u32[]{:S(2)}, u32[]{:S(2)}) collective-permute-start(bf16[1,64,1024]{2,1,0:T(8,128)(2,1)S(1)} %dynamic-slice_convert_fusion.2), channel_id=1, source_target_pairs={{0,4},{1,5},{2,6},{3,7},{4,0},{5,1},{6,2},{7,3},{8,12},{9,13},{10,... | collective-permute-start | bytes 393224 | tf_op jit(solution)/shard_map/ppermute | solution.py:31
  166.6 8.3 %collective-permute-start.29 = (bf16[1,64,1024]{2,1,0:T(8,128)(2,1)S(1)}, bf16[1,64,1024]{2,1,0:T(8,128)(2,1)S(1)}, u32[]{:S(2)}, u32[]{:S(2)}) collective-permute-start(bf16[1,64,1024]{2,1,0:T(8,128)(2,1)S(1)} %dynamic-slice_convert_fusion.1), channel_id=1, source_target_pairs={{0,4},{1,5},{2,6},{3,7},{4,0},{5,1},{6,2},{7,3},{8,12},{9,13},{10,... | collective-permute-start | bytes 393224 | tf_op jit(solution)/shard_map/ppermute | solution.py:31
  (32 other events, 190.7 us)
